TPU v7x, 32 devices: a whole 2x2x4 slice. The times are simulated.
32 devices in a mesh: mp: 4 (over y, x), item: 8 (over z, core).
Axes of the slice: x: 2, y: 2, z: 4, core: 2. Of those that a mesh axis runs over, the one named last changes fastest.
Arguments:
- response: int32 [8192, 16384], P('mp', 'item'), may hold values from 0 to 2
- difficulty: float32 [16384], P('item'), may hold values from -4 to 4
- ability: float32 [8192, 256], P('mp', 'item'), may hold values from -6 to 6
- ability_m: float32 [8192, 256], P('mp', 'item'), may hold values from -3 to 3
- ability_v: float32 [8192, 256], P('mp', 'item'), may hold values from 0.02 to 0.5
- discrim: float32 [16384, 256], P('item', 'mp'), may hold values from -0.375 to 0.375
- discrim_m: float32 [16384, 256], P('item', 'mp'), may hold values from -3 to 3
- discrim_v: float32 [16384, 256], P('item', 'mp'), may hold values from 0.02 to 0.5
Outputs:
- ability_new: float32 [8192, 256], P('mp', 'item')
- ability_m_new: float32 [8192, 256], P('mp', 'item')
- ability_v_new: float32 [8192, 256], P('mp', 'item')
- discrim_new: float32 [16384, 256], P('item', 'mp')
- discrim_m_new: float32 [16384, 256], P('item', 'mp')
- discrim_v_new: float32 [16384, 256], P('item', 'mp')
Inputs may be any that keep to these rules, and one draw needn't show every extreme that they name: `response`: 0 marks an unobserved pair, 1 an observed wrong answer, 2 an observed right answer.
All inputs are finite; a program needn't handle non-finite values.
Results may differ from a plain program's by a relative error of at most 0.0012.
Values may be sent and summed in bfloat16 or wider, within the bound.
No kernel may reach another device: no remote copies, remote signals or barrier semaphores. Data moves between devices by JAX's collectives and lax.ppermute only.
A program may use at most 128 MiB of HBM per device.

v0:
```python
import math

import jax
import jax.numpy as jnp
from jax import lax
from jax.sharding import PartitionSpec as P

K = 256


beta_one = 0.9
beta_two = 0.999
corr_one = 1.0 - 0.9**10
corr_two = 1.0 - 0.999**10
adam_eps = 1e-08


def adam_update(factor, moment, second, gradient, step_rate):
    moment_new = beta_one * moment + (1.0 - beta_one) * gradient
    second_new = beta_two * second + (1.0 - beta_two) * gradient * gradient
    update = moment_new / corr_one / (jnp.sqrt(second_new / corr_two) + adam_eps)
    return (factor - step_rate * update, moment_new, second_new)


def shards(response, difficulty, ability, ability_m, ability_v, discrim, discrim_m, discrim_v):
    ability_full = lax.all_gather(ability.astype(jnp.bfloat16), "item", axis=1, tiled=True)
    discrim_full = lax.all_gather(discrim.astype(jnp.bfloat16), "mp", axis=1, tiled=True)
    logits = lax.dot_general(
        ability_full, discrim_full, (((1,), (1,)), ((), ())), preferred_element_type=jnp.float32
    )
    logits = logits + difficulty[None, :]
    correct = (response == 2).astype(jnp.float32)
    residual = jnp.where(response > 0, jax.nn.sigmoid(logits) - correct, jnp.float32(0.0))
    ability_wide = ability_full.astype(jnp.float32)
    discrim_wide = discrim_full.astype(jnp.float32)
    highest = lax.Precision.HIGHEST
    items_total = response.shape[1] * lax.axis_size("item")
    ckpts_total = response.shape[0] * lax.axis_size("mp")
    ability_partial = jnp.dot(residual, discrim_wide, precision=highest)
    ability_grad = lax.psum_scatter(ability_partial, "item", scatter_dimension=1, tiled=True)
    discrim_partial = lax.dot_general(
        residual, ability_wide, (((0,), (0,)), ((), ())), precision=highest
    )
    discrim_grad = lax.psum_scatter(discrim_partial, "mp", scatter_dimension=1, tiled=True)
    ability_grad = ability_grad * math.sqrt(K / items_total)
    discrim_grad = discrim_grad * math.sqrt(1.0 / ckpts_total)
    ability_new, ability_m_new, ability_v_new = adam_update(
        ability, ability_m, ability_v, ability_grad, 0.05
    )
    discrim_new, discrim_m_new, discrim_v_new = adam_update(
        discrim, discrim_m, discrim_v, discrim_grad, 0.01
    )
    return (ability_new, ability_m_new, ability_v_new, discrim_new, discrim_m_new, discrim_v_new)


def solution(mesh):
    return jax.shard_map(
        shards,
        mesh=mesh,
        in_specs=(
            P("mp", "item"),
            P("item"),
            P("mp", "item"),
            P("mp", "item"),
            P("mp", "item"),
            P("item", "mp"),
            P("item", "mp"),
            P("item", "mp"),
        ),
        out_specs=(
            P("mp", "item"),
            P("mp", "item"),
            P("mp", "item"),
            P("item", "mp"),
            P("item", "mp"),
            P("item", "mp"),
        ),
        check_vma=False,
    )
```

profile of v0, /device:TPU:0, one launch (start us, length us, event | category | flops | bytes accessed | tf_op | source)
XLA Modules:
  0.0 173.2 jit_solution(591156198732833946)
XLA Ops:
  7.2 0.0 all-gather.5.cloned.1.call-start
  7.2 1.8 %convert_element_type.12 = bf16[2048,64]{0,1:T(8,128)(2,1)} convert(f32[2048,64]{0,1:T(8,128)} %param.13) | non-fusion elementwise | flops 131072 | bytes 786432 | tf_op jit(solution)/shard_map/convert_element_type | solution.py:27
  9.0 0.0 all-gather.5.cloned.1.call-update
  9.0 0.0 all-gather.3.cloned.1.call-start
  9.1 1.6 convert_element_type.11
  10.7 0.0 all-gather.3.cloned.1.call-update
  10.7 0.0 reduce-scatter.3.cloned.1.call-start
  10.8 29.0 %all-gather.5.cloned.1.call-done = bf16[2048,256]{0,1:T(8,128)(2,1)} async-done(((bf16[2048,64]{0,1:T(8,128)(2,1)}), bf16[2048,256]{0,1:T(8,128)(2,1)}) %all-gather.5.cloned.1.call-update) | async-done | bytes 1048592 | tf_op jit(solution)/shard_map/all_gather | solution.py:27
  39.8 24.3 %all-gather.3.cloned.1.call-done = bf16[2048,256]{0,1:T(8,128)(2,1)} async-done(((bf16[2048,32]{0,1:T(8,128)(2,1)}), bf16[2048,256]{0,1:T(8,128)(2,1)}) %all-gather.3.cloned.1.call-update) | async-done | bytes 1048592 | tf_op jit(solution)/shard_map/all_gather | solution.py:26
  64.1 12.2 %subtract_select_fusion = f32[2048,2048]{1,0:T(8,128)S(1)} fusion(s32[2048,2048]{1,0:T(8,128)} %param.8, bf16[2048,256]{0,1:T(8,128)(2,1)} %all-gather.3.cloned.1.call-done, bf16[2048,256]{0,1:T(8,128)(2,1)} %all-gather.5.cloned.1.call-done, f32[2048]{0:T(1024)} %param.9), kind=kOutput, calls=%fused_computation | convolution fusion | flops 2185232384 | bytes 35659776 | tf_op jit(solution)/shard_map/dot_general | solution.py:28
  76.2 5.7 %copy-done = f32[2048,2048]{1,0:T(8,128)} copy-done((f32[2048,2048]{1,0:T(8,128)}, f32[2048,2048]{1,0:T(8,128)S(1)}, u32[]{:S(2)}) %copy-start) | copy-done | bytes 16777240
  82.0 9.8 %fusion = f32[2048,256]{0,1:T(8,128)} fusion(f32[2048,2048]{1,0:T(8,128)S(1)} %subtract_select_fusion, bf16[2048,256]{0,1:T(8,128)(2,1)S(1)} %copy-done.3), kind=kOutput, calls=%fused_computation.7 | convolution fusion | flops 12884901888 | bytes 19922944 | tf_op jit(solution)/shard_map/dot_general | solution.py:39
  91.8 0.0 copy-start.5
  91.8 0.0 copy-start.6
  91.8 0.0 reduce-scatter.3.cloned.1.call-update
  91.8 0.2 reduce-scatter.5.cloned.1.call-start
  92.1 13.3 %fusion.1 = f32[2048,256]{0,1:T(8,128)} fusion(f32[2048,2048]{1,0:T(8,128)} %copy-done, bf16[2048,256]{0,1:T(8,128)(2,1)S(1)} %copy-done.2), kind=kOutput, calls=%fused_computation.8 | convolution fusion | flops 12884901888 | bytes 19922944 | tf_op jit(solution)/shard_map/dot_general | solution.py:41
  105.4 0.0 reduce-scatter.5.cloned.1.call-update
  105.4 22.0 %reduce-scatter.3.cloned.1.call-done = f32[2048,32]{0,1:T(8,128)} async-done(((f32[2048,256]{0,1:T(8,128)}), f32[2048,32]{0,1:T(8,128)}) %reduce-scatter.3.cloned.1.call-update) | async-done | bytes 262160 | tf_op jit(solution)/shard_map/reduce_scatter | solution.py:40
  127.4 0.0 copy-done.8
  127.4 1.9 %multiply_subtract_fusion.1 = (f32[2048,32]{0,1:T(8,128)}, f32[2048,32]{0,1:T(8,128)}, f32[2048,32]{0,1:T(8,128)}) fusion(f32[2048,32]{0,1:T(8,128)S(1)} %copy-done.4, f32[2048,32]{0,1:T(8,128)} %reduce-scatter.3.cloned.1.call-done, f32[2048,32]{0,1:T(8,128)S(1)} %copy-done.7, f32[2048,32]{0,1:T(8,128)S(1)} %copy-done.8), kind=kLoop, calls=%fused_computation.4 | loop fusion | flops 917504 | bytes 1835008 | tf_op jit(solution)/shard_map/sub | solution.py:22
  129.3 34.9 %reduce-scatter.5.cloned.1.call-done = f32[2048,64]{0,1:T(8,128)} async-done(((f32[2048,256]{0,1:T(8,128)}), f32[2048,64]{0,1:T(8,128)}) %reduce-scatter.5.cloned.1.call-update) | async-done | bytes 524304 | tf_op jit(solution)/shard_map/reduce_scatter | solution.py:44
  164.2 0.0 copy-done.5
  164.2 2.4 %multiply_subtract_fusion = (f32[2048,64]{0,1:T(8,128)}, f32[2048,64]{0,1:T(8,128)}, f32[2048,64]{0,1:T(8,128)}) fusion(f32[2048,64]{0,1:T(8,128)S(1)} %copy-done.1, f32[2048,64]{0,1:T(8,128)} %reduce-scatter.5.cloned.1.call-done, f32[2048,64]{0,1:T(8,128)S(1)} %copy-done.5, f32[2048,64]{0,1:T(8,128)S(1)} %copy-done.6), kind=kLoop, calls=%fused_computation.1 | loop fusion | flops 1835008 | bytes 3670016 | tf_op jit(solution)/shard_map/sub | solution.py:22
  (13 shorter events, 0.0 us)
Async XLA Ops:
  7.2 32.6 %all-gather.5.cloned.1.call-start = ((), (), s32[]{:S(2)}) async-start(), calls=%async_computation.3 | async-start | bytes 1310720 | tf_op jit(solution)/shard_map/all_gather | solution.py:27
  9.0 55.1 %all-gather.3.cloned.1.call-start = ((), (), s32[]{:S(2)}) async-start(), calls=%async_computation.2 | async-start | bytes 1179648 | tf_op jit(solution)/shard_map/all_gather | solution.py:26
  10.7 116.7 %reduce-scatter.3.cloned.1.call-start = ((), (), s32[]{:S(2)}) async-start(), calls=%async_computation.4 | async-start | bytes 2359296 | tf_op jit(solution)/shard_map/reduce_scatter | solution.py:40
  39.8 42.2 %copy-start.3 = (bf16[2048,256]{0,1:T(8,128)(2,1)S(1)}, bf16[2048,256]{0,1:T(8,128)(2,1)}, u32[]{:S(2)}) copy-start(bf16[2048,256]{0,1:T(8,128)(2,1)} %all-gather.5.cloned.1.call-done) | copy-start | bytes 3145732
  76.2 5.7 %copy-start = (f32[2048,2048]{1,0:T(8,128)}, f32[2048,2048]{1,0:T(8,128)S(1)}, u32[]{:S(2)}) copy-start(f32[2048,2048]{1,0:T(8,128)S(1)} %subtract_select_fusion) | copy-start | bytes 50331652
  82.0 10.1 %copy-start.2 = (bf16[2048,256]{0,1:T(8,128)(2,1)S(1)}, bf16[2048,256]{0,1:T(8,128)(2,1)}, u32[]{:S(2)}) copy-start(bf16[2048,256]{0,1:T(8,128)(2,1)} %all-gather.3.cloned.1.call-done) | copy-start | bytes 3145732
  91.8 35.6 %copy-start.4 = (f32[2048,32]{0,1:T(8,128)S(1)}, f32[2048,32]{0,1:T(8,128)}, u32[]{:S(2)}) copy-start(f32[2048,32]{0,1:T(8,128)} %param.10) | copy-start | bytes 786436
  91.8 35.6 %copy-start.7 = (f32[2048,32]{0,1:T(8,128)S(1)}, f32[2048,32]{0,1:T(8,128)}, u32[]{:S(2)}) copy-start(f32[2048,32]{0,1:T(8,128)} %param.11) | copy-start | bytes 786436
  91.8 35.6 %copy-start.8 = (f32[2048,32]{0,1:T(8,128)S(1)}, f32[2048,32]{0,1:T(8,128)}, u32[]{:S(2)}) copy-start(f32[2048,32]{0,1:T(8,128)} %param.12) | copy-start | bytes 786436
  91.8 72.4 %copy-start.1 = (f32[2048,64]{0,1:T(8,128)S(1)}, f32[2048,64]{0,1:T(8,128)}, u32[]{:S(2)}) copy-start(f32[2048,64]{0,1:T(8,128)} %param.13) | copy-start | bytes 1572868
  91.8 72.4 %copy-start.5 = (f32[2048,64]{0,1:T(8,128)S(1)}, f32[2048,64]{0,1:T(8,128)}, u32[]{:S(2)}) copy-start(f32[2048,64]{0,1:T(8,128)} %param.14) | copy-start | bytes 1572868
  91.8 72.4 %copy-start.6 = (f32[2048,64]{0,1:T(8,128)S(1)}, f32[2048,64]{0,1:T(8,128)}, u32[]{:S(2)}) copy-start(f32[2048,64]{0,1:T(8,128)} %param.15) | copy-start | bytes 1572868
  91.8 72.4 %reduce-scatter.5.cloned.1.call-start = ((), (), s32[]{:S(2)}) async-start(), calls=%async_computation.5 | async-start | bytes 2621440 | tf_op jit(solution)/shard_map/reduce_scatter | solution.py:44
Sparse Core Ops, SparseCore 0:
  10.4 29.3 all-gather.4
  42.0 22.0 all-gather.2
  91.9 35.3 reduce-scatter.2
  130.2 33.9 reduce-scatter.4
where the time goes:
time: 173 us
  waiting for transfers between devices  110 us (64%)
  matrix products  35.2 us (20%)
  between operations  13.8 us (8%)
  other arithmetic  7.75 us (4%)
  local copies, waits for them, and re-layouts  5.78 us (3%)
    reduce_scatter x1, waiting for transfers between devices, shards(): lax.psum_scatter(discrim_partial, 'mp', scatter_dimension=1, tiled=True)  34.9 us
    all_gather x1, waiting for transfers between devices, shards(): lax.all_gather(discrim.astype(jnp.bfloat16), 'mp', axis=1, tiled=True)  29 us
    all_gather x1, waiting for transfers between devices, shards(): lax.all_gather(ability.astype(jnp.bfloat16), 'item', axis=1, tiled=True)  24.3 us
    reduce_scatter x1, waiting for transfers between devices, shards(): lax.psum_scatter(ability_partial, 'item', scatter_dimension=1, tiled=True)  22 us
    dot_general x1, matrix products, shards(): lax.dot_general(residual, ability_wide, (((0,), (0,)), ((), ())), precisi...  13.3 us
    dot_general x1, matrix products, shards(): lax.dot_general(ability_full, discrim_full, (((1,), (1,)), ((), ())), pre...  12.2 us
    dot_general x1, matrix products, shards(): ability_partial = jnp.dot(residual, discrim_wide, precision=highest)  9.77 us
    unnamed x18, local copies, waits for them, and re-layouts  5.78 us
  transfers between devices with their start and end apart: 4, of which 4 were waited for; matrix products, arithmetic and copies ran while one was open for 10% of the time, Pallas kernels for 0%

commit v1 on v0

v1 whole, which is shorter than its diff:
```python
import functools
import math

import jax
import jax.numpy as jnp
from jax import lax
from jax.experimental import pallas as pl
from jax.experimental.pallas import tpu as pltpu
from jax.sharding import PartitionSpec as P

beta_one = 0.9
beta_two = 0.999
corr_one = 1.0 - 0.9**10
corr_two = 1.0 - 0.999**10
adam_eps = 1e-08

BF = jnp.bfloat16
F32 = jnp.float32
VMEM_BYTES = 52 * 2**20
ROW_TILE = 512
COL_TILE = 512


def adam_update(factor, moment, second, gradient, step_rate):
    moment_new = beta_one * moment + (1.0 - beta_one) * gradient
    second_new = beta_two * second + (1.0 - beta_two) * gradient * gradient
    update = moment_new / corr_one / (jnp.sqrt(second_new / corr_two) + adam_eps)
    return (factor - step_rate * update, moment_new, second_new)


def cast_kernel(a_ref, d_ref, a_out, d_out):
    a_out[...] = a_ref[...].astype(BF)
    d_out[...] = d_ref[...].astype(BF)


def cast_both(a, d):
    return pl.pallas_call(
        cast_kernel,
        out_shape=(jax.ShapeDtypeStruct(a.shape, BF), jax.ShapeDtypeStruct(d.shape, BF)),
        name="cast_factors",
    )(a, d)


def swap_item(n_item, mask):
    return [(i, i ^ mask) for i in range(n_item)]


def swap_mp(n_mp, n_item, mask):
    pairs = []
    for m in range(n_mp):
        for i in range(n_item):
            other = mask if i % 2 == 0 or n_mp < 4 else {1: 2, 2: 1}.get(mask, mask)
            pairs.append((m * n_item + i, (m ^ other) * n_item + i))
    return pairs


def mp_masks(n_mp):
    swap = lambda x: x if n_mp < 4 else (x & ~3) | ((x & 1) << 1) | ((x >> 1) & 1)
    return [(x, swap(x)) for x in range(n_mp)]


def gather_mp(d, n_mp, n_item):
    blocks = [d]
    bit = 1
    while bit < n_mp:
        perm = swap_mp(n_mp, n_item, bit)
        blocks += [lax.ppermute(b, ("mp", "item"), perm) for b in blocks]
        bit *= 2
    return blocks


def gather_item(a, n_item):
    chips = n_item // 2
    mine = [a] + [lax.ppermute(a, "item", swap_item(n_item, 2 * x)) for x in range(1, chips)]
    theirs = [lax.ppermute(b, "item", swap_item(n_item, 1)) for b in mine]
    return mine + theirs


def grad_kernel(n_mp, n_item, *refs):
    chips = n_item // 2
    a_in, refs = refs[:n_item], refs[n_item:]
    d_in, refs = refs[:n_mp], refs[n_mp:]
    diff_ref, r_hbm = refs[:2]
    keep_ref, give_ref, *h_out = refs[2 : 4 + n_mp]
    at, dt, resp, rs, gs, acc, sem_in, sem_r = refs[4 + n_mp :]
    k, rows = at.shape
    cols = dt.shape[1]
    ka, kd = k // n_item, k // n_mp
    tiles = rows // ROW_TILE

    item = lax.axis_index("item")
    m = lax.axis_index("mp")
    chip, core = item // 2, lax.rem(item, 2)

    def owner_item(x, flip):
        return (chip ^ x) * 2 + (core ^ flip)

    copies = []
    for q, (x, flip) in enumerate((x, f) for f in range(2) for x in range(chips)):
        off = pl.multiple_of(owner_item(x, flip) * ka, ka)
        copies.append(pltpu.make_async_copy(a_in[q], at.at[pl.ds(off, ka)], sem_in.at[q]))
    for q, (even, odd) in enumerate(mp_masks(n_mp)):
        off = pl.multiple_of((m ^ jnp.where(core == 0, even, odd)) * kd, kd)
        copies.append(pltpu.make_async_copy(d_in[q], dt.at[pl.ds(off, kd)], sem_in.at[n_item + q]))
    loads = []
    for t in range(tiles):
        rng = pl.ds(t * ROW_TILE, ROW_TILE)
        loads.append(pltpu.make_async_copy(r_hbm.at[rng], resp.at[rng], sem_r.at[t]))
    for c in copies:
        c.start()
    for c in loads:
        c.start()
    for c in copies:
        c.wait()

    n_cols = cols // COL_TILE
    sub = ROW_TILE // n_cols
    for t in range(tiles + 1):
        if t < tiles:
            loads[t].wait()
            rng = slice(t * ROW_TILE, (t + 1) * ROW_TILE)
            half = (at[:, rng].astype(F32) * 0.5).T.astype(BF)
        if t > 0:
            old = slice((t - 1) * ROW_TILE, t * ROW_TILE)
            at_old = at[:, old]
        for c in range(n_cols):
            cr = slice(c * COL_TILE, (c + 1) * COL_TILE)
            if t < tiles:
                lg = jnp.dot(half, dt[:, cr], preferred_element_type=F32) + 0.5 * diff_ref[:, cr]
                r = resp[rng, cr]
                sign = jnp.where(r == 2, -1.0, 1.0)
                rs[t % 2, :, cr] = jnp.where(r == 0, 0.0, jnp.tanh(lg) + sign).astype(BF)
            if t > 0:
                p = (t - 1) % 2
                h = jnp.dot(at_old, rs[p, :, cr], preferred_element_type=F32)
                if t == 1:
                    acc[:, cr] = h
                else:
                    acc[:, cr] += h
                g = lax.dot_general(
                    rs[p, c * sub : (c + 1) * sub, :],
                    dt[...],
                    (((1,), (1,)), ((), ())),
                    preferred_element_type=F32,
                )
                lo = (t - 1) * ROW_TILE + c * sub
                gs[:, lo : lo + sub] = g.T

    for x in range(chips):
        dst = pl.ds(x * ka, ka)
        keep_ref[dst, :] = gs[pl.ds(pl.multiple_of(owner_item(x, 0) * ka, ka), ka), :]
        give_ref[dst, :] = gs[pl.ds(pl.multiple_of(owner_item(x, 1) * ka, ka), ka), :].astype(BF)
    for x in range(n_mp):
        h = acc[pl.ds(pl.multiple_of((m ^ x) * kd, kd), kd), :]
        h_out[x][...] = h.astype(h_out[x].dtype)


def gradients(a_blocks, d_blocks, difficulty, response, n_mp, n_item):
    ka, rows = a_blocks[0].shape
    kd, cols = d_blocks[0].shape
    k = ka * n_item
    tiles = rows // ROW_TILE
    flops = 3 * 2 * rows * cols * k
    shape = jax.ShapeDtypeStruct
    any_spec = pl.BlockSpec(memory_space=pl.ANY)
    vmem = pl.BlockSpec(memory_space=pltpu.VMEM)
    outs = [shape((k // 2, rows), F32), shape((k // 2, rows), BF), shape((kd, cols), F32)]
    outs += [shape((kd, cols), BF)] * (n_mp - 1)
    return pl.pallas_call(
        functools.partial(grad_kernel, n_mp, n_item),
        out_shape=outs,
        in_specs=[any_spec] * (n_item + n_mp) + [vmem, any_spec],
        out_specs=[vmem] * len(outs),
        scratch_shapes=[
            pltpu.VMEM((k, rows), BF),
            pltpu.VMEM((k, cols), BF),
            pltpu.VMEM((rows, cols), jnp.int32),
            pltpu.VMEM((2, ROW_TILE, cols), BF),
            pltpu.VMEM((k, rows), F32),
            pltpu.VMEM((k, cols), F32),
            pltpu.SemaphoreType.DMA((n_item + n_mp,)),
            pltpu.SemaphoreType.DMA((tiles,)),
        ],
        compiler_params=pltpu.CompilerParams(vmem_limit_bytes=VMEM_BYTES),
        cost_estimate=pl.CostEstimate(
            flops=flops, bytes_accessed=4 * rows * cols, transcendentals=rows * cols
        ),
        name="residual_gradients",
    )(*a_blocks, *d_blocks, difficulty, response)


def pair_kernel(ka, keep_ref, got_ref, own_ref, *outs):
    own_ref[...] = keep_ref[:ka, :] + got_ref[:ka, :].astype(F32)
    for q, out in enumerate(outs):
        rng = slice((q + 1) * ka, (q + 2) * ka)
        out[...] = (keep_ref[rng, :] + got_ref[rng, :].astype(F32)).astype(BF)


def pair_sum(keep, got, chips):
    ka, rows = keep.shape[0] // chips, keep.shape[1]
    shape = jax.ShapeDtypeStruct
    return pl.pallas_call(
        functools.partial(pair_kernel, ka),
        out_shape=[shape((ka, rows), F32)] + [shape((ka, rows), BF)] * (chips - 1),
        name="core_pair_sum",
    )(keep, got)


def shards(response, difficulty, ability, ability_m, ability_v, discrim, discrim_m, discrim_v):
    n_item, n_mp = lax.axis_size("item"), lax.axis_size("mp")
    chips = n_item // 2
    rows, cols = response.shape
    k = discrim.shape[1] * n_mp
    items_total, ckpts_total = cols * n_item, rows * n_mp
    a_bf, d_bf = cast_both(ability.T, discrim.T)
    d_blocks = gather_mp(d_bf, n_mp, n_item)
    a_blocks = gather_item(a_bf, n_item)
    keep, give, *h = gradients(
        a_blocks, d_blocks, difficulty.reshape(1, cols), response, n_mp, n_item
    )
    h_sum = h[0]
    h_got = [
        lax.ppermute(h[x], "mp", [(i, i ^ x) for i in range(n_mp)]) for x in range(1, n_mp)
    ]
    got = lax.ppermute(give, "item", swap_item(n_item, 1))
    g_sum, *g = pair_sum(keep, got, chips)
    g_got = [
        lax.ppermute(g[x - 1], "item", swap_item(n_item, 2 * x)) for x in range(1, chips)
    ]
    for b in g_got:
        g_sum = g_sum + b.astype(F32)
    for b in h_got:
        h_sum = h_sum + b.astype(F32)
    a_out = adam_update(
        ability.T, ability_m.T, ability_v.T, g_sum * (0.5 * math.sqrt(k / items_total)), 0.05
    )
    d_out = adam_update(
        discrim.T, discrim_m.T, discrim_v.T, h_sum * (0.5 * math.sqrt(1.0 / ckpts_total)), 0.01
    )
    return tuple(x.T for x in a_out + d_out)


def solution(mesh):
    a_spec, d_spec = P("mp", "item"), P("item", "mp")
    return jax.shard_map(
        shards,
        mesh=mesh,
        in_specs=(a_spec, P("item")) + (a_spec,) * 3 + (d_spec,) * 3,
        out_specs=(a_spec,) * 3 + (d_spec,) * 3,
        check_vma=False,
    )
```

time: 173 us -> 82.1 us (0.47)
  waiting for transfers between devices: 110 us -> 29.1 us
  matrix products: 35.2 us -> 0 us
  Pallas kernels: 0 us -> 24.7 us
  starting transfers between devices: 0.34 us -> 18 us
  between operations: 13.8 us -> 0.71 us
  local copies, waits for them, and re-layouts: 5.78 us -> 3.18 us
    reduce_scatter x2 -> x0, waiting for transfers between devices: 56.9 us -> none  [the longest x1 34.9 us: shards(): lax.psum_scatter(discrim_partial, 'mp', scatter_dimension=1, tiled=True)]
    all_gather x2 -> x0, waiting for transfers between devices: 53.3 us -> none  [the longest x1 29 us: shards(): lax.all_gather(discrim.astype(jnp.bfloat16), 'mp', axis=1, tiled=True)]
    dot_general x3 -> x0, matrix products: 35.2 us -> none  [the longest x1 13.3 us: shards(): lax.dot_general(residual, ability_wide, (((0,), (0,)), ((), ())), precisi...]
    ppermute x0 -> x17, waiting for transfers between devices: none -> 29.1 us  [the longest x3 11.6 us: shards(): lax.ppermute(h[x], 'mp', [(i, i ^ x) for i in range(n_mp)])]
    pallas_call x0 -> x3, Pallas kernels: none -> 24.7 us  [the longest x1 20.6 us: gradients(): pl.pallas_call(functools.partial(grad_kernel, n_mp, n_item), out_shape=ou...]
    ppermute x0 -> x17, starting transfers between devices: none -> 18 us  [the longest x3 5.15 us: gather_mp(): blocks += [lax.ppermute(b, ('mp', 'item'), perm) for b in blocks]]
    transpose x0 -> x4, other arithmetic: none -> 6.09 us  [shards(): return tuple((x.T for x in a_out + d_out))]
    sub x2 -> x0, other arithmetic: 4.35 us -> none  [adam_update(): return (factor - step_rate * update, moment_new, second_new)]
  transfers between devices with their start and end apart: 4 -> 17, of which waited for: 4 -> 9; matrix products, arithmetic and copies ran while one was open for 10% -> 4% of each run, Pallas kernels for 0% -> 0%
where the time goes in v1:
time: 82.1 us; the launch traced here: 81.8 us
  waiting for transfers between devices  29.1 us (35%)
  Pallas kernels  24.7 us (30%)
  starting transfers between devices  18 us (22%)
  other arithmetic  6.09 us (7%)
  local copies, waits for them, and re-layouts  3.18 us (4%)
    pallas_call x1, Pallas kernels, gradients(): pl.pallas_call(functools.partial(grad_kernel, n_mp, n_item), out_shape=ou...  20.6 us
    ppermute x3, waiting for transfers between devices, shards(): lax.ppermute(h[x], 'mp', [(i, i ^ x) for i in range(n_mp)])  11.6 us
    ppermute x3, waiting for transfers between devices, gather_item(): lax.ppermute(a, 'item', swap_item(n_item, 2 * x))  8.95 us
    ppermute x3, waiting for transfers between devices, shards(): lax.ppermute(g[x - 1], 'item', swap_item(n_item, 2 * x))  7.49 us
    transpose x4, other arithmetic, shards(): return tuple((x.T for x in a_out + d_out))  6.09 us
    ppermute x3, starting transfers between devices, gather_mp(): blocks += [lax.ppermute(b, ('mp', 'item'), perm) for b in blocks]  5.15 us
    ppermute x3, starting transfers between devices, gather_item(): lax.ppermute(a, 'item', swap_item(n_item, 2 * x))  4.39 us
    ppermute x3, starting transfers between devices, shards(): lax.ppermute(g[x - 1], 'item', swap_item(n_item, 2 * x))  4.39 us
  transfers between devices with their start and end apart: 17, of which 9 were waited for; matrix products, arithmetic and copies ran while one was open for 4% of the time, Pallas kernels for 0%

profile of v1, /device:TPU:0, one launch (start us, length us, event | category | flops | bytes accessed | tf_op | source)
XLA Modules:
  0.0 81.8 jit_solution(14073588062451191086)
XLA Ops:
  0.7 2.0 %cast_factors.1 = (bf16[32,2048]{1,0:T(8,128)(2,1)}, bf16[64,2048]{1,0:T(8,128)(2,1)}) custom-call(f32[32,2048]{1,0:T(8,128)} %bitcast.43, f32[64,2048]{1,0:T(8,128)} %bitcast.42), custom_call_target="tpu_custom_call" | custom-call | tf_op jit(solution)/shard_map/cast_factors/pallas_call | solution.py:37
  2.6 2.9 %collective-permute-start.7 = (bf16[64,2048]{1,0:T(8,128)(2,1)}, bf16[64,2048]{1,0:T(8,128)(2,1)S(1)}, u32[]{:S(2)}, u32[]{:S(2)}) collective-permute-start(bf16[64,2048]{1,0:T(8,128)(2,1)} %get-tuple-element.19.refs_8_), channel_id=1, source_target_pairs={{0,8},{1,17},{2,10},{3,19},{4,12},{5,21},{6,14},{7,23},{8,0},{9,25... | collective-permute-start | bytes 786440 | tf_op jit(solution)/shard_map/ppermute | solution.py:67
  5.5 3.6 %collective-permute-start.2 = (bf16[32,2048]{1,0:T(8,128)(2,1)}, bf16[32,2048]{1,0:T(8,128)(2,1)S(1)}, u32[]{:S(2)}, u32[]{:S(2)}) collective-permute-start(bf16[32,2048]{1,0:T(8,128)(2,1)} %get-tuple-element.18.refs_0_), channel_id=1, source_target_pairs={{0,6},{1,7},{2,4},{3,5},{4,2},{5,3},{6,0},{7,1},{8,14},{9,15},{10,... | collective-permute-start | bytes 393224 | tf_op jit(solution)/shard_map/ppermute | solution.py:74
  9.9 1.5 %collective-permute-start.8 = (bf16[64,2048]{1,0:T(8,128)(2,1)}, bf16[64,2048]{1,0:T(8,128)(2,1)S(1)}, u32[]{:S(2)}, u32[]{:S(2)}) collective-permute-start(bf16[64,2048]{1,0:T(8,128)(2,1)} %get-tuple-element.19.refs_8_), channel_id=1, source_target_pairs={{0,16},{1,9},{2,18},{3,11},{4,20},{5,13},{6,22},{7,15},{8,24},{9,1... | collective-permute-start | bytes 786440 | tf_op jit(solution)/shard_map/ppermute | solution.py:67
  12.2 1.8 %collective-permute-done.2.refs_3_ = bf16[32,2048]{1,0:T(8,128)(2,1)S(1)} collective-permute-done((bf16[32,2048]{1,0:T(8,128)(2,1)}, bf16[32,2048]{1,0:T(8,128)(2,1)S(1)}, u32[]{:S(2)}, u32[]{:S(2)}) %collective-permute-start.2) | collective-permute-done | bytes 131104 | tf_op jit(solution)/shard_map/ppermute | solution.py:74
  13.9 7.2 %collective-permute-done.1.refs_2_ = bf16[32,2048]{1,0:T(8,128)(2,1)S(1)} collective-permute-done((bf16[32,2048]{1,0:T(8,128)(2,1)}, bf16[32,2048]{1,0:T(8,128)(2,1)S(1)}, u32[]{:S(2)}, u32[]{:S(2)}) %collective-permute-start.1) | collective-permute-done | bytes 131104 | tf_op jit(solution)/shard_map/ppermute | solution.py:74
  21.6 0.8 %collective-permute-done.5.refs_6_ = bf16[32,2048]{1,0:T(8,128)(2,1)S(1)} collective-permute-done((bf16[32,2048]{1,0:T(8,128)(2,1)S(1)}, bf16[32,2048]{1,0:T(8,128)(2,1)S(1)}, u32[]{:S(2)}, u32[]{:S(2)}) %collective-permute-start.5) | collective-permute-done | bytes 131104 | tf_op jit(solution)/shard_map/ppermute | solution.py:75
  23.4 0.9 %copy-done = bf16[32,2048]{1,0:T(8,128)(2,1)S(1)} copy-done((bf16[32,2048]{1,0:T(8,128)(2,1)S(1)}, bf16[32,2048]{1,0:T(8,128)(2,1)}, u32[]{:S(2)}) %copy-start) | copy-done | bytes 131096
  25.0 20.6 %residual_gradients.1 = (f32[128,2048]{1,0:T(8,128)}, bf16[128,2048]{1,0:T(8,128)(2,1)}, f32[64,2048]{1,0:T(8,128)}, bf16[64,2048]{1,0:T(8,128)(2,1)S(1)}, bf16[...) custom-call(bf16[32,2048]{1,0:T(8,128)(2,1)S(1)} %copy-done, bf16[32,2048]{1,0:T(8,128)(2,1)S(1)} %collective-permute-done.refs_1_, ...), custom_call_target="tpu_custom_call" | custom-call | flops 6442450944 | bytes 16777216 | tf_op jit(solution)/shard_map/residual_gradients/pallas_call | solution.py:169
  46.3 1.5 %collective-permute-start.15 = (bf16[64,2048]{1,0:T(8,128)(2,1)S(1)}, bf16[64,2048]{1,0:T(8,128)(2,1)S(1)}, u32[]{:S(2)}, u32[]{:S(2)}) collective-permute-start(bf16[64,2048]{1,0:T(8,128)(2,1)S(1)} %get-tuple-element.28), channel_id=1, source_target_pairs={{0,16},{8,24},{16,0},{24,8},{1,17},{9,25},{17,1},{25,9},{2,18},{10... | collective-permute-start | bytes 786440 | tf_op jit(solution)/shard_map/ppermute | solution.py:223
  47.8 1.4 %collective-permute-start.16 = (bf16[64,2048]{1,0:T(8,128)(2,1)S(1)}, bf16[64,2048]{1,0:T(8,128)(2,1)S(1)}, u32[]{:S(2)}, u32[]{:S(2)}) collective-permute-start(bf16[64,2048]{1,0:T(8,128)(2,1)S(1)} %get-tuple-element.29), channel_id=1, source_target_pairs={{0,24},{8,16},{16,8},{24,0},{1,25},{9,17},{17,9},{25,1},{2,26},{10... | collective-permute-start | bytes 786440 | tf_op jit(solution)/shard_map/ppermute | solution.py:223
  49.2 5.6 %collective-permute-done.14 = bf16[64,2048]{1,0:T(8,128)(2,1)S(1)} collective-permute-done((bf16[64,2048]{1,0:T(8,128)(2,1)S(1)}, bf16[64,2048]{1,0:T(8,128)(2,1)S(1)}, u32[]{:S(2)}, u32[]{:S(2)}) %collective-permute-start.14) | collective-permute-done | bytes 262176 | tf_op jit(solution)/shard_map/ppermute | solution.py:223
  54.8 4.4 %collective-permute-done.15 = bf16[64,2048]{1,0:T(8,128)(2,1)S(1)} collective-permute-done((bf16[64,2048]{1,0:T(8,128)(2,1)S(1)}, bf16[64,2048]{1,0:T(8,128)(2,1)S(1)}, u32[]{:S(2)}, u32[]{:S(2)}) %collective-permute-start.15) | collective-permute-done | bytes 262176 | tf_op jit(solution)/shard_map/ppermute | solution.py:223
  59.2 1.6 %collective-permute-done.16 = bf16[64,2048]{1,0:T(8,128)(2,1)S(1)} collective-permute-done((bf16[64,2048]{1,0:T(8,128)(2,1)S(1)}, bf16[64,2048]{1,0:T(8,128)(2,1)S(1)}, u32[]{:S(2)}, u32[]{:S(2)}) %collective-permute-start.16) | collective-permute-done | bytes 262176 | tf_op jit(solution)/shard_map/ppermute | solution.py:223
  60.8 2.0 %fusion.1 = (f32[2048,64]{0,1:T(8,128)}, f32[64,2048]{1,0:T(8,128)S(1)}) fusion(f32[2048,64]{0,1:T(8,128)S(1)} %copy-done.3, bf16[64,2048]{1,0:T(8,128)(2,1)S(1)} %collective-permute-done.16, bf16[64,2048]{1,0:T(8,128)(2,1)S(1)} %collective-permute-done.15, f32[64,2048]{1,0:T(8,128)} %get-tuple-element.26, bf16[64,2048]{1,0:T(8,128)(2,1)S(1)} %collective-permute-done.14), kind=kLoop, calls=%fused_computation.9 | loop fusion | flops 1441792 | bytes 2883584 | tf_op jit(solution)/shard_map/transpose | solution.py:240
  62.8 0.8 copy-done.6
  63.6 2.2 %core_pair_sum.1 = (f32[32,2048]{1,0:T(8,128)}, bf16[32,2048]{1,0:T(8,128)(2,1)}, bf16[32,2048]{1,0:T(8,128)(2,1)}, bf16[32,2048]{1,0:T(8,128)(2,1)}) custom-call(f32[128,2048]{1,0:T(8,128)} %get-tuple-element.20.keep_ref, bf16[128,2048]{1,0:T(8,128)(2,1)} %copy-done.6), custom_call_target="tpu_custom_call" | custom-call | tf_op jit(solution)/shard_map/core_pair_sum/pallas_call | solution.py:202
  65.8 3.0 %collective-permute-start.12 = (bf16[32,2048]{1,0:T(8,128)(2,1)}, bf16[32,2048]{1,0:T(8,128)(2,1)S(1)}, u32[]{:S(2)}, u32[]{:S(2)}) collective-permute-start(bf16[32,2048]{1,0:T(8,128)(2,1)} %get-tuple-element.24), channel_id=1, source_target_pairs={{0,4},{1,5},{2,6},{3,7},{4,0},{5,1},{6,2},{7,3},{8,12},{9,13},{10,... | collective-permute-start | bytes 393224 | tf_op jit(solution)/shard_map/ppermute | solution.py:228
  68.9 1.3 %collective-permute-start.13 = (bf16[32,2048]{1,0:T(8,128)(2,1)}, bf16[32,2048]{1,0:T(8,128)(2,1)S(1)}, u32[]{:S(2)}, u32[]{:S(2)}) collective-permute-start(bf16[32,2048]{1,0:T(8,128)(2,1)} %get-tuple-element.25), channel_id=1, source_target_pairs={{0,6},{1,7},{2,4},{3,5},{4,2},{5,3},{6,0},{7,1},{8,14},{9,15},{10,... | collective-permute-start | bytes 393224 | tf_op jit(solution)/shard_map/ppermute | solution.py:228
  70.2 1.3 %fusion = (f32[2048,64]{0,1:T(8,128)}, f32[2048,64]{0,1:T(8,128)}) fusion(f32[64,2048]{1,0:T(8,128)S(1)} %get-tuple-element.31, f32[2048,64]{0,1:T(8,128)S(1)} %copy-done.7, f32[2048,64]{0,1:T(8,128)S(1)} %copy-done.3, f32[2048,64]{0,1:T(8,128)S(1)} %copy-done.2), kind=kLoop, calls=%fused_computation.8 | loop fusion | flops 1835008 | bytes 3145728 | tf_op jit(solution)/shard_map/transpose | solution.py:240
  71.6 1.3 %collective-permute-done.11 = bf16[32,2048]{1,0:T(8,128)(2,1)S(1)} collective-permute-done((bf16[32,2048]{1,0:T(8,128)(2,1)}, bf16[32,2048]{1,0:T(8,128)(2,1)S(1)}, u32[]{:S(2)}, u32[]{:S(2)}) %collective-permute-start.11) | collective-permute-done | bytes 131104 | tf_op jit(solution)/shard_map/ppermute | solution.py:228
  72.9 6.1 %collective-permute-done.12 = bf16[32,2048]{1,0:T(8,128)(2,1)S(1)} collective-permute-done((bf16[32,2048]{1,0:T(8,128)(2,1)}, bf16[32,2048]{1,0:T(8,128)(2,1)S(1)}, u32[]{:S(2)}, u32[]{:S(2)}) %collective-permute-start.12) | collective-permute-done | bytes 131104 | tf_op jit(solution)/shard_map/ppermute | solution.py:228
  79.0 1.8 %fusion.3 = (f32[2048,32]{0,1:T(8,128)}, f32[32,2048]{1,0:T(8,128)S(1)}) fusion(f32[2048,32]{0,1:T(8,128)S(1)} %copy-done.5, bf16[32,2048]{1,0:T(8,128)(2,1)S(1)} %collective-permute-done.13, bf16[32,2048]{1,0:T(8,128)(2,1)S(1)} %collective-permute-done.12, f32[32,2048]{1,0:T(8,128)} %get-tuple-element.22, bf16[32,2048]{1,0:T(8,128)(2,1)S(1)} %collective-permute-done.11), kind=kLoop, calls=%fused_computation.11 | loop fusion | flops 720896 | bytes 1441792 | tf_op jit(solution)/shard_map/transpose | solution.py:240
  80.8 1.0 %fusion.2 = (f32[2048,32]{0,1:T(8,128)}, f32[2048,32]{0,1:T(8,128)}) fusion(f32[32,2048]{1,0:T(8,128)S(1)} %get-tuple-element.33, f32[2048,32]{0,1:T(8,128)S(1)} %copy-done.8, f32[2048,32]{0,1:T(8,128)S(1)} %copy-done.5, f32[2048,32]{0,1:T(8,128)S(1)} %copy-done.4), kind=kLoop, calls=%fused_computation.10 | loop fusion | flops 917504 | bytes 1572864 | tf_op jit(solution)/shard_map/transpose | solution.py:240
  (41 shorter events, 4.3 us)
Async XLA Ops:
  0.6 69.6 %copy-start.2 = (f32[2048,64]{0,1:T(8,128)S(1)}, f32[2048,64]{0,1:T(8,128)}, u32[]{:S(2)}) copy-start(f32[2048,64]{0,1:T(8,128)} %param.13) | copy-start | bytes 1572868
  0.6 80.2 %copy-start.4 = (f32[2048,32]{0,1:T(8,128)S(1)}, f32[2048,32]{0,1:T(8,128)}, u32[]{:S(2)}) copy-start(f32[2048,32]{0,1:T(8,128)} %param.10) | copy-start | bytes 786436
  2.6 8.9 %collective-permute-start.7 = (bf16[64,2048]{1,0:T(8,128)(2,1)}, bf16[64,2048]{1,0:T(8,128)(2,1)S(1)}, u32[]{:S(2)}, u32[]{:S(2)}) collective-permute-start(bf16[64,2048]{1,0:T(8,128)(2,1)} %get-tuple-element.19.refs_8_), channel_id=1, source_target_pairs={{0,8},{1,17},{2,10},{3,19},{4,12},{5,21},{6,14},{7,23},{8,0},{9,25... | collective-permute-start | bytes 786440 | tf_op jit(solution)/shard_map/ppermute | solution.py:67
  5.5 4.4 %collective-permute-start.3 = (bf16[32,2048]{1,0:T(8,128)(2,1)}, bf16[32,2048]{1,0:T(8,128)(2,1)S(1)}, u32[]{:S(2)}, u32[]{:S(2)}) collective-permute-start(bf16[32,2048]{1,0:T(8,128)(2,1)} %get-tuple-element.18.refs_0_), channel_id=1, source_target_pairs={{0,1},{1,0},{2,3},{3,2},{4,5},{5,4},{6,7},{7,6},{8,9},{9,8},{10,11... | collective-permute-start | bytes 393224 | tf_op jit(solution)/shard_map/ppermute | solution.py:75
  5.5 8.4 %collective-permute-start.2 = (bf16[32,2048]{1,0:T(8,128)(2,1)}, bf16[32,2048]{1,0:T(8,128)(2,1)S(1)}, u32[]{:S(2)}, u32[]{:S(2)}) collective-permute-start(bf16[32,2048]{1,0:T(8,128)(2,1)} %get-tuple-element.18.refs_0_), channel_id=1, source_target_pairs={{0,6},{1,7},{2,4},{3,5},{4,2},{5,3},{6,0},{7,1},{8,14},{9,15},{10,... | collective-permute-start | bytes 393224 | tf_op jit(solution)/shard_map/ppermute | solution.py:74
  9.1 12.0 %collective-permute-start.1 = (bf16[32,2048]{1,0:T(8,128)(2,1)}, bf16[32,2048]{1,0:T(8,128)(2,1)S(1)}, u32[]{:S(2)}, u32[]{:S(2)}) collective-permute-start(bf16[32,2048]{1,0:T(8,128)(2,1)} %get-tuple-element.18.refs_0_), channel_id=1, source_target_pairs={{0,4},{1,5},{2,6},{3,7},{4,0},{5,1},{6,2},{7,3},{8,12},{9,13},{10,... | collective-permute-start | bytes 393224 | tf_op jit(solution)/shard_map/ppermute | solution.py:74
  9.2 12.0 %collective-permute-start = (bf16[32,2048]{1,0:T(8,128)(2,1)}, bf16[32,2048]{1,0:T(8,128)(2,1)S(1)}, u32[]{:S(2)}, u32[]{:S(2)}) collective-permute-start(bf16[32,2048]{1,0:T(8,128)(2,1)} %get-tuple-element.18.refs_0_), channel_id=1, source_target_pairs={{0,2},{1,3},{2,0},{3,1},{4,6},{5,7},{6,4},{7,5},{8,10},{9,11},{10,... | collective-permute-start | bytes 393224 | tf_op jit(solution)/shard_map/ppermute | solution.py:74
  9.9 12.7 %collective-permute-start.8 = (bf16[64,2048]{1,0:T(8,128)(2,1)}, bf16[64,2048]{1,0:T(8,128)(2,1)S(1)}, u32[]{:S(2)}, u32[]{:S(2)}) collective-permute-start(bf16[64,2048]{1,0:T(8,128)(2,1)} %get-tuple-element.19.refs_8_), channel_id=1, source_target_pairs={{0,16},{1,9},{2,18},{3,11},{4,20},{5,13},{6,22},{7,15},{8,24},{9,1... | collective-permute-start | bytes 786440 | tf_op jit(solution)/shard_map/ppermute | solution.py:67
  11.5 11.2 %copy-start.9 = (bf16[64,2048]{1,0:T(8,128)(2,1)}, bf16[64,2048]{1,0:T(8,128)(2,1)S(1)}, u32[]{:S(2)}) copy-start(bf16[64,2048]{1,0:T(8,128)(2,1)S(1)} %collective-permute-done.7.refs_9_) | copy-start | bytes 786436
  11.5 11.2 %collective-permute-start.9 = (bf16[64,2048]{1,0:T(8,128)(2,1)S(1)}, bf16[64,2048]{1,0:T(8,128)(2,1)S(1)}, u32[]{:S(2)}, u32[]{:S(2)}) collective-permute-start(bf16[64,2048]{1,0:T(8,128)(2,1)S(1)} %collective-permute-done.7.refs_9_), channel_id=1, source_target_pairs={{0,16},{1,9},{2,18},{3,11},{4,20},{5,13},{6,22},{7,15},{8,24},{9,1... | collective-permute-start | bytes 786440 | tf_op jit(solution)/shard_map/ppermute | solution.py:67
  13.9 7.7 %collective-permute-start.6 = (bf16[32,2048]{1,0:T(8,128)(2,1)S(1)}, bf16[32,2048]{1,0:T(8,128)(2,1)S(1)}, u32[]{:S(2)}, u32[]{:S(2)}) collective-permute-start(bf16[32,2048]{1,0:T(8,128)(2,1)S(1)} %collective-permute-done.2.refs_3_), channel_id=1, source_target_pairs={{0,1},{1,0},{2,3},{3,2},{4,5},{5,4},{6,7},{7,6},{8,9},{9,8},{10,11... | collective-permute-start | bytes 393224 | tf_op jit(solution)/shard_map/ppermute | solution.py:75
  21.1 1.3 %collective-permute-start.5 = (bf16[32,2048]{1,0:T(8,128)(2,1)S(1)}, bf16[32,2048]{1,0:T(8,128)(2,1)S(1)}, u32[]{:S(2)}, u32[]{:S(2)}) collective-permute-start(bf16[32,2048]{1,0:T(8,128)(2,1)S(1)} %collective-permute-done.1.refs_2_), channel_id=1, source_target_pairs={{0,1},{1,0},{2,3},{3,2},{4,5},{5,4},{6,7},{7,6},{8,9},{9,8},{10,11... | collective-permute-start | bytes 393224 | tf_op jit(solution)/shard_map/ppermute | solution.py:75
  21.1 1.5 %collective-permute-start.4 = (bf16[32,2048]{1,0:T(8,128)(2,1)S(1)}, bf16[32,2048]{1,0:T(8,128)(2,1)S(1)}, u32[]{:S(2)}, u32[]{:S(2)}) collective-permute-start(bf16[32,2048]{1,0:T(8,128)(2,1)S(1)} %collective-permute-done.refs_1_), channel_id=1, source_target_pairs={{0,1},{1,0},{2,3},{3,2},{4,5},{5,4},{6,7},{7,6},{8,9},{9,8},{10,11... | collective-permute-start | bytes 393224 | tf_op jit(solution)/shard_map/ppermute | solution.py:75
  25.0 35.8 %copy-start.3 = (f32[2048,64]{0,1:T(8,128)S(1)}, f32[2048,64]{0,1:T(8,128)}, u32[]{:S(2)}) copy-start(f32[2048,64]{0,1:T(8,128)} %param.15) | copy-start | bytes 1572868
  25.0 45.2 %copy-start.7 = (f32[2048,64]{0,1:T(8,128)S(1)}, f32[2048,64]{0,1:T(8,128)}, u32[]{:S(2)}) copy-start(f32[2048,64]{0,1:T(8,128)} %param.14) | copy-start | bytes 1572868
  25.0 54.0 %copy-start.5 = (f32[2048,32]{0,1:T(8,128)S(1)}, f32[2048,32]{0,1:T(8,128)}, u32[]{:S(2)}) copy-start(f32[2048,32]{0,1:T(8,128)} %param.12) | copy-start | bytes 786436
  25.0 55.8 %copy-start.8 = (f32[2048,32]{0,1:T(8,128)S(1)}, f32[2048,32]{0,1:T(8,128)}, u32[]{:S(2)}) copy-start(f32[2048,32]{0,1:T(8,128)} %param.11) | copy-start | bytes 786436
  45.6 9.2 %collective-permute-start.14 = (bf16[64,2048]{1,0:T(8,128)(2,1)S(1)}, bf16[64,2048]{1,0:T(8,128)(2,1)S(1)}, u32[]{:S(2)}, u32[]{:S(2)}) collective-permute-start(bf16[64,2048]{1,0:T(8,128)(2,1)S(1)} %get-tuple-element.27), channel_id=1, source_target_pairs={{0,8},{8,0},{16,24},{24,16},{1,9},{9,1},{17,25},{25,17},{2,10},{10... | collective-permute-start | bytes 786440 | tf_op jit(solution)/shard_map/ppermute | solution.py:223
  46.3 12.9 %collective-permute-start.15 = (bf16[64,2048]{1,0:T(8,128)(2,1)S(1)}, bf16[64,2048]{1,0:T(8,128)(2,1)S(1)}, u32[]{:S(2)}, u32[]{:S(2)}) collective-permute-start(bf16[64,2048]{1,0:T(8,128)(2,1)S(1)} %get-tuple-element.28), channel_id=1, source_target_pairs={{0,16},{8,24},{16,0},{24,8},{1,17},{9,25},{17,1},{25,9},{2,18},{10... | collective-permute-start | bytes 786440 | tf_op jit(solution)/shard_map/ppermute | solution.py:223
  47.8 13.0 %collective-permute-start.16 = (bf16[64,2048]{1,0:T(8,128)(2,1)S(1)}, bf16[64,2048]{1,0:T(8,128)(2,1)S(1)}, u32[]{:S(2)}, u32[]{:S(2)}) collective-permute-start(bf16[64,2048]{1,0:T(8,128)(2,1)S(1)} %get-tuple-element.29), channel_id=1, source_target_pairs={{0,24},{8,16},{16,8},{24,0},{1,25},{9,17},{17,9},{25,1},{2,26},{10... | collective-permute-start | bytes 786440 | tf_op jit(solution)/shard_map/ppermute | solution.py:223
  49.2 13.7 %collective-permute-start.10 = (bf16[128,2048]{1,0:T(8,128)(2,1)}, bf16[128,2048]{1,0:T(8,128)(2,1)S(1)}, u32[]{:S(2)}, u32[]{:S(2)}) collective-permute-start(bf16[128,2048]{1,0:T(8,128)(2,1)} %get-tuple-element.21), channel_id=1, source_target_pairs={{0,1},{1,0},{2,3},{3,2},{4,5},{5,4},{6,7},{7,6},{8,9},{9,8},{10,11... | collective-permute-start | bytes 1572872 | tf_op jit(solution)/shard_map/ppermute | solution.py:225
  65.8 7.1 %collective-permute-start.11 = (bf16[32,2048]{1,0:T(8,128)(2,1)}, bf16[32,2048]{1,0:T(8,128)(2,1)S(1)}, u32[]{:S(2)}, u32[]{:S(2)}) collective-permute-start(bf16[32,2048]{1,0:T(8,128)(2,1)} %get-tuple-element.23), channel_id=1, source_target_pairs={{0,2},{1,3},{2,0},{3,1},{4,6},{5,7},{6,4},{7,5},{8,10},{9,11},{10,... | collective-permute-start | bytes 393224 | tf_op jit(solution)/shard_map/ppermute | solution.py:228
  65.8 13.2 %collective-permute-start.12 = (bf16[32,2048]{1,0:T(8,128)(2,1)}, bf16[32,2048]{1,0:T(8,128)(2,1)S(1)}, u32[]{:S(2)}, u32[]{:S(2)}) collective-permute-start(bf16[32,2048]{1,0:T(8,128)(2,1)} %get-tuple-element.24), channel_id=1, source_target_pairs={{0,4},{1,5},{2,6},{3,7},{4,0},{5,1},{6,2},{7,3},{8,12},{9,13},{10,... | collective-permute-start | bytes 393224 | tf_op jit(solution)/shard_map/ppermute | solution.py:228
  68.9 10.2 %collective-permute-start.13 = (bf16[32,2048]{1,0:T(8,128)(2,1)}, bf16[32,2048]{1,0:T(8,128)(2,1)S(1)}, u32[]{:S(2)}, u32[]{:S(2)}) collective-permute-start(bf16[32,2048]{1,0:T(8,128)(2,1)} %get-tuple-element.25), channel_id=1, source_target_pairs={{0,6},{1,7},{2,4},{3,5},{4,2},{5,3},{6,0},{7,1},{8,14},{9,15},{10,... | collective-permute-start | bytes 393224 | tf_op jit(solution)/shard_map/ppermute | solution.py:228
  (5 other events, 3.9 us)

commit v2 on v1

--- a/solution.py
+++ b/solution.py
@@ -16,7 +16,8 @@
 
 BF = jnp.bfloat16
 F32 = jnp.float32
-VMEM_BYTES = 52 * 2**20
+VMEM_BYTES = 34 * 2**20
+SMALL_VMEM = 8 * 2**20
 ROW_TILE = 512
 COL_TILE = 512
 
@@ -28,17 +29,17 @@
     return (factor - step_rate * update, moment_new, second_new)
 
 
-def cast_kernel(a_ref, d_ref, a_out, d_out):
-    a_out[...] = a_ref[...].astype(BF)
-    d_out[...] = d_ref[...].astype(BF)
-
-
-def cast_both(a, d):
+def cast_kernel(x_ref, out_ref):
+    out_ref[...] = x_ref[...].astype(BF)
+
+
+def cast(x):
     return pl.pallas_call(
         cast_kernel,
-        out_shape=(jax.ShapeDtypeStruct(a.shape, BF), jax.ShapeDtypeStruct(d.shape, BF)),
-        name="cast_factors",
-    )(a, d)
+        out_shape=jax.ShapeDtypeStruct(x.shape, BF),
+        compiler_params=pltpu.CompilerParams(vmem_limit_bytes=SMALL_VMEM),
+        name="cast_factor",
+    )(x)
 
 
 def swap_item(n_item, mask):
@@ -102,49 +103,40 @@
     for q, (even, odd) in enumerate(mp_masks(n_mp)):
         off = pl.multiple_of((m ^ jnp.where(core == 0, even, odd)) * kd, kd)
         copies.append(pltpu.make_async_copy(d_in[q], dt.at[pl.ds(off, kd)], sem_in.at[n_item + q]))
-    loads = []
-    for t in range(tiles):
-        rng = pl.ds(t * ROW_TILE, ROW_TILE)
-        loads.append(pltpu.make_async_copy(r_hbm.at[rng], resp.at[rng], sem_r.at[t]))
+
+    def load(t):
+        rng = pl.ds(pl.multiple_of(t * ROW_TILE, ROW_TILE), ROW_TILE)
+        return pltpu.make_async_copy(r_hbm.at[rng], resp.at[rng], sem_r.at[t])
+
     for c in copies:
         c.start()
-    for c in loads:
-        c.start()
+    for t in range(tiles):
+        load(t).start()
     for c in copies:
         c.wait()
 
-    n_cols = cols // COL_TILE
-    sub = ROW_TILE // n_cols
-    for t in range(tiles + 1):
-        if t < tiles:
-            loads[t].wait()
-            rng = slice(t * ROW_TILE, (t + 1) * ROW_TILE)
-            half = (at[:, rng].astype(F32) * 0.5).T.astype(BF)
-        if t > 0:
-            old = slice((t - 1) * ROW_TILE, t * ROW_TILE)
-            at_old = at[:, old]
-        for c in range(n_cols):
-            cr = slice(c * COL_TILE, (c + 1) * COL_TILE)
-            if t < tiles:
-                lg = jnp.dot(half, dt[:, cr], preferred_element_type=F32) + 0.5 * diff_ref[:, cr]
-                r = resp[rng, cr]
-                sign = jnp.where(r == 2, -1.0, 1.0)
-                rs[t % 2, :, cr] = jnp.where(r == 0, 0.0, jnp.tanh(lg) + sign).astype(BF)
-            if t > 0:
-                p = (t - 1) % 2
-                h = jnp.dot(at_old, rs[p, :, cr], preferred_element_type=F32)
-                if t == 1:
-                    acc[:, cr] = h
-                else:
-                    acc[:, cr] += h
-                g = lax.dot_general(
-                    rs[p, c * sub : (c + 1) * sub, :],
-                    dt[...],
-                    (((1,), (1,)), ((), ())),
-                    preferred_element_type=F32,
-                )
-                lo = (t - 1) * ROW_TILE + c * sub
-                gs[:, lo : lo + sub] = g.T
+    acc[...] = jnp.zeros_like(acc)
+
+    def step(t, carry):
+        rng = pl.ds(pl.multiple_of(t * ROW_TILE, ROW_TILE), ROW_TILE)
+        load(t).wait()
+        a_tile = at[:, rng]
+        half = (a_tile.astype(F32) * 0.5).T.astype(BF)
+        for c in range(0, cols, COL_TILE):
+            cr = slice(c, c + COL_TILE)
+            lg = jnp.dot(half, dt[:, cr], preferred_element_type=F32) + 0.5 * diff_ref[:, cr]
+            r = resp[rng, cr]
+            sign = jnp.where(r == 2, -1.0, 1.0)
+            rs[:, cr] = jnp.where(r == 0, 0.0, jnp.tanh(lg) + sign).astype(BF)
+        gs[:, rng] = lax.dot_general(
+            dt[...], rs[...], (((1,), (1,)), ((), ())), preferred_element_type=F32
+        )
+        for c in range(0, cols, COL_TILE):
+            cr = slice(c, c + COL_TILE)
+            acc[:, cr] += jnp.dot(a_tile, rs[:, cr], preferred_element_type=F32)
+        return carry
+
+    lax.fori_loop(0, tiles, step, 0)
 
     for x in range(chips):
         dst = pl.ds(x * ka, ka)
@@ -175,7 +167,7 @@
             pltpu.VMEM((k, rows), BF),
             pltpu.VMEM((k, cols), BF),
             pltpu.VMEM((rows, cols), jnp.int32),
-            pltpu.VMEM((2, ROW_TILE, cols), BF),
+            pltpu.VMEM((ROW_TILE, cols), BF),
             pltpu.VMEM((k, rows), F32),
             pltpu.VMEM((k, cols), F32),
             pltpu.SemaphoreType.DMA((n_item + n_mp,)),
@@ -202,8 +194,28 @@
     return pl.pallas_call(
         functools.partial(pair_kernel, ka),
         out_shape=[shape((ka, rows), F32)] + [shape((ka, rows), BF)] * (chips - 1),
+        compiler_params=pltpu.CompilerParams(vmem_limit_bytes=SMALL_VMEM),
         name="core_pair_sum",
     )(keep, got)
+
+
+def adam_kernel(n_sums, scale, rate, *refs):
+    sums, (x_ref, m_ref, v_ref, x_out, m_out, v_out) = refs[:n_sums], refs[n_sums:]
+    g = sums[0][...]
+    for part in sums[1:]:
+        g = g + part[...].astype(F32)
+    x_out[...], m_out[...], v_out[...] = adam_update(
+        x_ref[...], m_ref[...], v_ref[...], g * scale, rate
+    )
+
+
+def adam(sums, x, m, v, scale, rate):
+    return pl.pallas_call(
+        functools.partial(adam_kernel, len(sums), scale, rate),
+        out_shape=[jax.ShapeDtypeStruct(x.shape, F32)] * 3,
+        compiler_params=pltpu.CompilerParams(vmem_limit_bytes=SMALL_VMEM),
+        name="adam",
+    )(*sums, x, m, v)
 
 
 def shards(response, difficulty, ability, ability_m, ability_v, discrim, discrim_m, discrim_v):
@@ -212,32 +224,33 @@
     rows, cols = response.shape
     k = discrim.shape[1] * n_mp
     items_total, ckpts_total = cols * n_item, rows * n_mp
-    a_bf, d_bf = cast_both(ability.T, discrim.T)
-    d_blocks = gather_mp(d_bf, n_mp, n_item)
+    a_t, d_t = ability.T, discrim.T
+    a_bf = cast(a_t)
+    a_bf, d_late = lax.optimization_barrier((a_bf, d_t))
     a_blocks = gather_item(a_bf, n_item)
+    d_blocks = gather_mp(cast(d_late), n_mp, n_item)
     keep, give, *h = gradients(
         a_blocks, d_blocks, difficulty.reshape(1, cols), response, n_mp, n_item
     )
-    h_sum = h[0]
-    h_got = [
-        lax.ppermute(h[x], "mp", [(i, i ^ x) for i in range(n_mp)]) for x in range(1, n_mp)
-    ]
+
+    def swap_h(x):
+        return lax.ppermute(h[x], "mp", [(i, i ^ x) for i in range(n_mp)])
+
+    h_got = [swap_h(1)]
     got = lax.ppermute(give, "item", swap_item(n_item, 1))
     g_sum, *g = pair_sum(keep, got, chips)
+    g[0], *h[2:] = lax.optimization_barrier((g[0], *h[2:]))
     g_got = [
         lax.ppermute(g[x - 1], "item", swap_item(n_item, 2 * x)) for x in range(1, chips)
     ]
-    for b in g_got:
-        g_sum = g_sum + b.astype(F32)
-    for b in h_got:
-        h_sum = h_sum + b.astype(F32)
-    a_out = adam_update(
-        ability.T, ability_m.T, ability_v.T, g_sum * (0.5 * math.sqrt(k / items_total)), 0.05
-    )
-    d_out = adam_update(
-        discrim.T, discrim_m.T, discrim_v.T, h_sum * (0.5 * math.sqrt(1.0 / ckpts_total)), 0.01
-    )
-    return tuple(x.T for x in a_out + d_out)
+    h_got += [swap_h(x) for x in range(2, n_mp)]
+    d_out = adam(
+        [h[0]] + h_got, d_t, discrim_m.T, discrim_v.T, 0.5 * math.sqrt(1.0 / ckpts_total), 0.01
+    )
+    a_out = adam(
+        [g_sum] + g_got, a_t, ability_m.T, ability_v.T, 0.5 * math.sqrt(k / items_total), 0.05
+    )
+    return tuple(x.T for x in (*a_out, *d_out))
 
 
 def solution(mesh):

time: 82.1 us -> 58.3 us (0.71)
  waiting for transfers between devices: 29.1 us -> 19.6 us
  Pallas kernels: 24.7 us -> 16.5 us
  other arithmetic: 6.09 us -> 0 us
    ppermute x3, waiting for transfers between devices: 11.6 us -> 0.01 us  [swap_h(): return lax.ppermute(h[x], 'mp', [(i, i ^ x) for i in range(n_mp)])]
    pallas_call x1, Pallas kernels: 20.6 us -> 13.9 us  [gradients(): pl.pallas_call(functools.partial(grad_kernel, n_mp, n_item), out_shape=ou...]
    transpose x4 -> x0, other arithmetic: 6.09 us -> none  [shards(): return tuple((x.T for x in a_out + d_out))]
    pallas_call x1, Pallas kernels: 2.2 us -> 0.12 us  [pair_sum(): pl.pallas_call(functools.partial(pair_kernel, ka), out_shape=[shape((ka,...]
    ppermute x1, waiting for transfers between devices: 0.01 us -> 1.59 us  [shards(): got = lax.ppermute(give, 'item', swap_item(n_item, 1))]
    pallas_call x1 -> x4, Pallas kernels: 1.95 us -> 2.48 us  [the longest x2 2.44 us: adam(): pl.pallas_call(functools.partial(adam_kernel, len(sums), scale, rate), ou...]
    unnamed x24 -> x18, local copies, waits for them, and re-layouts: 3.18 us -> 2.74 us
  transfers between devices with their start and end apart: 17 -> 17, of which waited for: 9 -> 6; matrix products, arithmetic and copies ran while one was open for 4% -> 0% of each run, Pallas kernels for 0% -> 2%
where the time goes in v2:
time: 58.3 us; the launch traced here: 58.1 us
  waiting for transfers between devices  19.6 us (34%)
  starting transfers between devices  18.6 us (32%)
  Pallas kernels  16.5 us (28%)
  local copies, waits for them, and re-layouts  2.74 us (5%)
  between operations  0.75 us (1%)
    pallas_call x1, Pallas kernels, gradients(): pl.pallas_call(functools.partial(grad_kernel, n_mp, n_item), out_shape=ou...  13.9 us
    ppermute x3, waiting for transfers between devices, gather_item(): lax.ppermute(a, 'item', swap_item(n_item, 2 * x))  8.92 us
    ppermute x3, waiting for transfers between devices, shards(): lax.ppermute(g[x - 1], 'item', swap_item(n_item, 2 * x))  8.04 us
    ppermute x3, starting transfers between devices, gather_mp(): blocks += [lax.ppermute(b, ('mp', 'item'), perm) for b in blocks]  5.03 us
    ppermute x3, starting transfers between devices, shards(): lax.ppermute(g[x - 1], 'item', swap_item(n_item, 2 * x))  4.69 us
    ppermute x3, starting transfers between devices, gather_item(): lax.ppermute(a, 'item', swap_item(n_item, 2 * x))  4.39 us
    ppermute x3, starting transfers between devices, swap_h(): return lax.ppermute(h[x], 'mp', [(i, i ^ x) for i in range(n_mp)])  3.55 us
    unnamed x18, local copies, waits for them, and re-layouts  2.74 us
  transfers between devices with their start and end apart: 17, of which 6 were waited for; matrix products, arithmetic and copies ran while one was open for 0% of the time, Pallas kernels for 2%

profile of v2, /device:TPU:0, one launch (start us, length us, event | category | flops | bytes accessed | tf_op | source)
XLA Modules:
  0.0 58.1 jit_solution(5359819041748565066)
XLA Ops:
  0.6 0.9 %copy-done.2 = f32[2048,32]{0,1:T(8,128)S(1)} copy-done((f32[2048,32]{0,1:T(8,128)S(1)}, f32[2048,32]{0,1:T(8,128)}, u32[]{:S(2)}) %copy-start.2) | copy-done | bytes 262168
  1.6 1.1 %copy-done = f32[2048,64]{0,1:T(8,128)S(1)} copy-done((f32[2048,64]{0,1:T(8,128)S(1)}, f32[2048,64]{0,1:T(8,128)}, u32[]{:S(2)}) %copy-start) | copy-done | bytes 524312
  2.7 3.0 %collective-permute-start.7 = (bf16[64,2048]{1,0:T(8,128)(2,1)S(1)}, bf16[64,2048]{1,0:T(8,128)(2,1)S(1)}, u32[]{:S(2)}, u32[]{:S(2)}) collective-permute-start(bf16[64,2048]{1,0:T(8,128)(2,1)S(1)} %cast_factor.3.refs_8_), channel_id=1, source_target_pairs={{0,8},{1,17},{2,10},{3,19},{4,12},{5,21},{6,14},{7,23},{8,0},{9,25... | collective-permute-start | bytes 786440 | tf_op jit(solution)/shard_map/ppermute | solution.py:68
  5.8 3.6 %collective-permute-start.2 = (bf16[32,2048]{1,0:T(8,128)(2,1)S(1)}, bf16[32,2048]{1,0:T(8,128)(2,1)S(1)}, u32[]{:S(2)}, u32[]{:S(2)}) collective-permute-start(bf16[32,2048]{1,0:T(8,128)(2,1)S(1)} %cast_factor.2.refs_0_), channel_id=1, source_target_pairs={{0,6},{1,7},{2,4},{3,5},{4,2},{5,3},{6,0},{7,1},{8,14},{9,15},{10,... | collective-permute-start | bytes 393224 | tf_op jit(solution)/shard_map/ppermute | solution.py:75
  9.4 0.8 %collective-permute-start = (bf16[32,2048]{1,0:T(8,128)(2,1)S(1)}, bf16[32,2048]{1,0:T(8,128)(2,1)S(1)}, u32[]{:S(2)}, u32[]{:S(2)}) collective-permute-start(bf16[32,2048]{1,0:T(8,128)(2,1)S(1)} %cast_factor.2.refs_0_), channel_id=1, source_target_pairs={{0,2},{1,3},{2,0},{3,1},{4,6},{5,7},{6,4},{7,5},{8,10},{9,11},{10,... | collective-permute-start | bytes 393224 | tf_op jit(solution)/shard_map/ppermute | solution.py:75
  10.1 1.5 %collective-permute-start.8 = (bf16[64,2048]{1,0:T(8,128)(2,1)S(1)}, bf16[64,2048]{1,0:T(8,128)(2,1)S(1)}, u32[]{:S(2)}, u32[]{:S(2)}) collective-permute-start(bf16[64,2048]{1,0:T(8,128)(2,1)S(1)} %cast_factor.3.refs_8_), channel_id=1, source_target_pairs={{0,16},{1,9},{2,18},{3,11},{4,20},{5,13},{6,22},{7,15},{8,24},{9,1... | collective-permute-start | bytes 786440 | tf_op jit(solution)/shard_map/ppermute | solution.py:68
  11.7 0.5 collective-permute-start.9
  12.2 1.8 %collective-permute-done.2.refs_3_ = bf16[32,2048]{1,0:T(8,128)(2,1)S(1)} collective-permute-done((bf16[32,2048]{1,0:T(8,128)(2,1)S(1)}, bf16[32,2048]{1,0:T(8,128)(2,1)S(1)}, u32[]{:S(2)}, u32[]{:S(2)}) %collective-permute-start.2) | collective-permute-done | bytes 131104 | tf_op jit(solution)/shard_map/ppermute | solution.py:75
  13.9 7.2 %collective-permute-done.1.refs_2_ = bf16[32,2048]{1,0:T(8,128)(2,1)S(1)} collective-permute-done((bf16[32,2048]{1,0:T(8,128)(2,1)S(1)}, bf16[32,2048]{1,0:T(8,128)(2,1)S(1)}, u32[]{:S(2)}, u32[]{:S(2)}) %collective-permute-start.1) | collective-permute-done | bytes 131104 | tf_op jit(solution)/shard_map/ppermute | solution.py:75
  21.1 0.5 collective-permute-start.4
  21.6 0.8 %collective-permute-done.5.refs_6_ = bf16[32,2048]{1,0:T(8,128)(2,1)S(1)} collective-permute-done((bf16[32,2048]{1,0:T(8,128)(2,1)S(1)}, bf16[32,2048]{1,0:T(8,128)(2,1)S(1)}, u32[]{:S(2)}, u32[]{:S(2)}) %collective-permute-start.5) | collective-permute-done | bytes 131104 | tf_op jit(solution)/shard_map/ppermute | solution.py:76
  22.5 0.2 collective-permute-done.4.refs_5_
  22.7 0.7 %copy-done.8 = f32[2048]{0:T(1024)S(1)} copy-done((f32[2048]{0:T(1024)S(1)}, f32[2048]{0:T(1024)}, u32[]{:S(2)}) %copy-start.8) | copy-done | bytes 8216
  23.3 13.9 %residual_gradients.1 = (f32[128,2048]{1,0:T(8,128)S(1)}, bf16[128,2048]{1,0:T(8,128)(2,1)S(1)}, f32[64,2048]{1,0:T(8,128)S(1)}, bf16[64,2048]{1,0:T(8,128)(2,1)...) custom-call(bf16[32,2048]{1,0:T(8,128)(2,1)S(1)} %cast_factor.2.refs_0_, ...), custom_call_target="tpu_custom_call" | custom-call | flops 6442450944 | bytes 16777216 | tf_op jit(solution)/shard_map/residual_gradients/pallas_call | solution.py:161
  37.2 0.4 collective-permute-start.10
  37.6 1.6 %collective-permute-done.10.got_ref = bf16[128,2048]{1,0:T(8,128)(2,1)S(1)} collective-permute-done((bf16[128,2048]{1,0:T(8,128)(2,1)S(1)}, bf16[128,2048]{1,0:T(8,128)(2,1)S(1)}, u32[]{:S(2)}, u32[]{:S(2)}) %collective-permute-start.10) | collective-permute-done | bytes 524320 | tf_op jit(solution)/shard_map/ppermute | solution.py:240
  39.4 0.6 %collective-permute-start.14 = (bf16[64,2048]{1,0:T(8,128)(2,1)S(1)}, bf16[64,2048]{1,0:T(8,128)(2,1)S(1)}, u32[]{:S(2)}, u32[]{:S(2)}) collective-permute-start(bf16[64,2048]{1,0:T(8,128)(2,1)S(1)} %get-tuple-element.42), channel_id=1, source_target_pairs={{0,8},{8,0},{16,24},{24,16},{1,9},{9,1},{17,25},{25,17},{2,10},{10... | collective-permute-start | bytes 786440 | tf_op jit(solution)/shard_map/ppermute | solution.py:237
  40.0 1.5 %collective-permute-start.15 = (bf16[64,2048]{1,0:T(8,128)(2,1)S(1)}, bf16[64,2048]{1,0:T(8,128)(2,1)S(1)}, u32[]{:S(2)}, u32[]{:S(2)}) collective-permute-start(bf16[64,2048]{1,0:T(8,128)(2,1)S(1)} %get-tuple-element.43), channel_id=1, source_target_pairs={{0,16},{8,24},{16,0},{24,8},{1,17},{9,25},{17,1},{25,9},{2,18},{10... | collective-permute-start | bytes 786440 | tf_op jit(solution)/shard_map/ppermute | solution.py:237
  41.5 1.4 %collective-permute-start.16 = (bf16[64,2048]{1,0:T(8,128)(2,1)S(1)}, bf16[64,2048]{1,0:T(8,128)(2,1)S(1)}, u32[]{:S(2)}, u32[]{:S(2)}) collective-permute-start(bf16[64,2048]{1,0:T(8,128)(2,1)S(1)} %get-tuple-element.44), channel_id=1, source_target_pairs={{0,24},{8,16},{16,8},{24,0},{1,25},{9,17},{17,9},{25,1},{2,26},{10... | collective-permute-start | bytes 786440 | tf_op jit(solution)/shard_map/ppermute | solution.py:237
  43.0 3.0 %collective-permute-start.12 = (bf16[32,2048]{1,0:T(8,128)(2,1)S(1)}, bf16[32,2048]{1,0:T(8,128)(2,1)S(1)}, u32[]{:S(2)}, u32[]{:S(2)}) collective-permute-start(bf16[32,2048]{1,0:T(8,128)(2,1)S(1)} %get-tuple-element.36), channel_id=1, source_target_pairs={{0,4},{1,5},{2,6},{3,7},{4,0},{5,1},{6,2},{7,3},{8,12},{9,13},{10,... | collective-permute-start | bytes 393224 | tf_op jit(solution)/shard_map/ppermute | solution.py:244
  45.9 1.7 %collective-permute-start.13 = (bf16[32,2048]{1,0:T(8,128)(2,1)S(1)}, bf16[32,2048]{1,0:T(8,128)(2,1)S(1)}, u32[]{:S(2)}, u32[]{:S(2)}) collective-permute-start(bf16[32,2048]{1,0:T(8,128)(2,1)S(1)} %get-tuple-element.37), channel_id=1, source_target_pairs={{0,6},{1,7},{2,4},{3,5},{4,2},{5,3},{6,0},{7,1},{8,14},{9,15},{10,... | collective-permute-start | bytes 393224 | tf_op jit(solution)/shard_map/ppermute | solution.py:244
  47.6 8.0 %collective-permute-done.12.refs_2_ = bf16[32,2048]{1,0:T(8,128)(2,1)S(1)} collective-permute-done((bf16[32,2048]{1,0:T(8,128)(2,1)S(1)}, bf16[32,2048]{1,0:T(8,128)(2,1)S(1)}, u32[]{:S(2)}, u32[]{:S(2)}) %collective-permute-start.12) | collective-permute-done | bytes 131104 | tf_op jit(solution)/shard_map/ppermute | solution.py:244
  55.7 1.0 %adam.2 = (f32[32,2048]{1,0:T(8,128)}, f32[32,2048]{1,0:T(8,128)}, f32[32,2048]{1,0:T(8,128)}) custom-call(f32[32,2048]{1,0:T(8,128)S(1)} %get-tuple-element.31.refs_0_, bf16[32,2048]{1,0:T(8,128)(2,1)S(1)} %collective-permute-done.11.refs_1_, bf16[32,2048]{1,0:T(8,128)(2,1)S(1)} %collective-permute-done.12.refs_2_, ...), custom_call_target="tpu_custom_call" | custom-call | tf_op jit(solution)/shard_map/adam/pallas_call | solution.py:213
  56.7 1.4 %adam.3 = (f32[64,2048]{1,0:T(8,128)}, f32[64,2048]{1,0:T(8,128)}, f32[64,2048]{1,0:T(8,128)}) custom-call(f32[64,2048]{1,0:T(8,128)S(1)} %get-tuple-element.41.refs_0_, bf16[64,2048]{1,0:T(8,128)(2,1)S(1)} %collective-permute-done.14.refs_1_, bf16[64,2048]{1,0:T(8,128)(2,1)S(1)} %collective-permute-done.15.refs_2_, ...), custom_call_target="tpu_custom_call" | custom-call | tf_op jit(solution)/shard_map/adam/pallas_call | solution.py:213
  (34 shorter events, 0.3 us)
Async XLA Ops:
  1.6 54.1 %copy-start.3 = (f32[2048,32]{0,1:T(8,128)S(1)}, f32[2048,32]{0,1:T(8,128)}, u32[]{:S(2)}) copy-start(f32[2048,32]{0,1:T(8,128)} %param.10) | copy-start | bytes 786436
  1.6 1.1 %copy-start = (f32[2048,64]{0,1:T(8,128)S(1)}, f32[2048,64]{0,1:T(8,128)}, u32[]{:S(2)}) copy-start(f32[2048,64]{0,1:T(8,128)} %param.13) | copy-start | bytes 1572868
  2.7 53.0 %copy-start.6 = (f32[2048,32]{0,1:T(8,128)S(1)}, f32[2048,32]{0,1:T(8,128)}, u32[]{:S(2)}) copy-start(f32[2048,32]{0,1:T(8,128)} %param.11) | copy-start | bytes 786436
  2.7 53.0 %copy-start.7 = (f32[2048,32]{0,1:T(8,128)S(1)}, f32[2048,32]{0,1:T(8,128)}, u32[]{:S(2)}) copy-start(f32[2048,32]{0,1:T(8,128)} %param.12) | copy-start | bytes 786436
  2.7 54.0 %copy-start.1 = (f32[2048,64]{0,1:T(8,128)S(1)}, f32[2048,64]{0,1:T(8,128)}, u32[]{:S(2)}) copy-start(f32[2048,64]{0,1:T(8,128)} %param.13) | copy-start | bytes 1572868
  2.7 54.0 %copy-start.4 = (f32[2048,64]{0,1:T(8,128)S(1)}, f32[2048,64]{0,1:T(8,128)}, u32[]{:S(2)}) copy-start(f32[2048,64]{0,1:T(8,128)} %param.14) | copy-start | bytes 1572868
  2.7 54.0 %copy-start.5 = (f32[2048,64]{0,1:T(8,128)S(1)}, f32[2048,64]{0,1:T(8,128)}, u32[]{:S(2)}) copy-start(f32[2048,64]{0,1:T(8,128)} %param.15) | copy-start | bytes 1572868
  2.7 8.9 %collective-permute-start.7 = (bf16[64,2048]{1,0:T(8,128)(2,1)S(1)}, bf16[64,2048]{1,0:T(8,128)(2,1)S(1)}, u32[]{:S(2)}, u32[]{:S(2)}) collective-permute-start(bf16[64,2048]{1,0:T(8,128)(2,1)S(1)} %cast_factor.3.refs_8_), channel_id=1, source_target_pairs={{0,8},{1,17},{2,10},{3,19},{4,12},{5,21},{6,14},{7,23},{8,0},{9,25... | collective-permute-start | bytes 786440 | tf_op jit(solution)/shard_map/ppermute | solution.py:68
  5.8 4.4 %collective-permute-start.3 = (bf16[32,2048]{1,0:T(8,128)(2,1)S(1)}, bf16[32,2048]{1,0:T(8,128)(2,1)S(1)}, u32[]{:S(2)}, u32[]{:S(2)}) collective-permute-start(bf16[32,2048]{1,0:T(8,128)(2,1)S(1)} %cast_factor.2.refs_0_), channel_id=1, source_target_pairs={{0,1},{1,0},{2,3},{3,2},{4,5},{5,4},{6,7},{7,6},{8,9},{9,8},{10,11... | collective-permute-start | bytes 393224 | tf_op jit(solution)/shard_map/ppermute | solution.py:76
  5.8 8.2 %collective-permute-start.2 = (bf16[32,2048]{1,0:T(8,128)(2,1)S(1)}, bf16[32,2048]{1,0:T(8,128)(2,1)S(1)}, u32[]{:S(2)}, u32[]{:S(2)}) collective-permute-start(bf16[32,2048]{1,0:T(8,128)(2,1)S(1)} %cast_factor.2.refs_0_), channel_id=1, source_target_pairs={{0,6},{1,7},{2,4},{3,5},{4,2},{5,3},{6,0},{7,1},{8,14},{9,15},{10,... | collective-permute-start | bytes 393224 | tf_op jit(solution)/shard_map/ppermute | solution.py:75
  9.4 11.7 %collective-permute-start.1 = (bf16[32,2048]{1,0:T(8,128)(2,1)S(1)}, bf16[32,2048]{1,0:T(8,128)(2,1)S(1)}, u32[]{:S(2)}, u32[]{:S(2)}) collective-permute-start(bf16[32,2048]{1,0:T(8,128)(2,1)S(1)} %cast_factor.2.refs_0_), channel_id=1, source_target_pairs={{0,4},{1,5},{2,6},{3,7},{4,0},{5,1},{6,2},{7,3},{8,12},{9,13},{10,... | collective-permute-start | bytes 393224 | tf_op jit(solution)/shard_map/ppermute | solution.py:75
  9.4 11.8 %collective-permute-start = (bf16[32,2048]{1,0:T(8,128)(2,1)S(1)}, bf16[32,2048]{1,0:T(8,128)(2,1)S(1)}, u32[]{:S(2)}, u32[]{:S(2)}) collective-permute-start(bf16[32,2048]{1,0:T(8,128)(2,1)S(1)} %cast_factor.2.refs_0_), channel_id=1, source_target_pairs={{0,2},{1,3},{2,0},{3,1},{4,6},{5,7},{6,4},{7,5},{8,10},{9,11},{10,... | collective-permute-start | bytes 393224 | tf_op jit(solution)/shard_map/ppermute | solution.py:75
  10.1 12.5 %collective-permute-start.8 = (bf16[64,2048]{1,0:T(8,128)(2,1)S(1)}, bf16[64,2048]{1,0:T(8,128)(2,1)S(1)}, u32[]{:S(2)}, u32[]{:S(2)}) collective-permute-start(bf16[64,2048]{1,0:T(8,128)(2,1)S(1)} %cast_factor.3.refs_8_), channel_id=1, source_target_pairs={{0,16},{1,9},{2,18},{3,11},{4,20},{5,13},{6,22},{7,15},{8,24},{9,1... | collective-permute-start | bytes 786440 | tf_op jit(solution)/shard_map/ppermute | solution.py:68
  11.7 11.0 %collective-permute-start.9 = (bf16[64,2048]{1,0:T(8,128)(2,1)S(1)}, bf16[64,2048]{1,0:T(8,128)(2,1)S(1)}, u32[]{:S(2)}, u32[]{:S(2)}) collective-permute-start(bf16[64,2048]{1,0:T(8,128)(2,1)S(1)} %collective-permute-done.7.refs_9_), channel_id=1, source_target_pairs={{0,16},{1,9},{2,18},{3,11},{4,20},{5,13},{6,22},{7,15},{8,24},{9,1... | collective-permute-start | bytes 786440 | tf_op jit(solution)/shard_map/ppermute | solution.py:68
  13.9 7.7 %collective-permute-start.6 = (bf16[32,2048]{1,0:T(8,128)(2,1)S(1)}, bf16[32,2048]{1,0:T(8,128)(2,1)S(1)}, u32[]{:S(2)}, u32[]{:S(2)}) collective-permute-start(bf16[32,2048]{1,0:T(8,128)(2,1)S(1)} %collective-permute-done.2.refs_3_), channel_id=1, source_target_pairs={{0,1},{1,0},{2,3},{3,2},{4,5},{5,4},{6,7},{7,6},{8,9},{9,8},{10,11... | collective-permute-start | bytes 393224 | tf_op jit(solution)/shard_map/ppermute | solution.py:76
  21.1 1.3 %collective-permute-start.5 = (bf16[32,2048]{1,0:T(8,128)(2,1)S(1)}, bf16[32,2048]{1,0:T(8,128)(2,1)S(1)}, u32[]{:S(2)}, u32[]{:S(2)}) collective-permute-start(bf16[32,2048]{1,0:T(8,128)(2,1)S(1)} %collective-permute-done.1.refs_2_), channel_id=1, source_target_pairs={{0,1},{1,0},{2,3},{3,2},{4,5},{5,4},{6,7},{7,6},{8,9},{9,8},{10,11... | collective-permute-start | bytes 393224 | tf_op jit(solution)/shard_map/ppermute | solution.py:76
  21.1 1.5 %collective-permute-start.4 = (bf16[32,2048]{1,0:T(8,128)(2,1)S(1)}, bf16[32,2048]{1,0:T(8,128)(2,1)S(1)}, u32[]{:S(2)}, u32[]{:S(2)}) collective-permute-start(bf16[32,2048]{1,0:T(8,128)(2,1)S(1)} %collective-permute-done.refs_1_), channel_id=1, source_target_pairs={{0,1},{1,0},{2,3},{3,2},{4,5},{5,4},{6,7},{7,6},{8,9},{9,8},{10,11... | collective-permute-start | bytes 393224 | tf_op jit(solution)/shard_map/ppermute | solution.py:76
  37.2 2.0 %collective-permute-start.10 = (bf16[128,2048]{1,0:T(8,128)(2,1)S(1)}, bf16[128,2048]{1,0:T(8,128)(2,1)S(1)}, u32[]{:S(2)}, u32[]{:S(2)}) collective-permute-start(bf16[128,2048]{1,0:T(8,128)(2,1)S(1)} %get-tuple-element.30), channel_id=1, source_target_pairs={{0,1},{1,0},{2,3},{3,2},{4,5},{5,4},{6,7},{7,6},{8,9},{9,8},{10,11... | collective-permute-start | bytes 1572872 | tf_op jit(solution)/shard_map/ppermute | solution.py:240
  39.3 6.6 %collective-permute-start.11 = (bf16[32,2048]{1,0:T(8,128)(2,1)S(1)}, bf16[32,2048]{1,0:T(8,128)(2,1)S(1)}, u32[]{:S(2)}, u32[]{:S(2)}) collective-permute-start(bf16[32,2048]{1,0:T(8,128)(2,1)S(1)} %get-tuple-element.35), channel_id=1, source_target_pairs={{0,2},{1,3},{2,0},{3,1},{4,6},{5,7},{6,4},{7,5},{8,10},{9,11},{10,... | collective-permute-start | bytes 393224 | tf_op jit(solution)/shard_map/ppermute | solution.py:244
  39.4 17.3 %collective-permute-start.14 = (bf16[64,2048]{1,0:T(8,128)(2,1)S(1)}, bf16[64,2048]{1,0:T(8,128)(2,1)S(1)}, u32[]{:S(2)}, u32[]{:S(2)}) collective-permute-start(bf16[64,2048]{1,0:T(8,128)(2,1)S(1)} %get-tuple-element.42), channel_id=1, source_target_pairs={{0,8},{8,0},{16,24},{24,16},{1,9},{9,1},{17,25},{25,17},{2,10},{10... | collective-permute-start | bytes 786440 | tf_op jit(solution)/shard_map/ppermute | solution.py:237
  40.0 16.6 %collective-permute-start.15 = (bf16[64,2048]{1,0:T(8,128)(2,1)S(1)}, bf16[64,2048]{1,0:T(8,128)(2,1)S(1)}, u32[]{:S(2)}, u32[]{:S(2)}) collective-permute-start(bf16[64,2048]{1,0:T(8,128)(2,1)S(1)} %get-tuple-element.43), channel_id=1, source_target_pairs={{0,16},{8,24},{16,0},{24,8},{1,17},{9,25},{17,1},{25,9},{2,18},{10... | collective-permute-start | bytes 786440 | tf_op jit(solution)/shard_map/ppermute | solution.py:237
  41.5 15.1 %collective-permute-start.16 = (bf16[64,2048]{1,0:T(8,128)(2,1)S(1)}, bf16[64,2048]{1,0:T(8,128)(2,1)S(1)}, u32[]{:S(2)}, u32[]{:S(2)}) collective-permute-start(bf16[64,2048]{1,0:T(8,128)(2,1)S(1)} %get-tuple-element.44), channel_id=1, source_target_pairs={{0,24},{8,16},{16,8},{24,0},{1,25},{9,17},{17,9},{25,1},{2,26},{10... | collective-permute-start | bytes 786440 | tf_op jit(solution)/shard_map/ppermute | solution.py:237
  43.0 12.7 %collective-permute-start.12 = (bf16[32,2048]{1,0:T(8,128)(2,1)S(1)}, bf16[32,2048]{1,0:T(8,128)(2,1)S(1)}, u32[]{:S(2)}, u32[]{:S(2)}) collective-permute-start(bf16[32,2048]{1,0:T(8,128)(2,1)S(1)} %get-tuple-element.36), channel_id=1, source_target_pairs={{0,4},{1,5},{2,6},{3,7},{4,0},{5,1},{6,2},{7,3},{8,12},{9,13},{10,... | collective-permute-start | bytes 393224 | tf_op jit(solution)/shard_map/ppermute | solution.py:244
  45.9 9.7 %collective-permute-start.13 = (bf16[32,2048]{1,0:T(8,128)(2,1)S(1)}, bf16[32,2048]{1,0:T(8,128)(2,1)S(1)}, u32[]{:S(2)}, u32[]{:S(2)}) collective-permute-start(bf16[32,2048]{1,0:T(8,128)(2,1)S(1)} %get-tuple-element.37), channel_id=1, source_target_pairs={{0,6},{1,7},{2,4},{3,5},{4,2},{5,3},{6,0},{7,1},{8,14},{9,15},{10,... | collective-permute-start | bytes 393224 | tf_op jit(solution)/shard_map/ppermute | solution.py:244
  (2 other events, 1.7 us)

commit v3 on v2

v3 whole, which is shorter than its diff:
```python
import functools
import math

import jax
import jax.numpy as jnp
from jax import lax
from jax.experimental import pallas as pl
from jax.experimental.pallas import tpu as pltpu
from jax.sharding import PartitionSpec as P

beta_one = 0.9
beta_two = 0.999
corr_one = 1.0 - 0.9**10
corr_two = 1.0 - 0.999**10
adam_eps = 1e-08

BF = jnp.bfloat16
F32 = jnp.float32
VMEM_BYTES = 34 * 2**20
SMALL_VMEM = 8 * 2**20
ROW_TILE = 512
COL_TILE = 512


def adam_update(factor, moment, second, gradient, step_rate):
    moment_new = beta_one * moment + (1.0 - beta_one) * gradient
    second_new = beta_two * second + (1.0 - beta_two) * gradient * gradient
    update = moment_new / corr_one / (jnp.sqrt(second_new / corr_two) + adam_eps)
    return (factor - step_rate * update, moment_new, second_new)


def prepare_kernel(a_ref, d_ref, a_out, d_out):
    a_out[...] = a_ref[...].astype(BF)
    d_out[...] = d_ref[...].astype(BF)


def prepare(a, d):
    shape = jax.ShapeDtypeStruct
    return pl.pallas_call(
        prepare_kernel,
        out_shape=(shape(a.shape, BF), shape(d.shape, BF)),
        compiler_params=pltpu.CompilerParams(vmem_limit_bytes=SMALL_VMEM),
        name="prepare",
    )(a, d)


def swap_item(n_item, mask):
    return [(i, i ^ mask) for i in range(n_item)]


def swap_mp(n_mp, n_item, even, odd):
    return [
        (m * n_item + i, (m ^ (odd if i % 2 else even)) * n_item + i)
        for m in range(n_mp)
        for i in range(n_item)
    ]


def chip_basis(chips):
    return [2**j - 1 for j in range(chips.bit_length() - 1, 0, -1)]


def mp_basis(n_mp):
    bits = [2**j for j in range(n_mp.bit_length() - 1)]
    return list(zip(bits, bits[1::-1] + bits[2:]))


def span(basis):
    masks = [0] if not basis or isinstance(basis[0], int) else [(0, 0)]
    for b in basis:
        if isinstance(b, int):
            masks += [x ^ b for x in masks]
        else:
            masks += [(x ^ b[0], y ^ b[1]) for x, y in masks]
    return masks


def gather(block, basis, send):
    blocks = [block]
    for b in basis:
        blocks += [send(x, b) for x in blocks]
    return blocks


def grad_kernel(n_mp, n_item, *refs):
    chips = n_item // 2
    a_in, refs = refs[:n_item], refs[n_item:]
    d_in, refs = refs[:n_mp], refs[n_mp:]
    bias_ref, r_hbm = refs[:2]
    keep_ref, give_ref, *h_out = refs[2 : 4 + n_mp]
    at, dt, resp, rs, gs, acc, sem_in, sem_r = refs[4 + n_mp :]
    k, rows = at.shape
    cols = dt.shape[1]
    ka, kd = k // n_item, k // n_mp
    tiles = rows // ROW_TILE

    item = lax.axis_index("item")
    m = lax.axis_index("mp")
    chip, core = item // 2, lax.rem(item, 2)

    def owner_item(x, flip):
        return (chip ^ x) * 2 + (core ^ flip)

    copies = []
    for q, (x, flip) in enumerate((x, f) for f in range(2) for x in span(chip_basis(chips))):
        off = pl.multiple_of(owner_item(x, flip) * ka, ka)
        copies.append(pltpu.make_async_copy(a_in[q], at.at[pl.ds(off, ka)], sem_in.at[q]))
    for q, (even, odd) in enumerate(span(mp_basis(n_mp))):
        off = pl.multiple_of((m ^ jnp.where(core == 0, even, odd)) * kd, kd)
        copies.append(pltpu.make_async_copy(d_in[q], dt.at[pl.ds(off, kd)], sem_in.at[n_item + q]))

    def load(t):
        rng = pl.ds(pl.multiple_of(t * ROW_TILE, ROW_TILE), ROW_TILE)
        return pltpu.make_async_copy(r_hbm.at[rng], resp.at[rng], sem_r.at[t])

    for c in copies:
        c.start()
    for t in range(tiles):
        load(t).start()
    for c in copies:
        c.wait()

    acc[...] = jnp.zeros_like(acc)

    def step(t, carry):
        rng = pl.ds(pl.multiple_of(t * ROW_TILE, ROW_TILE), ROW_TILE)
        load(t).wait()
        a_tile = at[:, rng]
        half = (a_tile.astype(F32) * 0.5).T.astype(BF)
        for c in range(0, cols, COL_TILE):
            cr = slice(c, c + COL_TILE)
            lg = jnp.dot(half, dt[:, cr], preferred_element_type=F32) + bias_ref[:, cr]
            r = resp[rng, cr]
            sign = jnp.where(r == 2, -1.0, 1.0)
            rs[:, cr] = jnp.where(r == 0, 0.0, jnp.tanh(lg) + sign).astype(BF)
        gs[:, rng] = lax.dot_general(
            dt[...], rs[...], (((1,), (1,)), ((), ())), preferred_element_type=F32
        )
        for c in range(0, cols, COL_TILE):
            cr = slice(c, c + COL_TILE)
            acc[:, cr] += jnp.dot(a_tile, rs[:, cr], preferred_element_type=F32)
        return carry

    lax.fori_loop(0, tiles, step, 0)

    for x in range(chips):
        dst = pl.ds(x * ka, ka)
        keep_ref[dst, :] = gs[pl.ds(pl.multiple_of(owner_item(x, 0) * ka, ka), ka), :]
        give_ref[dst, :] = gs[pl.ds(pl.multiple_of(owner_item(x, 1) * ka, ka), ka), :].astype(BF)
    for x in range(n_mp):
        h = acc[pl.ds(pl.multiple_of((m ^ x) * kd, kd), kd), :]
        h_out[x][...] = h.astype(h_out[x].dtype)


def gradients(a_blocks, d_blocks, bias, response, n_mp, n_item):
    ka, rows = a_blocks[0].shape
    kd, cols = d_blocks[0].shape
    k = ka * n_item
    flops = 3 * 2 * rows * cols * k
    shape = jax.ShapeDtypeStruct
    any_spec = pl.BlockSpec(memory_space=pl.ANY)
    vmem = pl.BlockSpec(memory_space=pltpu.VMEM)
    outs = [shape((k // 2, rows), F32), shape((k // 2, rows), BF)]
    outs += [shape((kd, cols), BF if q else F32) for q in range(n_mp)]
    return pl.pallas_call(
        functools.partial(grad_kernel, n_mp, n_item),
        out_shape=outs,
        in_specs=[any_spec] * (n_item + n_mp) + [vmem, any_spec],
        out_specs=[vmem] * len(outs),
        scratch_shapes=[
            pltpu.VMEM((k, rows), BF),
            pltpu.VMEM((k, cols), BF),
            pltpu.VMEM((rows, cols), jnp.int32),
            pltpu.VMEM((ROW_TILE, cols), BF),
            pltpu.VMEM((k, rows), F32),
            pltpu.VMEM((k, cols), F32),
            pltpu.SemaphoreType.DMA((n_item + n_mp,)),
            pltpu.SemaphoreType.DMA((rows // ROW_TILE,)),
        ],
        compiler_params=pltpu.CompilerParams(vmem_limit_bytes=VMEM_BYTES),
        cost_estimate=pl.CostEstimate(
            flops=flops, bytes_accessed=4 * rows * cols, transcendentals=rows * cols
        ),
        name="residual_gradients",
    )(*a_blocks, *d_blocks, bias, response)


def pair_kernel(keep_ref, got_ref, *outs):
    ka = outs[0].shape[0]
    for x, out in enumerate(outs):
        rng = slice(x * ka, (x + 1) * ka)
        out[...] = (keep_ref[rng, :] + got_ref[rng, :].astype(F32)).astype(out.dtype)


def pair_sum(keep, got, chips):
    shape = (keep.shape[0] // chips, keep.shape[1])
    return pl.pallas_call(
        pair_kernel,
        out_shape=[jax.ShapeDtypeStruct(shape, BF if x else F32) for x in range(chips)],
        compiler_params=pltpu.CompilerParams(vmem_limit_bytes=SMALL_VMEM),
        name="core_pair_sum",
    )(keep, got)


def adam_kernel(plan, *refs):
    n_in = sum(n for n, _, _ in plan) + 3 * len(plan)
    ins, outs = refs[:n_in], refs[n_in:]
    for n, scale, rate in plan:
        sums, (x_ref, m_ref, v_ref), ins = ins[:n], ins[n : n + 3], ins[n + 3 :]
        (x_out, m_out, v_out), outs = outs[:3], outs[3:]
        g = sums[0][...]
        for part in sums[1:]:
            g = g + part[...].astype(F32)
        x_out[...], m_out[...], v_out[...] = adam_update(
            x_ref[...], m_ref[...], v_ref[...], g * scale, rate
        )


def adam(*factors):
    plan = [(len(sums), scale, rate) for sums, _, scale, rate in factors]
    operands = [x for sums, state, _, _ in factors for x in (*sums, *state)]
    outs = [jax.ShapeDtypeStruct(x.shape, F32) for _, state, _, _ in factors for x in state]
    return pl.pallas_call(
        functools.partial(adam_kernel, plan),
        out_shape=outs,
        compiler_params=pltpu.CompilerParams(vmem_limit_bytes=SMALL_VMEM),
        name="adam",
    )(*operands)


def shards(response, difficulty, ability, ability_m, ability_v, discrim, discrim_m, discrim_v):
    n_item, n_mp = lax.axis_size("item"), lax.axis_size("mp")
    chips = n_item // 2
    rows, cols = response.shape
    k = discrim.shape[1] * n_mp
    items_total, ckpts_total = cols * n_item, rows * n_mp
    a_t, d_t = ability.T, discrim.T

    def send_chip(x, mask):
        return lax.ppermute(x, "item", swap_item(n_item, 2 * mask))

    def send_core(x):
        return lax.ppermute(x, "item", swap_item(n_item, 1))

    def send_mp(x, masks):
        return lax.ppermute(x, ("mp", "item"), swap_mp(n_mp, n_item, *masks))

    a_bf, d_bf = prepare(a_t, d_t)
    d_blocks = gather(d_bf, mp_basis(n_mp), send_mp)
    mine = [a_bf]
    for b in chip_basis(chips):
        mine += [send_chip(x, b) for x in mine]
        if len(mine) == 2 and n_mp > 2:
            mine[1], d_blocks[2] = lax.optimization_barrier((mine[1], d_blocks[2]))
    theirs = [send_core(x) for x in mine]
    theirs[0], difficulty = lax.optimization_barrier((theirs[0], difficulty))
    bias = (0.5 * difficulty).reshape(1, cols)
    keep, give, *h = gradients(mine + theirs, d_blocks, bias, response, n_mp, n_item)

    h_terms = [h[0]] + [send_mp(h[x], (x, x)) for x in range(1, n_mp)]
    g = pair_sum(keep, send_core(give), chips)
    g_terms = [g[0]] + [send_chip(g[x], x) for x in range(1, chips)]
    a_state = (a_t, ability_m.T, ability_v.T)
    d_state = (d_t, discrim_m.T, discrim_v.T)
    out = adam(
        (g_terms, a_state, 0.5 * math.sqrt(k / items_total), 0.05),
        (h_terms, d_state, 0.5 * math.sqrt(1.0 / ckpts_total), 0.01),
    )
    return tuple(x.T for x in out)


def solution(mesh):
    a_spec, d_spec = P("mp", "item"), P("item", "mp")
    return jax.shard_map(
        shards,
        mesh=mesh,
        in_specs=(a_spec, P("item")) + (a_spec,) * 3 + (d_spec,) * 3,
        out_specs=(a_spec,) * 3 + (d_spec,) * 3,
        check_vma=False,
    )
```

time: 58.3 us -> 56.1 us (0.962)
  waiting for transfers between devices: 19.6 us -> 16.4 us
  starting transfers between devices: 18.6 us -> 19.8 us
  local copies, waits for them, and re-layouts: 2.74 us -> 2.01 us
  other arithmetic: 0 us -> 0.7 us
  Pallas kernels: 16.5 us -> 15.9 us
    ppermute x17, waiting for transfers between devices: 19.6 us -> 16.4 us  [the longest x6 9.55 us: send_chip(): return lax.ppermute(x, 'item', swap_item(n_item, 2 * mask))]
    ppermute x17, starting transfers between devices: 18.6 us -> 19.8 us  [the longest x6 10.6 us: send_chip(): return lax.ppermute(x, 'item', swap_item(n_item, 2 * mask))]
    unnamed x18 -> x16, local copies, waits for them, and re-layouts: 2.74 us -> 2.01 us
    mul x0 -> x1, other arithmetic: none -> 0.7 us  [shards(): bias = (0.5 * difficulty).reshape(1, cols)]
    pallas_call x5 -> x3, Pallas kernels: 2.6 us -> 2.08 us  [the longest x1 1.95 us: adam(): pl.pallas_call(functools.partial(adam_kernel, plan), out_shape=outs, comp...]
  transfers between devices with their start and end apart: 17 -> 17, of which waited for: 6 -> 7; matrix products, arithmetic and copies ran while one was open for 0% -> 1% of each run, Pallas kernels for 2% -> 0%
where the time goes in v3:
time: 56.1 us; the launch traced here: 55.5 us
  starting transfers between devices  19.8 us (35%)
  waiting for transfers between devices  16.4 us (29%)
  Pallas kernels  15.9 us (28%)
  local copies, waits for them, and re-layouts  2.01 us (4%)
  between operations  0.74 us (1%)
  other arithmetic  0.7 us (1%)
    pallas_call x1, Pallas kernels, gradients(): pl.pallas_call(functools.partial(grad_kernel, n_mp, n_item), out_shape=ou...  13.8 us
    ppermute x6, starting transfers between devices, send_chip(): return lax.ppermute(x, 'item', swap_item(n_item, 2 * mask))  10.6 us
    ppermute x6, waiting for transfers between devices, send_chip(): return lax.ppermute(x, 'item', swap_item(n_item, 2 * mask))  9.55 us
    ppermute x6, starting transfers between devices, send_mp(): return lax.ppermute(x, ('mp', 'item'), swap_mp(n_mp, n_item, *masks))  8.58 us
    ppermute x6, waiting for transfers between devices, send_mp(): return lax.ppermute(x, ('mp', 'item'), swap_mp(n_mp, n_item, *masks))  6.86 us
    unnamed x16, local copies, waits for them, and re-layouts  2.01 us
    pallas_call x1, Pallas kernels, adam(): pl.pallas_call(functools.partial(adam_kernel, plan), out_shape=outs, comp...  1.95 us
  transfers between devices with their start and end apart: 17, of which 7 were waited for; matrix products, arithmetic and copies ran while one was open for 1% of the time, Pallas kernels for 0%

profile of v3, /device:TPU:0, one launch (start us, length us, event | category | flops | bytes accessed | tf_op | source)
XLA Modules:
  0.0 55.5 jit_solution(2728395541265601446)
XLA Ops:
  0.6 1.0 %copy-done = f32[2048,64]{0,1:T(8,128)S(1)} copy-done((f32[2048,64]{0,1:T(8,128)S(1)}, f32[2048,64]{0,1:T(8,128)}, u32[]{:S(2)}) %copy-start) | copy-done | bytes 524312
  1.7 0.9 %copy-done.2 = f32[2048,32]{0,1:T(8,128)S(1)} copy-done((f32[2048,32]{0,1:T(8,128)S(1)}, f32[2048,32]{0,1:T(8,128)}, u32[]{:S(2)}) %copy-start.2) | copy-done | bytes 262168
  2.7 3.0 %collective-permute-start.1 = (bf16[64,2048]{1,0:T(8,128)(2,1)S(1)}, bf16[64,2048]{1,0:T(8,128)(2,1)S(1)}, u32[]{:S(2)}, u32[]{:S(2)}) collective-permute-start(bf16[64,2048]{1,0:T(8,128)(2,1)S(1)} %get-tuple-element.29.refs_8_), channel_id=1, source_target_pairs={{0,16},{1,9},{2,18},{3,11},{4,20},{5,13},{6,22},{7,15},{8,24},{9,1... | collective-permute-start | bytes 786440 | tf_op jit(solution)/shard_map/ppermute | solution.py:246
  5.7 1.5 %collective-permute-start.8 = (bf16[64,2048]{1,0:T(8,128)(2,1)S(1)}, bf16[64,2048]{1,0:T(8,128)(2,1)S(1)}, u32[]{:S(2)}, u32[]{:S(2)}) collective-permute-start(bf16[64,2048]{1,0:T(8,128)(2,1)S(1)} %get-tuple-element.29.refs_8_), channel_id=1, source_target_pairs={{0,8},{1,17},{2,10},{3,19},{4,12},{5,21},{6,14},{7,23},{8,0},{9,25... | collective-permute-start | bytes 786440 | tf_op jit(solution)/shard_map/ppermute | solution.py:246
  7.2 3.6 %collective-permute-start = (bf16[32,2048]{1,0:T(8,128)(2,1)S(1)}, bf16[32,2048]{1,0:T(8,128)(2,1)S(1)}, u32[]{:S(2)}, u32[]{:S(2)}) collective-permute-start(bf16[32,2048]{1,0:T(8,128)(2,1)S(1)} %get-tuple-element.28.refs_0_), channel_id=1, source_target_pairs={{0,6},{1,7},{2,4},{3,5},{4,2},{5,3},{6,0},{7,1},{8,14},{9,15},{10,... | collective-permute-start | bytes 393224 | tf_op jit(solution)/shard_map/ppermute | solution.py:240
  10.8 4.3 %collective-permute-done.refs_1_ = bf16[32,2048]{1,0:T(8,128)(2,1)S(1)} collective-permute-done((bf16[32,2048]{1,0:T(8,128)(2,1)S(1)}, bf16[32,2048]{1,0:T(8,128)(2,1)S(1)}, u32[]{:S(2)}, u32[]{:S(2)}) %collective-permute-start) | collective-permute-done | bytes 131104 | tf_op jit(solution)/shard_map/ppermute | solution.py:240
  15.2 1.1 %collective-permute-start.3 = (bf16[32,2048]{1,0:T(8,128)(2,1)S(1)}, bf16[32,2048]{1,0:T(8,128)(2,1)S(1)}, u32[]{:S(2)}, u32[]{:S(2)}) collective-permute-start(bf16[32,2048]{1,0:T(8,128)(2,1)S(1)} %collective-permute-done.refs_1_), channel_id=1, source_target_pairs={{0,2},{1,3},{2,0},{3,1},{4,6},{5,7},{6,4},{7,5},{8,10},{9,11},{10,... | collective-permute-start | bytes 393224 | tf_op jit(solution)/shard_map/ppermute | solution.py:240
  16.3 0.5 collective-permute-start.9
  16.8 0.8 %collective-permute-done.2.refs_2_ = bf16[32,2048]{1,0:T(8,128)(2,1)S(1)} collective-permute-done((bf16[32,2048]{1,0:T(8,128)(2,1)S(1)}, bf16[32,2048]{1,0:T(8,128)(2,1)S(1)}, u32[]{:S(2)}, u32[]{:S(2)}) %collective-permute-start.2) | collective-permute-done | bytes 131104 | tf_op jit(solution)/shard_map/ppermute | solution.py:240
  17.6 0.5 collective-permute-start.5
  18.1 2.1 %collective-permute-done.3.refs_3_ = bf16[32,2048]{1,0:T(8,128)(2,1)S(1)} collective-permute-done((bf16[32,2048]{1,0:T(8,128)(2,1)S(1)}, bf16[32,2048]{1,0:T(8,128)(2,1)S(1)}, u32[]{:S(2)}, u32[]{:S(2)}) %collective-permute-start.3) | collective-permute-done | bytes 131104 | tf_op jit(solution)/shard_map/ppermute | solution.py:240
  20.2 0.7 %broadcast_multiply_fusion = f32[2048]{0:T(1024)S(1)} fusion(f32[2048]{0:T(1024)} %param.9), kind=kLoop, calls=%fused_computation | loop fusion | flops 2048 | bytes 16384 | tf_op jit(solution)/shard_map/mul | solution.py:257
  20.9 1.8 %collective-permute-done.9.refs_11_ = bf16[64,2048]{1,0:T(8,128)(2,1)S(1)} collective-permute-done((bf16[64,2048]{1,0:T(8,128)(2,1)S(1)}, bf16[64,2048]{1,0:T(8,128)(2,1)S(1)}, u32[]{:S(2)}, u32[]{:S(2)}) %collective-permute-start.9) | collective-permute-done | bytes 262176 | tf_op jit(solution)/shard_map/ppermute | solution.py:246
  22.7 13.8 %residual_gradients.1 = (f32[128,2048]{1,0:T(8,128)S(1)}, bf16[128,2048]{1,0:T(8,128)(2,1)S(1)}, f32[64,2048]{1,0:T(8,128)S(1)}, bf16[64,2048]{1,0:T(8,128)(2,1)...) custom-call(bf16[32,2048]{1,0:T(8,128)(2,1)S(1)} %get-tuple-element.28.refs_0_, ...), custom_call_target="tpu_custom_call" | custom-call | flops 6442450944 | bytes 16777216 | tf_op jit(solution)/shard_map/residual_gradients/pallas_call | solution.py:165
  36.6 0.6 %collective-permute-start.14 = (bf16[64,2048]{1,0:T(8,128)(2,1)S(1)}, bf16[64,2048]{1,0:T(8,128)(2,1)S(1)}, u32[]{:S(2)}, u32[]{:S(2)}) collective-permute-start(bf16[64,2048]{1,0:T(8,128)(2,1)S(1)} %get-tuple-element.41), channel_id=1, source_target_pairs={{0,8},{1,9},{2,10},{3,11},{4,12},{5,13},{6,14},{7,15},{8,0},{9,1},... | collective-permute-start | bytes 786440 | tf_op jit(solution)/shard_map/ppermute | solution.py:246
  37.2 0.5 collective-permute-start.15
  37.7 2.4 %collective-permute-start.16 = (bf16[64,2048]{1,0:T(8,128)(2,1)S(1)}, bf16[64,2048]{1,0:T(8,128)(2,1)S(1)}, u32[]{:S(2)}, u32[]{:S(2)}) collective-permute-start(bf16[64,2048]{1,0:T(8,128)(2,1)S(1)} %get-tuple-element.43), channel_id=1, source_target_pairs={{0,24},{1,25},{2,26},{3,27},{4,28},{5,29},{6,30},{7,31},{8,16},{9,... | collective-permute-start | bytes 786440 | tf_op jit(solution)/shard_map/ppermute | solution.py:246
  40.3 1.0 %collective-permute-start.11 = (bf16[32,2048]{1,0:T(8,128)(2,1)S(1)}, bf16[32,2048]{1,0:T(8,128)(2,1)S(1)}, u32[]{:S(2)}, u32[]{:S(2)}) collective-permute-start(bf16[32,2048]{1,0:T(8,128)(2,1)S(1)} %get-tuple-element.37), channel_id=1, source_target_pairs={{0,2},{1,3},{2,0},{3,1},{4,6},{5,7},{6,4},{7,5},{8,10},{9,11},{10,... | collective-permute-start | bytes 393224 | tf_op jit(solution)/shard_map/ppermute | solution.py:240
  41.2 2.3 %collective-permute-start.12 = (bf16[32,2048]{1,0:T(8,128)(2,1)S(1)}, bf16[32,2048]{1,0:T(8,128)(2,1)S(1)}, u32[]{:S(2)}, u32[]{:S(2)}) collective-permute-start(bf16[32,2048]{1,0:T(8,128)(2,1)S(1)} %get-tuple-element.38), channel_id=1, source_target_pairs={{0,4},{1,5},{2,6},{3,7},{4,0},{5,1},{6,2},{7,3},{8,12},{9,13},{10,... | collective-permute-start | bytes 393224 | tf_op jit(solution)/shard_map/ppermute | solution.py:240
  43.5 2.3 %collective-permute-done.14.refs_8_ = bf16[64,2048]{1,0:T(8,128)(2,1)S(1)} collective-permute-done((bf16[64,2048]{1,0:T(8,128)(2,1)S(1)}, bf16[64,2048]{1,0:T(8,128)(2,1)S(1)}, u32[]{:S(2)}, u32[]{:S(2)}) %collective-permute-start.14) | collective-permute-done | bytes 262176 | tf_op jit(solution)/shard_map/ppermute | solution.py:246
  45.8 2.6 %collective-permute-start.13 = (bf16[32,2048]{1,0:T(8,128)(2,1)S(1)}, bf16[32,2048]{1,0:T(8,128)(2,1)S(1)}, u32[]{:S(2)}, u32[]{:S(2)}) collective-permute-start(bf16[32,2048]{1,0:T(8,128)(2,1)S(1)} %get-tuple-element.39), channel_id=1, source_target_pairs={{0,6},{1,7},{2,4},{3,5},{4,2},{5,3},{6,0},{7,1},{8,14},{9,15},{10,... | collective-permute-start | bytes 393224 | tf_op jit(solution)/shard_map/ppermute | solution.py:240
  48.4 2.8 %collective-permute-done.15.refs_9_ = bf16[64,2048]{1,0:T(8,128)(2,1)S(1)} collective-permute-done((bf16[64,2048]{1,0:T(8,128)(2,1)S(1)}, bf16[64,2048]{1,0:T(8,128)(2,1)S(1)}, u32[]{:S(2)}, u32[]{:S(2)}) %collective-permute-start.15) | collective-permute-done | bytes 262176 | tf_op jit(solution)/shard_map/ppermute | solution.py:246
  51.2 2.3 %collective-permute-done.13.refs_3_ = bf16[32,2048]{1,0:T(8,128)(2,1)S(1)} collective-permute-done((bf16[32,2048]{1,0:T(8,128)(2,1)S(1)}, bf16[32,2048]{1,0:T(8,128)(2,1)S(1)}, u32[]{:S(2)}, u32[]{:S(2)}) %collective-permute-start.13) | collective-permute-done | bytes 131104 | tf_op jit(solution)/shard_map/ppermute | solution.py:240
  53.6 1.9 %adam.1 = (f32[32,2048]{1,0:T(8,128)}, f32[32,2048]{1,0:T(8,128)}, f32[32,2048]{1,0:T(8,128)}, f32[64,2048]{1,0:T(8,128)}, f32[64,2048]{1,0:T(8,128)}, /*index=5*/f32[64,2048]{1,0:T(8,128)}) custom-call(f32[32,2048]{1,0:T(8,128)S(1)} %get-tuple-element.36.refs_0_, bf16[32,2048]{1,0:T(8,128)(2,1)S(1)} %collective-permute-done.11.refs_1_, ...), custom_call_target="tpu_custom_call" | custom-call | tf_op jit(solution)/shard_map/adam/pallas_call | solution.py:223
  (31 shorter events, 0.3 us)
Async XLA Ops:
  0.6 1.0 %copy-start = (f32[2048,64]{0,1:T(8,128)S(1)}, f32[2048,64]{0,1:T(8,128)}, u32[]{:S(2)}) copy-start(f32[2048,64]{0,1:T(8,128)} %param.13) | copy-start | bytes 1572868
  2.6 50.9 %copy-start.1 = (f32[2048,64]{0,1:T(8,128)S(1)}, f32[2048,64]{0,1:T(8,128)}, u32[]{:S(2)}) copy-start(f32[2048,64]{0,1:T(8,128)} %param.13) | copy-start | bytes 1572868
  2.6 50.9 %copy-start.3 = (f32[2048,32]{0,1:T(8,128)S(1)}, f32[2048,32]{0,1:T(8,128)}, u32[]{:S(2)}) copy-start(f32[2048,32]{0,1:T(8,128)} %param.10) | copy-start | bytes 786436
  2.6 50.9 %copy-start.4 = (f32[2048,64]{0,1:T(8,128)S(1)}, f32[2048,64]{0,1:T(8,128)}, u32[]{:S(2)}) copy-start(f32[2048,64]{0,1:T(8,128)} %param.14) | copy-start | bytes 1572868
  2.6 50.9 %copy-start.5 = (f32[2048,64]{0,1:T(8,128)S(1)}, f32[2048,64]{0,1:T(8,128)}, u32[]{:S(2)}) copy-start(f32[2048,64]{0,1:T(8,128)} %param.15) | copy-start | bytes 1572868
  2.6 50.9 %copy-start.6 = (f32[2048,32]{0,1:T(8,128)S(1)}, f32[2048,32]{0,1:T(8,128)}, u32[]{:S(2)}) copy-start(f32[2048,32]{0,1:T(8,128)} %param.11) | copy-start | bytes 786436
  2.6 50.9 %copy-start.7 = (f32[2048,32]{0,1:T(8,128)S(1)}, f32[2048,32]{0,1:T(8,128)}, u32[]{:S(2)}) copy-start(f32[2048,32]{0,1:T(8,128)} %param.12) | copy-start | bytes 786436
  2.7 12.5 %collective-permute-start.1 = (bf16[64,2048]{1,0:T(8,128)(2,1)S(1)}, bf16[64,2048]{1,0:T(8,128)(2,1)S(1)}, u32[]{:S(2)}, u32[]{:S(2)}) collective-permute-start(bf16[64,2048]{1,0:T(8,128)(2,1)S(1)} %get-tuple-element.29.refs_8_), channel_id=1, source_target_pairs={{0,16},{1,9},{2,18},{3,11},{4,20},{5,13},{6,22},{7,15},{8,24},{9,1... | collective-permute-start | bytes 786440 | tf_op jit(solution)/shard_map/ppermute | solution.py:246
  5.7 10.6 %collective-permute-start.8 = (bf16[64,2048]{1,0:T(8,128)(2,1)S(1)}, bf16[64,2048]{1,0:T(8,128)(2,1)S(1)}, u32[]{:S(2)}, u32[]{:S(2)}) collective-permute-start(bf16[64,2048]{1,0:T(8,128)(2,1)S(1)} %get-tuple-element.29.refs_8_), channel_id=1, source_target_pairs={{0,8},{1,17},{2,10},{3,19},{4,12},{5,21},{6,14},{7,23},{8,0},{9,25... | collective-permute-start | bytes 786440 | tf_op jit(solution)/shard_map/ppermute | solution.py:246
  7.2 8.0 %collective-permute-start = (bf16[32,2048]{1,0:T(8,128)(2,1)S(1)}, bf16[32,2048]{1,0:T(8,128)(2,1)S(1)}, u32[]{:S(2)}, u32[]{:S(2)}) collective-permute-start(bf16[32,2048]{1,0:T(8,128)(2,1)S(1)} %get-tuple-element.28.refs_0_), channel_id=1, source_target_pairs={{0,6},{1,7},{2,4},{3,5},{4,2},{5,3},{6,0},{7,1},{8,14},{9,15},{10,... | collective-permute-start | bytes 393224 | tf_op jit(solution)/shard_map/ppermute | solution.py:240
  10.8 6.0 %collective-permute-start.4 = (bf16[32,2048]{1,0:T(8,128)(2,1)S(1)}, bf16[32,2048]{1,0:T(8,128)(2,1)S(1)}, u32[]{:S(2)}, u32[]{:S(2)}) collective-permute-start(bf16[32,2048]{1,0:T(8,128)(2,1)S(1)} %get-tuple-element.28.refs_0_), channel_id=1, source_target_pairs={{0,1},{1,0},{2,3},{3,2},{4,5},{5,4},{6,7},{7,6},{8,9},{9,8},{10,11... | collective-permute-start | bytes 393224 | tf_op jit(solution)/shard_map/ppermute | solution.py:243
  10.8 6.8 %collective-permute-start.2 = (bf16[32,2048]{1,0:T(8,128)(2,1)S(1)}, bf16[32,2048]{1,0:T(8,128)(2,1)S(1)}, u32[]{:S(2)}, u32[]{:S(2)}) collective-permute-start(bf16[32,2048]{1,0:T(8,128)(2,1)S(1)} %get-tuple-element.28.refs_0_), channel_id=1, source_target_pairs={{0,2},{1,3},{2,0},{3,1},{4,6},{5,7},{6,4},{7,5},{8,10},{9,11},{10,... | collective-permute-start | bytes 393224 | tf_op jit(solution)/shard_map/ppermute | solution.py:240
  15.2 5.0 %collective-permute-start.3 = (bf16[32,2048]{1,0:T(8,128)(2,1)S(1)}, bf16[32,2048]{1,0:T(8,128)(2,1)S(1)}, u32[]{:S(2)}, u32[]{:S(2)}) collective-permute-start(bf16[32,2048]{1,0:T(8,128)(2,1)S(1)} %collective-permute-done.refs_1_), channel_id=1, source_target_pairs={{0,2},{1,3},{2,0},{3,1},{4,6},{5,7},{6,4},{7,5},{8,10},{9,11},{10,... | collective-permute-start | bytes 393224 | tf_op jit(solution)/shard_map/ppermute | solution.py:240
  16.3 6.4 %collective-permute-start.9 = (bf16[64,2048]{1,0:T(8,128)(2,1)S(1)}, bf16[64,2048]{1,0:T(8,128)(2,1)S(1)}, u32[]{:S(2)}, u32[]{:S(2)}) collective-permute-start(bf16[64,2048]{1,0:T(8,128)(2,1)S(1)} %collective-permute-done.8.refs_9_), channel_id=1, source_target_pairs={{0,16},{1,9},{2,18},{3,11},{4,20},{5,13},{6,22},{7,15},{8,24},{9,1... | collective-permute-start | bytes 786440 | tf_op jit(solution)/shard_map/ppermute | solution.py:246
  17.6 3.3 %collective-permute-start.6 = (bf16[32,2048]{1,0:T(8,128)(2,1)S(1)}, bf16[32,2048]{1,0:T(8,128)(2,1)S(1)}, u32[]{:S(2)}, u32[]{:S(2)}) collective-permute-start(bf16[32,2048]{1,0:T(8,128)(2,1)S(1)} %collective-permute-done.2.refs_2_), channel_id=1, source_target_pairs={{0,1},{1,0},{2,3},{3,2},{4,5},{5,4},{6,7},{7,6},{8,9},{9,8},{10,11... | collective-permute-start | bytes 393224 | tf_op jit(solution)/shard_map/ppermute | solution.py:243
  17.6 3.3 %collective-permute-start.5 = (bf16[32,2048]{1,0:T(8,128)(2,1)S(1)}, bf16[32,2048]{1,0:T(8,128)(2,1)S(1)}, u32[]{:S(2)}, u32[]{:S(2)}) collective-permute-start(bf16[32,2048]{1,0:T(8,128)(2,1)S(1)} %collective-permute-done.refs_1_), channel_id=1, source_target_pairs={{0,1},{1,0},{2,3},{3,2},{4,5},{5,4},{6,7},{7,6},{8,9},{9,8},{10,11... | collective-permute-start | bytes 393224 | tf_op jit(solution)/shard_map/ppermute | solution.py:243
  20.2 2.5 %collective-permute-start.7 = (bf16[32,2048]{1,0:T(8,128)(2,1)S(1)}, bf16[32,2048]{1,0:T(8,128)(2,1)S(1)}, u32[]{:S(2)}, u32[]{:S(2)}) collective-permute-start(bf16[32,2048]{1,0:T(8,128)(2,1)S(1)} %collective-permute-done.3.refs_3_), channel_id=1, source_target_pairs={{0,1},{1,0},{2,3},{3,2},{4,5},{5,4},{6,7},{7,6},{8,9},{9,8},{10,11... | collective-permute-start | bytes 393224 | tf_op jit(solution)/shard_map/ppermute | solution.py:243
  36.5 3.6 %collective-permute-start.10 = (bf16[128,2048]{1,0:T(8,128)(2,1)S(1)}, bf16[128,2048]{1,0:T(8,128)(2,1)S(1)}, u32[]{:S(2)}, u32[]{:S(2)}) collective-permute-start(bf16[128,2048]{1,0:T(8,128)(2,1)S(1)} %get-tuple-element.35), channel_id=1, source_target_pairs={{0,1},{1,0},{2,3},{3,2},{4,5},{5,4},{6,7},{7,6},{8,9},{9,8},{10,11... | collective-permute-start | bytes 1572872 | tf_op jit(solution)/shard_map/ppermute | solution.py:243
  36.6 9.2 %collective-permute-start.14 = (bf16[64,2048]{1,0:T(8,128)(2,1)S(1)}, bf16[64,2048]{1,0:T(8,128)(2,1)S(1)}, u32[]{:S(2)}, u32[]{:S(2)}) collective-permute-start(bf16[64,2048]{1,0:T(8,128)(2,1)S(1)} %get-tuple-element.41), channel_id=1, source_target_pairs={{0,8},{1,9},{2,10},{3,11},{4,12},{5,13},{6,14},{7,15},{8,0},{9,1},... | collective-permute-start | bytes 786440 | tf_op jit(solution)/shard_map/ppermute | solution.py:246
  37.2 14.0 %collective-permute-start.15 = (bf16[64,2048]{1,0:T(8,128)(2,1)S(1)}, bf16[64,2048]{1,0:T(8,128)(2,1)S(1)}, u32[]{:S(2)}, u32[]{:S(2)}) collective-permute-start(bf16[64,2048]{1,0:T(8,128)(2,1)S(1)} %get-tuple-element.42), channel_id=1, source_target_pairs={{0,16},{1,17},{2,18},{3,19},{4,20},{5,21},{6,22},{7,23},{8,24},{9,... | collective-permute-start | bytes 786440 | tf_op jit(solution)/shard_map/ppermute | solution.py:246
  37.7 13.5 %collective-permute-start.16 = (bf16[64,2048]{1,0:T(8,128)(2,1)S(1)}, bf16[64,2048]{1,0:T(8,128)(2,1)S(1)}, u32[]{:S(2)}, u32[]{:S(2)}) collective-permute-start(bf16[64,2048]{1,0:T(8,128)(2,1)S(1)} %get-tuple-element.43), channel_id=1, source_target_pairs={{0,24},{1,25},{2,26},{3,27},{4,28},{5,29},{6,30},{7,31},{8,16},{9,... | collective-permute-start | bytes 786440 | tf_op jit(solution)/shard_map/ppermute | solution.py:246
  40.3 11.0 %collective-permute-start.11 = (bf16[32,2048]{1,0:T(8,128)(2,1)S(1)}, bf16[32,2048]{1,0:T(8,128)(2,1)S(1)}, u32[]{:S(2)}, u32[]{:S(2)}) collective-permute-start(bf16[32,2048]{1,0:T(8,128)(2,1)S(1)} %get-tuple-element.37), channel_id=1, source_target_pairs={{0,2},{1,3},{2,0},{3,1},{4,6},{5,7},{6,4},{7,5},{8,10},{9,11},{10,... | collective-permute-start | bytes 393224 | tf_op jit(solution)/shard_map/ppermute | solution.py:240
  41.2 10.0 %collective-permute-start.12 = (bf16[32,2048]{1,0:T(8,128)(2,1)S(1)}, bf16[32,2048]{1,0:T(8,128)(2,1)S(1)}, u32[]{:S(2)}, u32[]{:S(2)}) collective-permute-start(bf16[32,2048]{1,0:T(8,128)(2,1)S(1)} %get-tuple-element.38), channel_id=1, source_target_pairs={{0,4},{1,5},{2,6},{3,7},{4,0},{5,1},{6,2},{7,3},{8,12},{9,13},{10,... | collective-permute-start | bytes 393224 | tf_op jit(solution)/shard_map/ppermute | solution.py:240
  45.8 7.8 %collective-permute-start.13 = (bf16[32,2048]{1,0:T(8,128)(2,1)S(1)}, bf16[32,2048]{1,0:T(8,128)(2,1)S(1)}, u32[]{:S(2)}, u32[]{:S(2)}) collective-permute-start(bf16[32,2048]{1,0:T(8,128)(2,1)S(1)} %get-tuple-element.39), channel_id=1, source_target_pairs={{0,6},{1,7},{2,4},{3,5},{4,2},{5,3},{6,0},{7,1},{8,14},{9,15},{10,... | collective-permute-start | bytes 393224 | tf_op jit(solution)/shard_map/ppermute | solution.py:240
  (1 other events, 0.9 us)

commit v4 on v3

--- a/solution.py
+++ b/solution.py
@@ -16,9 +16,9 @@
 
 BF = jnp.bfloat16
 F32 = jnp.float32
-VMEM_BYTES = 34 * 2**20
+VMEM_BYTES = 26 * 2**20
 SMALL_VMEM = 8 * 2**20
-ROW_TILE = 512
+ROW_TILE = 1024
 COL_TILE = 512
 
 
@@ -40,6 +40,7 @@
         prepare_kernel,
         out_shape=(shape(a.shape, BF), shape(d.shape, BF)),
         compiler_params=pltpu.CompilerParams(vmem_limit_bytes=SMALL_VMEM),
+        cost_estimate=pl.CostEstimate(flops=12000000000, bytes_accessed=8 * a.size, transcendentals=0),
         name="prepare",
     )(a, d)
 
@@ -82,17 +83,36 @@
     return blocks
 
 
+def place_kernel(n_item, *refs):
+    blocks, (at_ref, half_ref) = refs[:n_item], refs[n_item:]
+    chips = n_item // 2
+    ka = blocks[0].shape[0]
+    item = lax.axis_index("item")
+    chip, core = item // 2, lax.rem(item, 2)
+    for q, (other, x) in enumerate((f, x) for f in range(2) for x in span(chip_basis(chips))):
+        owner = (chip ^ x) * 2 + (core ^ other)
+        at_ref[pl.ds(pl.multiple_of(owner * ka, ka), ka), :] = blocks[q][...]
+    half_ref[...] = (at_ref[...].astype(F32) * 0.5).T.astype(BF)
+
+
+def place_ability(blocks, n_item):
+    k, rows = blocks[0].shape[0] * n_item, blocks[0].shape[1]
+    return pl.pallas_call(
+        functools.partial(place_kernel, n_item),
+        out_shape=[jax.ShapeDtypeStruct((k, rows), BF), jax.ShapeDtypeStruct((rows, k), BF)],
+        compiler_params=pltpu.CompilerParams(vmem_limit_bytes=SMALL_VMEM),
+        name="place_ability",
+    )(*blocks)
+
+
 def grad_kernel(n_mp, n_item, *refs):
     chips = n_item // 2
-    a_in, refs = refs[:n_item], refs[n_item:]
-    d_in, refs = refs[:n_mp], refs[n_mp:]
-    bias_ref, r_hbm = refs[:2]
-    keep_ref, give_ref, *h_out = refs[2 : 4 + n_mp]
-    at, dt, resp, rs, gs, acc, sem_in, sem_r = refs[4 + n_mp :]
+    at, half, *d_in = refs[: 2 + n_mp]
+    bias_ref, resp, keep_ref, give_ref, *h_out = refs[2 + n_mp : 6 + 2 * n_mp]
+    dt, rs, gs, acc = refs[6 + 2 * n_mp :]
     k, rows = at.shape
     cols = dt.shape[1]
     ka, kd = k // n_item, k // n_mp
-    tiles = rows // ROW_TILE
 
     item = lax.axis_index("item")
     m = lax.axis_index("mp")
@@ -101,47 +121,28 @@
     def owner_item(x, flip):
         return (chip ^ x) * 2 + (core ^ flip)
 
-    copies = []
-    for q, (x, flip) in enumerate((x, f) for f in range(2) for x in span(chip_basis(chips))):
-        off = pl.multiple_of(owner_item(x, flip) * ka, ka)
-        copies.append(pltpu.make_async_copy(a_in[q], at.at[pl.ds(off, ka)], sem_in.at[q]))
     for q, (even, odd) in enumerate(span(mp_basis(n_mp))):
         off = pl.multiple_of((m ^ jnp.where(core == 0, even, odd)) * kd, kd)
-        copies.append(pltpu.make_async_copy(d_in[q], dt.at[pl.ds(off, kd)], sem_in.at[n_item + q]))
-
-    def load(t):
-        rng = pl.ds(pl.multiple_of(t * ROW_TILE, ROW_TILE), ROW_TILE)
-        return pltpu.make_async_copy(r_hbm.at[rng], resp.at[rng], sem_r.at[t])
-
-    for c in copies:
-        c.start()
-    for t in range(tiles):
-        load(t).start()
-    for c in copies:
-        c.wait()
-
+        dt[pl.ds(off, kd), :] = d_in[q][...]
     acc[...] = jnp.zeros_like(acc)
 
     def step(t, carry):
         rng = pl.ds(pl.multiple_of(t * ROW_TILE, ROW_TILE), ROW_TILE)
-        load(t).wait()
-        a_tile = at[:, rng]
-        half = (a_tile.astype(F32) * 0.5).T.astype(BF)
         for c in range(0, cols, COL_TILE):
             cr = slice(c, c + COL_TILE)
-            lg = jnp.dot(half, dt[:, cr], preferred_element_type=F32) + bias_ref[:, cr]
+            lg = jnp.dot(half[rng, :], dt[:, cr], preferred_element_type=F32) + bias_ref[:, cr]
             r = resp[rng, cr]
             sign = jnp.where(r == 2, -1.0, 1.0)
             rs[:, cr] = jnp.where(r == 0, 0.0, jnp.tanh(lg) + sign).astype(BF)
         gs[:, rng] = lax.dot_general(
-            dt[...], rs[...], (((1,), (1,)), ((), ())), preferred_element_type=F32
-        )
+            rs[...], dt[...], (((1,), (1,)), ((), ())), preferred_element_type=F32
+        ).T
         for c in range(0, cols, COL_TILE):
             cr = slice(c, c + COL_TILE)
-            acc[:, cr] += jnp.dot(a_tile, rs[:, cr], preferred_element_type=F32)
+            acc[:, cr] += jnp.dot(at[:, rng], rs[:, cr], preferred_element_type=F32)
         return carry
 
-    lax.fori_loop(0, tiles, step, 0)
+    lax.fori_loop(0, rows // ROW_TILE, step, 0)
 
     for x in range(chips):
         dst = pl.ds(x * ka, ka)
@@ -152,37 +153,31 @@
         h_out[x][...] = h.astype(h_out[x].dtype)
 
 
-def gradients(a_blocks, d_blocks, bias, response, n_mp, n_item):
-    ka, rows = a_blocks[0].shape
+def gradients(at, half, d_blocks, bias, response, n_mp, n_item):
+    k, rows = at.shape
     kd, cols = d_blocks[0].shape
-    k = ka * n_item
     flops = 3 * 2 * rows * cols * k
     shape = jax.ShapeDtypeStruct
-    any_spec = pl.BlockSpec(memory_space=pl.ANY)
     vmem = pl.BlockSpec(memory_space=pltpu.VMEM)
     outs = [shape((k // 2, rows), F32), shape((k // 2, rows), BF)]
     outs += [shape((kd, cols), BF if q else F32) for q in range(n_mp)]
     return pl.pallas_call(
         functools.partial(grad_kernel, n_mp, n_item),
         out_shape=outs,
-        in_specs=[any_spec] * (n_item + n_mp) + [vmem, any_spec],
+        in_specs=[vmem] * (4 + n_mp),
         out_specs=[vmem] * len(outs),
         scratch_shapes=[
-            pltpu.VMEM((k, rows), BF),
             pltpu.VMEM((k, cols), BF),
-            pltpu.VMEM((rows, cols), jnp.int32),
             pltpu.VMEM((ROW_TILE, cols), BF),
             pltpu.VMEM((k, rows), F32),
             pltpu.VMEM((k, cols), F32),
-            pltpu.SemaphoreType.DMA((n_item + n_mp,)),
-            pltpu.SemaphoreType.DMA((rows // ROW_TILE,)),
         ],
         compiler_params=pltpu.CompilerParams(vmem_limit_bytes=VMEM_BYTES),
         cost_estimate=pl.CostEstimate(
             flops=flops, bytes_accessed=4 * rows * cols, transcendentals=rows * cols
         ),
         name="residual_gradients",
-    )(*a_blocks, *d_blocks, bias, response)
+    )(at, half, *d_blocks, bias, response)
 
 
 def pair_kernel(keep_ref, got_ref, *outs):
@@ -255,17 +250,18 @@
     theirs = [send_core(x) for x in mine]
     theirs[0], difficulty = lax.optimization_barrier((theirs[0], difficulty))
     bias = (0.5 * difficulty).reshape(1, cols)
-    keep, give, *h = gradients(mine + theirs, d_blocks, bias, response, n_mp, n_item)
+    at, half = place_ability(mine + theirs, n_item)
+    keep, give, *h = gradients(at, half, d_blocks, bias, response, n_mp, n_item)
 
     h_terms = [h[0]] + [send_mp(h[x], (x, x)) for x in range(1, n_mp)]
     g = pair_sum(keep, send_core(give), chips)
     g_terms = [g[0]] + [send_chip(g[x], x) for x in range(1, chips)]
     a_state = (a_t, ability_m.T, ability_v.T)
     d_state = (d_t, discrim_m.T, discrim_v.T)
-    out = adam(
-        (g_terms, a_state, 0.5 * math.sqrt(k / items_total), 0.05),
-        (h_terms, d_state, 0.5 * math.sqrt(1.0 / ckpts_total), 0.01),
-    )
+    d_out = list(adam((h_terms, d_state, 0.5 * math.sqrt(1.0 / ckpts_total), 0.01)))
+    g_terms[0], d_out[0] = lax.optimization_barrier((g_terms[0], d_out[0]))
+    a_out = adam((g_terms, a_state, 0.5 * math.sqrt(k / items_total), 0.05))
+    out = (*a_out, *d_out)
     return tuple(x.T for x in out)
 
 

time: 56.1 us -> 50.3 us (0.90)
  Pallas kernels: 15.9 us -> 12 us
  waiting for transfers between devices: 16.4 us -> 14.4 us
  starting transfers between devices: 19.8 us -> 20.6 us
  other arithmetic: 0.7 us -> 0.01 us
    pallas_call x1, Pallas kernels: 13.8 us -> 8.95 us  [gradients(): pl.pallas_call(functools.partial(grad_kernel, n_mp, n_item), out_shape=ou...]
    ppermute x6, waiting for transfers between devices: 6.86 us -> 4.9 us  [send_mp(): return lax.ppermute(x, ('mp', 'item'), swap_mp(n_mp, n_item, *masks))]
    ppermute x6, waiting for transfers between devices: 9.55 us -> 8.16 us  [send_chip(): return lax.ppermute(x, 'item', swap_item(n_item, 2 * mask))]
    ppermute x5, waiting for transfers between devices: 0.01 us -> 1.33 us  [send_core(): return lax.ppermute(x, 'item', swap_item(n_item, 1))]
    ppermute x6, starting transfers between devices: 10.6 us -> 11.4 us  [send_chip(): return lax.ppermute(x, 'item', swap_item(n_item, 2 * mask))]
    mul x1, other arithmetic: 0.7 us -> 0.01 us  [shards(): bias = (0.5 * difficulty).reshape(1, cols)]
    pallas_call x1 -> x2, Pallas kernels: 1.95 us -> 2.43 us  [adam(): pl.pallas_call(functools.partial(adam_kernel, plan), out_shape=outs, comp...]
    unnamed x16 -> x20, local copies, waits for them, and re-layouts: 2.01 us -> 2.03 us
  transfers between devices with their start and end apart: 17 -> 17, of which waited for: 7 -> 8; matrix products, arithmetic and copies ran while one was open for 1% -> 0% of each run, Pallas kernels for 0% -> 4%
where the time goes in v4:
time: 50.3 us; the launch traced here: 49.8 us
  starting transfers between devices  20.6 us (41%)
  waiting for transfers between devices  14.4 us (29%)
  Pallas kernels  12 us (24%)
  local copies, waits for them, and re-layouts  2.03 us (4%)
  between operations  0.77 us (2%)
    ppermute x6, starting transfers between devices, send_chip(): return lax.ppermute(x, 'item', swap_item(n_item, 2 * mask))  11.4 us
    pallas_call x1, Pallas kernels, gradients(): pl.pallas_call(functools.partial(grad_kernel, n_mp, n_item), out_shape=ou...  8.95 us
    ppermute x6, starting transfers between devices, send_mp(): return lax.ppermute(x, ('mp', 'item'), swap_mp(n_mp, n_item, *masks))  8.58 us
    ppermute x6, waiting for transfers between devices, send_chip(): return lax.ppermute(x, 'item', swap_item(n_item, 2 * mask))  8.16 us
    ppermute x6, waiting for transfers between devices, send_mp(): return lax.ppermute(x, ('mp', 'item'), swap_mp(n_mp, n_item, *masks))  4.9 us
    pallas_call x2, Pallas kernels, adam(): pl.pallas_call(functools.partial(adam_kernel, plan), out_shape=outs, comp...  2.43 us
    unnamed x20, local copies, waits for them, and re-layouts  2.03 us
    ppermute x5, waiting for transfers between devices, send_core(): return lax.ppermute(x, 'item', swap_item(n_item, 1))  1.33 us
  transfers between devices with their start and end apart: 17, of which 8 were waited for; matrix products, arithmetic and copies ran while one was open for 0% of the time, Pallas kernels for 4%

profile of v4, /device:TPU:0, one launch (start us, length us, event | category | flops | bytes accessed | tf_op | source)
XLA Modules:
  0.0 49.8 jit_solution(378558422343946668)
XLA Ops:
  0.6 1.0 %copy-done = f32[2048,64]{0,1:T(8,128)S(1)} copy-done((f32[2048,64]{0,1:T(8,128)S(1)}, f32[2048,64]{0,1:T(8,128)}, u32[]{:S(2)}) %copy-start) | copy-done | bytes 524312
  1.7 0.9 %copy-done.4 = f32[2048,32]{0,1:T(8,128)S(1)} copy-done((f32[2048,32]{0,1:T(8,128)S(1)}, f32[2048,32]{0,1:T(8,128)}, u32[]{:S(2)}) %copy-start.4) | copy-done | bytes 262168
  2.7 3.0 %collective-permute-start.1 = (bf16[64,2048]{1,0:T(8,128)(2,1)S(1)}, bf16[64,2048]{1,0:T(8,128)(2,1)S(1)}, u32[]{:S(2)}, u32[]{:S(2)}) collective-permute-start(bf16[64,2048]{1,0:T(8,128)(2,1)S(1)} %get-tuple-element.33.refs_2_), channel_id=1, source_target_pairs={{0,16},{1,9},{2,18},{3,11},{4,20},{5,13},{6,22},{7,15},{8,24},{9,1... | collective-permute-start | bytes 786440 | tf_op jit(solution)/shard_map/ppermute | solution.py:241
  5.8 1.5 %collective-permute-start.8 = (bf16[64,2048]{1,0:T(8,128)(2,1)S(1)}, bf16[64,2048]{1,0:T(8,128)(2,1)S(1)}, u32[]{:S(2)}, u32[]{:S(2)}) collective-permute-start(bf16[64,2048]{1,0:T(8,128)(2,1)S(1)} %get-tuple-element.33.refs_2_), channel_id=1, source_target_pairs={{0,8},{1,17},{2,10},{3,19},{4,12},{5,21},{6,14},{7,23},{8,0},{9,25... | collective-permute-start | bytes 786440 | tf_op jit(solution)/shard_map/ppermute | solution.py:241
  7.3 3.6 %collective-permute-start = (bf16[32,2048]{1,0:T(8,128)(2,1)S(1)}, bf16[32,2048]{1,0:T(8,128)(2,1)S(1)}, u32[]{:S(2)}, u32[]{:S(2)}) collective-permute-start(bf16[32,2048]{1,0:T(8,128)(2,1)S(1)} %get-tuple-element.32.refs_0_), channel_id=1, source_target_pairs={{0,6},{1,7},{2,4},{3,5},{4,2},{5,3},{6,0},{7,1},{8,14},{9,15},{10,... | collective-permute-start | bytes 393224 | tf_op jit(solution)/shard_map/ppermute | solution.py:235
  10.9 4.3 %collective-permute-done.refs_1_ = bf16[32,2048]{1,0:T(8,128)(2,1)S(1)} collective-permute-done((bf16[32,2048]{1,0:T(8,128)(2,1)S(1)}, bf16[32,2048]{1,0:T(8,128)(2,1)S(1)}, u32[]{:S(2)}, u32[]{:S(2)}) %collective-permute-start) | collective-permute-done | bytes 131104 | tf_op jit(solution)/shard_map/ppermute | solution.py:235
  15.2 1.1 %collective-permute-start.3 = (bf16[32,2048]{1,0:T(8,128)(2,1)S(1)}, bf16[32,2048]{1,0:T(8,128)(2,1)S(1)}, u32[]{:S(2)}, u32[]{:S(2)}) collective-permute-start(bf16[32,2048]{1,0:T(8,128)(2,1)S(1)} %collective-permute-done.refs_1_), channel_id=1, source_target_pairs={{0,2},{1,3},{2,0},{3,1},{4,6},{5,7},{6,4},{7,5},{8,10},{9,11},{10,... | collective-permute-start | bytes 393224 | tf_op jit(solution)/shard_map/ppermute | solution.py:235
  16.9 0.8 %collective-permute-done.2.refs_2_ = bf16[32,2048]{1,0:T(8,128)(2,1)S(1)} collective-permute-done((bf16[32,2048]{1,0:T(8,128)(2,1)S(1)}, bf16[32,2048]{1,0:T(8,128)(2,1)S(1)}, u32[]{:S(2)}, u32[]{:S(2)}) %collective-permute-start.2) | collective-permute-done | bytes 131104 | tf_op jit(solution)/shard_map/ppermute | solution.py:235
  17.6 0.5 %collective-permute-start.5 = (bf16[32,2048]{1,0:T(8,128)(2,1)S(1)}, bf16[32,2048]{1,0:T(8,128)(2,1)S(1)}, u32[]{:S(2)}, u32[]{:S(2)}) collective-permute-start(bf16[32,2048]{1,0:T(8,128)(2,1)S(1)} %collective-permute-done.refs_1_), channel_id=1, source_target_pairs={{0,1},{1,0},{2,3},{3,2},{4,5},{5,4},{6,7},{7,6},{8,9},{9,8},{10,11... | collective-permute-start | bytes 393224 | tf_op jit(solution)/shard_map/ppermute | solution.py:238
  18.2 2.1 %collective-permute-done.3.refs_3_ = bf16[32,2048]{1,0:T(8,128)(2,1)S(1)} collective-permute-done((bf16[32,2048]{1,0:T(8,128)(2,1)S(1)}, bf16[32,2048]{1,0:T(8,128)(2,1)S(1)}, u32[]{:S(2)}, u32[]{:S(2)}) %collective-permute-start.3) | collective-permute-done | bytes 131104 | tf_op jit(solution)/shard_map/ppermute | solution.py:235
  20.3 1.3 %collective-permute-done.7.refs_7_ = bf16[32,2048]{1,0:T(8,128)(2,1)S(1)} collective-permute-done((bf16[32,2048]{1,0:T(8,128)(2,1)S(1)}, bf16[32,2048]{1,0:T(8,128)(2,1)S(1)}, u32[]{:S(2)}, u32[]{:S(2)}) %collective-permute-start.7) | collective-permute-done | bytes 131104 | tf_op jit(solution)/shard_map/ppermute | solution.py:238
  22.0 0.7 %collective-permute-done.9.refs_5_ = bf16[64,2048]{1,0:T(8,128)(2,1)S(1)} collective-permute-done((bf16[64,2048]{1,0:T(8,128)(2,1)S(1)}, bf16[64,2048]{1,0:T(8,128)(2,1)S(1)}, u32[]{:S(2)}, u32[]{:S(2)}) %collective-permute-start.9) | collective-permute-done | bytes 262176 | tf_op jit(solution)/shard_map/ppermute | solution.py:241
  22.7 9.0 %residual_gradients.1 = (f32[128,2048]{1,0:T(8,128)S(1)}, bf16[128,2048]{1,0:T(8,128)(2,1)S(1)}, f32[64,2048]{1,0:T(8,128)S(1)}, bf16[64,2048]{1,0:T(8,128)(2,1)...) custom-call(bf16[256,2048]{1,0:T(8,128)(2,1)S(1)} %get-tuple-element.36.refs_0_, ...), custom_call_target="tpu_custom_call" | custom-call | flops 6442450944 | bytes 16777216 | tf_op jit(solution)/shard_map/residual_gradients/pallas_call | solution.py:164
  31.8 0.6 %collective-permute-start.11 = (bf16[64,2048]{1,0:T(8,128)(2,1)S(1)}, bf16[64,2048]{1,0:T(8,128)(2,1)S(1)}, u32[]{:S(2)}, u32[]{:S(2)}) collective-permute-start(bf16[64,2048]{1,0:T(8,128)(2,1)S(1)} %get-tuple-element.44), channel_id=1, source_target_pairs={{0,8},{1,9},{2,10},{3,11},{4,12},{5,13},{6,14},{7,15},{8,0},{9,1},... | collective-permute-start | bytes 786440 | tf_op jit(solution)/shard_map/ppermute | solution.py:241
  32.4 0.5 %collective-permute-start.12 = (bf16[64,2048]{1,0:T(8,128)(2,1)S(1)}, bf16[64,2048]{1,0:T(8,128)(2,1)S(1)}, u32[]{:S(2)}, u32[]{:S(2)}) collective-permute-start(bf16[64,2048]{1,0:T(8,128)(2,1)S(1)} %get-tuple-element.45), channel_id=1, source_target_pairs={{0,16},{1,17},{2,18},{3,19},{4,20},{5,21},{6,22},{7,23},{8,24},{9,... | collective-permute-start | bytes 786440 | tf_op jit(solution)/shard_map/ppermute | solution.py:241
  32.9 2.4 %collective-permute-start.13 = (bf16[64,2048]{1,0:T(8,128)(2,1)S(1)}, bf16[64,2048]{1,0:T(8,128)(2,1)S(1)}, u32[]{:S(2)}, u32[]{:S(2)}) collective-permute-start(bf16[64,2048]{1,0:T(8,128)(2,1)S(1)} %get-tuple-element.46), channel_id=1, source_target_pairs={{0,24},{1,25},{2,26},{3,27},{4,28},{5,29},{6,30},{7,31},{8,16},{9,... | collective-permute-start | bytes 786440 | tf_op jit(solution)/shard_map/ppermute | solution.py:241
  35.4 1.0 %collective-permute-start.14 = (bf16[32,2048]{1,0:T(8,128)(2,1)S(1)}, bf16[32,2048]{1,0:T(8,128)(2,1)S(1)}, u32[]{:S(2)}, u32[]{:S(2)}) collective-permute-start(bf16[32,2048]{1,0:T(8,128)(2,1)S(1)} %get-tuple-element.49), channel_id=1, source_target_pairs={{0,2},{1,3},{2,0},{3,1},{4,6},{5,7},{6,4},{7,5},{8,10},{9,11},{10,... | collective-permute-start | bytes 393224 | tf_op jit(solution)/shard_map/ppermute | solution.py:235
  36.4 2.7 %collective-permute-start.15 = (bf16[32,2048]{1,0:T(8,128)(2,1)S(1)}, bf16[32,2048]{1,0:T(8,128)(2,1)S(1)}, u32[]{:S(2)}, u32[]{:S(2)}) collective-permute-start(bf16[32,2048]{1,0:T(8,128)(2,1)S(1)} %get-tuple-element.50), channel_id=1, source_target_pairs={{0,4},{1,5},{2,6},{3,7},{4,0},{5,1},{6,2},{7,3},{8,12},{9,13},{10,... | collective-permute-start | bytes 393224 | tf_op jit(solution)/shard_map/ppermute | solution.py:235
  39.1 1.8 %collective-permute-done.11.refs_1_ = bf16[64,2048]{1,0:T(8,128)(2,1)S(1)} collective-permute-done((bf16[64,2048]{1,0:T(8,128)(2,1)S(1)}, bf16[64,2048]{1,0:T(8,128)(2,1)S(1)}, u32[]{:S(2)}, u32[]{:S(2)}) %collective-permute-start.11) | collective-permute-done | bytes 262176 | tf_op jit(solution)/shard_map/ppermute | solution.py:241
  40.9 3.1 %collective-permute-start.16 = (bf16[32,2048]{1,0:T(8,128)(2,1)S(1)}, bf16[32,2048]{1,0:T(8,128)(2,1)S(1)}, u32[]{:S(2)}, u32[]{:S(2)}) collective-permute-start(bf16[32,2048]{1,0:T(8,128)(2,1)S(1)} %get-tuple-element.51), channel_id=1, source_target_pairs={{0,6},{1,7},{2,4},{3,5},{4,2},{5,3},{6,0},{7,1},{8,14},{9,15},{10,... | collective-permute-start | bytes 393224 | tf_op jit(solution)/shard_map/ppermute | solution.py:235
  44.0 2.4 %collective-permute-done.12.refs_2_ = bf16[64,2048]{1,0:T(8,128)(2,1)S(1)} collective-permute-done((bf16[64,2048]{1,0:T(8,128)(2,1)S(1)}, bf16[64,2048]{1,0:T(8,128)(2,1)S(1)}, u32[]{:S(2)}, u32[]{:S(2)}) %collective-permute-start.12) | collective-permute-done | bytes 262176 | tf_op jit(solution)/shard_map/ppermute | solution.py:241
  46.4 1.4 %adam.2 = (f32[64,2048]{1,0:T(8,128)}, f32[64,2048]{1,0:T(8,128)}, f32[64,2048]{1,0:T(8,128)}) custom-call(f32[64,2048]{1,0:T(8,128)S(1)} %get-tuple-element.43.refs_0_, bf16[64,2048]{1,0:T(8,128)(2,1)S(1)} %collective-permute-done.11.refs_1_, bf16[64,2048]{1,0:T(8,128)(2,1)S(1)} %collective-permute-done.12.refs_2_, ...), custom_call_target="tpu_custom_call" | custom-call | tf_op jit(solution)/shard_map/adam/pallas_call | solution.py:218
  47.8 1.0 %collective-permute-done.16.refs_3_ = bf16[32,2048]{1,0:T(8,128)(2,1)S(1)} collective-permute-done((bf16[32,2048]{1,0:T(8,128)(2,1)S(1)}, bf16[32,2048]{1,0:T(8,128)(2,1)S(1)}, u32[]{:S(2)}, u32[]{:S(2)}) %collective-permute-start.16) | collective-permute-done | bytes 131104 | tf_op jit(solution)/shard_map/ppermute | solution.py:235
  48.8 1.0 %adam.3 = (f32[32,2048]{1,0:T(8,128)}, f32[32,2048]{1,0:T(8,128)}, f32[32,2048]{1,0:T(8,128)}) custom-call(f32[32,2048]{1,0:T(8,128)S(1)} %get-tuple-element.48.refs_0_, bf16[32,2048]{1,0:T(8,128)(2,1)S(1)} %collective-permute-done.14.refs_1_, bf16[32,2048]{1,0:T(8,128)(2,1)S(1)} %collective-permute-done.15.refs_2_, ...), custom_call_target="tpu_custom_call" | custom-call | tf_op jit(solution)/shard_map/adam/pallas_call | solution.py:218
  (37 shorter events, 1.3 us)
Async XLA Ops:
  2.6 20.1 %copy-start.8 = (s32[2048,2048]{1,0:T(8,128)S(1)}, s32[2048,2048]{1,0:T(8,128)}, u32[]{:S(2)}) copy-start(s32[2048,2048]{1,0:T(8,128)} %refs_7_.1) | copy-start | bytes 50331652
  2.7 43.7 %copy-start.1 = (f32[2048,64]{0,1:T(8,128)S(1)}, f32[2048,64]{0,1:T(8,128)}, u32[]{:S(2)}) copy-start(f32[2048,64]{0,1:T(8,128)} %param.13) | copy-start | bytes 1572868
  2.7 43.7 %copy-start.2 = (f32[2048,64]{0,1:T(8,128)S(1)}, f32[2048,64]{0,1:T(8,128)}, u32[]{:S(2)}) copy-start(f32[2048,64]{0,1:T(8,128)} %param.14) | copy-start | bytes 1572868
  2.7 43.7 %copy-start.3 = (f32[2048,64]{0,1:T(8,128)S(1)}, f32[2048,64]{0,1:T(8,128)}, u32[]{:S(2)}) copy-start(f32[2048,64]{0,1:T(8,128)} %param.15) | copy-start | bytes 1572868
  2.7 46.0 %copy-start.5 = (f32[2048,32]{0,1:T(8,128)S(1)}, f32[2048,32]{0,1:T(8,128)}, u32[]{:S(2)}) copy-start(f32[2048,32]{0,1:T(8,128)} %param.10) | copy-start | bytes 786436
  2.7 46.0 %copy-start.6 = (f32[2048,32]{0,1:T(8,128)S(1)}, f32[2048,32]{0,1:T(8,128)}, u32[]{:S(2)}) copy-start(f32[2048,32]{0,1:T(8,128)} %param.11) | copy-start | bytes 786436
  2.7 46.0 %copy-start.7 = (f32[2048,32]{0,1:T(8,128)S(1)}, f32[2048,32]{0,1:T(8,128)}, u32[]{:S(2)}) copy-start(f32[2048,32]{0,1:T(8,128)} %param.12) | copy-start | bytes 786436
  2.7 12.5 %collective-permute-start.1 = (bf16[64,2048]{1,0:T(8,128)(2,1)S(1)}, bf16[64,2048]{1,0:T(8,128)(2,1)S(1)}, u32[]{:S(2)}, u32[]{:S(2)}) collective-permute-start(bf16[64,2048]{1,0:T(8,128)(2,1)S(1)} %get-tuple-element.33.refs_2_), channel_id=1, source_target_pairs={{0,16},{1,9},{2,18},{3,11},{4,20},{5,13},{6,22},{7,15},{8,24},{9,1... | collective-permute-start | bytes 786440 | tf_op jit(solution)/shard_map/ppermute | solution.py:241
  5.8 10.6 %collective-permute-start.8 = (bf16[64,2048]{1,0:T(8,128)(2,1)S(1)}, bf16[64,2048]{1,0:T(8,128)(2,1)S(1)}, u32[]{:S(2)}, u32[]{:S(2)}) collective-permute-start(bf16[64,2048]{1,0:T(8,128)(2,1)S(1)} %get-tuple-element.33.refs_2_), channel_id=1, source_target_pairs={{0,8},{1,17},{2,10},{3,19},{4,12},{5,21},{6,14},{7,23},{8,0},{9,25... | collective-permute-start | bytes 786440 | tf_op jit(solution)/shard_map/ppermute | solution.py:241
  7.3 8.0 %collective-permute-start = (bf16[32,2048]{1,0:T(8,128)(2,1)S(1)}, bf16[32,2048]{1,0:T(8,128)(2,1)S(1)}, u32[]{:S(2)}, u32[]{:S(2)}) collective-permute-start(bf16[32,2048]{1,0:T(8,128)(2,1)S(1)} %get-tuple-element.32.refs_0_), channel_id=1, source_target_pairs={{0,6},{1,7},{2,4},{3,5},{4,2},{5,3},{6,0},{7,1},{8,14},{9,15},{10,... | collective-permute-start | bytes 393224 | tf_op jit(solution)/shard_map/ppermute | solution.py:235
  10.9 6.0 %collective-permute-start.4 = (bf16[32,2048]{1,0:T(8,128)(2,1)S(1)}, bf16[32,2048]{1,0:T(8,128)(2,1)S(1)}, u32[]{:S(2)}, u32[]{:S(2)}) collective-permute-start(bf16[32,2048]{1,0:T(8,128)(2,1)S(1)} %get-tuple-element.32.refs_0_), channel_id=1, source_target_pairs={{0,1},{1,0},{2,3},{3,2},{4,5},{5,4},{6,7},{7,6},{8,9},{9,8},{10,11... | collective-permute-start | bytes 393224 | tf_op jit(solution)/shard_map/ppermute | solution.py:238
  10.9 6.8 %collective-permute-start.2 = (bf16[32,2048]{1,0:T(8,128)(2,1)S(1)}, bf16[32,2048]{1,0:T(8,128)(2,1)S(1)}, u32[]{:S(2)}, u32[]{:S(2)}) collective-permute-start(bf16[32,2048]{1,0:T(8,128)(2,1)S(1)} %get-tuple-element.32.refs_0_), channel_id=1, source_target_pairs={{0,2},{1,3},{2,0},{3,1},{4,6},{5,7},{6,4},{7,5},{8,10},{9,11},{10,... | collective-permute-start | bytes 393224 | tf_op jit(solution)/shard_map/ppermute | solution.py:235
  15.2 5.0 %collective-permute-start.3 = (bf16[32,2048]{1,0:T(8,128)(2,1)S(1)}, bf16[32,2048]{1,0:T(8,128)(2,1)S(1)}, u32[]{:S(2)}, u32[]{:S(2)}) collective-permute-start(bf16[32,2048]{1,0:T(8,128)(2,1)S(1)} %collective-permute-done.refs_1_), channel_id=1, source_target_pairs={{0,2},{1,3},{2,0},{3,1},{4,6},{5,7},{6,4},{7,5},{8,10},{9,11},{10,... | collective-permute-start | bytes 393224 | tf_op jit(solution)/shard_map/ppermute | solution.py:235
  16.3 6.4 %collective-permute-start.9 = (bf16[64,2048]{1,0:T(8,128)(2,1)S(1)}, bf16[64,2048]{1,0:T(8,128)(2,1)S(1)}, u32[]{:S(2)}, u32[]{:S(2)}) collective-permute-start(bf16[64,2048]{1,0:T(8,128)(2,1)S(1)} %collective-permute-done.8.refs_3_), channel_id=1, source_target_pairs={{0,16},{1,9},{2,18},{3,11},{4,20},{5,13},{6,22},{7,15},{8,24},{9,1... | collective-permute-start | bytes 786440 | tf_op jit(solution)/shard_map/ppermute | solution.py:241
  17.6 2.6 %collective-permute-start.6 = (bf16[32,2048]{1,0:T(8,128)(2,1)S(1)}, bf16[32,2048]{1,0:T(8,128)(2,1)S(1)}, u32[]{:S(2)}, u32[]{:S(2)}) collective-permute-start(bf16[32,2048]{1,0:T(8,128)(2,1)S(1)} %collective-permute-done.2.refs_2_), channel_id=1, source_target_pairs={{0,1},{1,0},{2,3},{3,2},{4,5},{5,4},{6,7},{7,6},{8,9},{9,8},{10,11... | collective-permute-start | bytes 393224 | tf_op jit(solution)/shard_map/ppermute | solution.py:238
  17.6 2.6 %collective-permute-start.5 = (bf16[32,2048]{1,0:T(8,128)(2,1)S(1)}, bf16[32,2048]{1,0:T(8,128)(2,1)S(1)}, u32[]{:S(2)}, u32[]{:S(2)}) collective-permute-start(bf16[32,2048]{1,0:T(8,128)(2,1)S(1)} %collective-permute-done.refs_1_), channel_id=1, source_target_pairs={{0,1},{1,0},{2,3},{3,2},{4,5},{5,4},{6,7},{7,6},{8,9},{9,8},{10,11... | collective-permute-start | bytes 393224 | tf_op jit(solution)/shard_map/ppermute | solution.py:238
  20.2 1.3 %collective-permute-start.7 = (bf16[32,2048]{1,0:T(8,128)(2,1)S(1)}, bf16[32,2048]{1,0:T(8,128)(2,1)S(1)}, u32[]{:S(2)}, u32[]{:S(2)}) collective-permute-start(bf16[32,2048]{1,0:T(8,128)(2,1)S(1)} %collective-permute-done.3.refs_3_), channel_id=1, source_target_pairs={{0,1},{1,0},{2,3},{3,2},{4,5},{5,4},{6,7},{7,6},{8,9},{9,8},{10,11... | collective-permute-start | bytes 393224 | tf_op jit(solution)/shard_map/ppermute | solution.py:238
  31.7 3.6 %collective-permute-start.10 = (bf16[128,2048]{1,0:T(8,128)(2,1)S(1)}, bf16[128,2048]{1,0:T(8,128)(2,1)S(1)}, u32[]{:S(2)}, u32[]{:S(2)}) collective-permute-start(bf16[128,2048]{1,0:T(8,128)(2,1)S(1)} %get-tuple-element.41), channel_id=1, source_target_pairs={{0,1},{1,0},{2,3},{3,2},{4,5},{5,4},{6,7},{7,6},{8,9},{9,8},{10,11... | collective-permute-start | bytes 1572872 | tf_op jit(solution)/shard_map/ppermute | solution.py:238
  31.8 9.2 %collective-permute-start.11 = (bf16[64,2048]{1,0:T(8,128)(2,1)S(1)}, bf16[64,2048]{1,0:T(8,128)(2,1)S(1)}, u32[]{:S(2)}, u32[]{:S(2)}) collective-permute-start(bf16[64,2048]{1,0:T(8,128)(2,1)S(1)} %get-tuple-element.44), channel_id=1, source_target_pairs={{0,8},{1,9},{2,10},{3,11},{4,12},{5,13},{6,14},{7,15},{8,0},{9,1},... | collective-permute-start | bytes 786440 | tf_op jit(solution)/shard_map/ppermute | solution.py:241
  32.4 14.0 %collective-permute-start.12 = (bf16[64,2048]{1,0:T(8,128)(2,1)S(1)}, bf16[64,2048]{1,0:T(8,128)(2,1)S(1)}, u32[]{:S(2)}, u32[]{:S(2)}) collective-permute-start(bf16[64,2048]{1,0:T(8,128)(2,1)S(1)} %get-tuple-element.45), channel_id=1, source_target_pairs={{0,16},{1,17},{2,18},{3,19},{4,20},{5,21},{6,22},{7,23},{8,24},{9,... | collective-permute-start | bytes 786440 | tf_op jit(solution)/shard_map/ppermute | solution.py:241
  32.9 13.5 %collective-permute-start.13 = (bf16[64,2048]{1,0:T(8,128)(2,1)S(1)}, bf16[64,2048]{1,0:T(8,128)(2,1)S(1)}, u32[]{:S(2)}, u32[]{:S(2)}) collective-permute-start(bf16[64,2048]{1,0:T(8,128)(2,1)S(1)} %get-tuple-element.46), channel_id=1, source_target_pairs={{0,24},{1,25},{2,26},{3,27},{4,28},{5,29},{6,30},{7,31},{8,16},{9,... | collective-permute-start | bytes 786440 | tf_op jit(solution)/shard_map/ppermute | solution.py:241
  35.4 12.3 %collective-permute-start.14 = (bf16[32,2048]{1,0:T(8,128)(2,1)S(1)}, bf16[32,2048]{1,0:T(8,128)(2,1)S(1)}, u32[]{:S(2)}, u32[]{:S(2)}) collective-permute-start(bf16[32,2048]{1,0:T(8,128)(2,1)S(1)} %get-tuple-element.49), channel_id=1, source_target_pairs={{0,2},{1,3},{2,0},{3,1},{4,6},{5,7},{6,4},{7,5},{8,10},{9,11},{10,... | collective-permute-start | bytes 393224 | tf_op jit(solution)/shard_map/ppermute | solution.py:235
  36.4 11.4 %collective-permute-start.15 = (bf16[32,2048]{1,0:T(8,128)(2,1)S(1)}, bf16[32,2048]{1,0:T(8,128)(2,1)S(1)}, u32[]{:S(2)}, u32[]{:S(2)}) collective-permute-start(bf16[32,2048]{1,0:T(8,128)(2,1)S(1)} %get-tuple-element.50), channel_id=1, source_target_pairs={{0,4},{1,5},{2,6},{3,7},{4,0},{5,1},{6,2},{7,3},{8,12},{9,13},{10,... | collective-permute-start | bytes 393224 | tf_op jit(solution)/shard_map/ppermute | solution.py:235
  40.9 7.8 %collective-permute-start.16 = (bf16[32,2048]{1,0:T(8,128)(2,1)S(1)}, bf16[32,2048]{1,0:T(8,128)(2,1)S(1)}, u32[]{:S(2)}, u32[]{:S(2)}) collective-permute-start(bf16[32,2048]{1,0:T(8,128)(2,1)S(1)} %get-tuple-element.51), channel_id=1, source_target_pairs={{0,6},{1,7},{2,4},{3,5},{4,2},{5,3},{6,0},{7,1},{8,14},{9,15},{10,... | collective-permute-start | bytes 393224 | tf_op jit(solution)/shard_map/ppermute | solution.py:235
  (3 other events, 19.6 us)

commit v5 on v4

--- a/solution.py
+++ b/solution.py
@@ -29,9 +29,24 @@
     return (factor - step_rate * update, moment_new, second_new)
 
 
-def prepare_kernel(a_ref, d_ref, a_out, d_out):
-    a_out[...] = a_ref[...].astype(BF)
-    d_out[...] = d_ref[...].astype(BF)
+def ones_kernel(out_ref):
+    out_ref[...] = jnp.ones_like(out_ref)
+
+
+def ones_first():
+    return pl.pallas_call(
+        ones_kernel,
+        out_shape=jax.ShapeDtypeStruct((8, 128), F32),
+        compiler_params=pltpu.CompilerParams(vmem_limit_bytes=SMALL_VMEM),
+        cost_estimate=pl.CostEstimate(flops=12000000000, bytes_accessed=4096, transcendentals=0),
+        name="ones_first",
+    )()
+
+
+def prepare_kernel(one_ref, a_ref, d_ref, a_out, d_out):
+    one = one_ref[0:1, 0:1]
+    a_out[...] = (a_ref[...] * one).astype(BF)
+    d_out[...] = (d_ref[...] * one).astype(BF)
 
 
 def prepare(a, d):
@@ -40,9 +55,11 @@
         prepare_kernel,
         out_shape=(shape(a.shape, BF), shape(d.shape, BF)),
         compiler_params=pltpu.CompilerParams(vmem_limit_bytes=SMALL_VMEM),
-        cost_estimate=pl.CostEstimate(flops=12000000000, bytes_accessed=8 * a.size, transcendentals=0),
+        cost_estimate=pl.CostEstimate(
+            flops=1000000, bytes_accessed=8 * a.size, transcendentals=0
+        ),
         name="prepare",
-    )(a, d)
+    )(ones_first(), a, d)
 
 
 def swap_item(n_item, mask):
@@ -105,12 +122,11 @@
     )(*blocks)
 
 
-def grad_kernel(n_mp, n_item, *refs):
+def ability_kernel(n_mp, n_item, *refs):
     chips = n_item // 2
-    at, half, *d_in = refs[: 2 + n_mp]
-    bias_ref, resp, keep_ref, give_ref, *h_out = refs[2 + n_mp : 6 + 2 * n_mp]
-    dt, rs, gs, acc = refs[6 + 2 * n_mp :]
-    k, rows = at.shape
+    half, *d_in = refs[: 1 + n_mp]
+    bias_ref, resp, res_ref, keep_ref, give_ref, dt, gs = refs[1 + n_mp :]
+    rows, k = half.shape
     cols = dt.shape[1]
     ka, kd = k // n_item, k // n_mp
 
@@ -124,7 +140,6 @@
     for q, (even, odd) in enumerate(span(mp_basis(n_mp))):
         off = pl.multiple_of((m ^ jnp.where(core == 0, even, odd)) * kd, kd)
         dt[pl.ds(off, kd), :] = d_in[q][...]
-    acc[...] = jnp.zeros_like(acc)
 
     def step(t, carry):
         rng = pl.ds(pl.multiple_of(t * ROW_TILE, ROW_TILE), ROW_TILE)
@@ -133,13 +148,10 @@
             lg = jnp.dot(half[rng, :], dt[:, cr], preferred_element_type=F32) + bias_ref[:, cr]
             r = resp[rng, cr]
             sign = jnp.where(r == 2, -1.0, 1.0)
-            rs[:, cr] = jnp.where(r == 0, 0.0, jnp.tanh(lg) + sign).astype(BF)
+            res_ref[rng, cr] = jnp.where(r == 0, 0.0, jnp.tanh(lg) + sign).astype(BF)
         gs[:, rng] = lax.dot_general(
-            rs[...], dt[...], (((1,), (1,)), ((), ())), preferred_element_type=F32
+            res_ref[rng, :], dt[...], (((1,), (1,)), ((), ())), preferred_element_type=F32
         ).T
-        for c in range(0, cols, COL_TILE):
-            cr = slice(c, c + COL_TILE)
-            acc[:, cr] += jnp.dot(at[:, rng], rs[:, cr], preferred_element_type=F32)
         return carry
 
     lax.fori_loop(0, rows // ROW_TILE, step, 0)
@@ -148,36 +160,56 @@
         dst = pl.ds(x * ka, ka)
         keep_ref[dst, :] = gs[pl.ds(pl.multiple_of(owner_item(x, 0) * ka, ka), ka), :]
         give_ref[dst, :] = gs[pl.ds(pl.multiple_of(owner_item(x, 1) * ka, ka), ka), :].astype(BF)
+
+
+def ability_gradient(half, d_blocks, bias, response, n_mp, n_item):
+    rows, k = half.shape
+    cols = response.shape[1]
+    shape = jax.ShapeDtypeStruct
+    vmem = pl.BlockSpec(memory_space=pltpu.VMEM)
+    return pl.pallas_call(
+        functools.partial(ability_kernel, n_mp, n_item),
+        out_shape=[shape((rows, cols), BF), shape((k // 2, rows), F32), shape((k // 2, rows), BF)],
+        in_specs=[vmem] * (3 + n_mp),
+        out_specs=[vmem] * 3,
+        scratch_shapes=[pltpu.VMEM((k, cols), BF), pltpu.VMEM((k, rows), F32)],
+        compiler_params=pltpu.CompilerParams(vmem_limit_bytes=VMEM_BYTES),
+        cost_estimate=pl.CostEstimate(
+            flops=2 * 2 * rows * cols * k, bytes_accessed=4 * rows * cols, transcendentals=rows * cols
+        ),
+        name="residual_ability_gradient",
+    )(half, *d_blocks, bias, response)
+
+
+def discrim_kernel(n_mp, at, res, *refs):
+    h_out, acc = refs[:n_mp], refs[n_mp]
+    kd, cols = h_out[0].shape
+    m = lax.axis_index("mp")
+    for c in range(0, cols, COL_TILE):
+        cr = slice(c, c + COL_TILE)
+        acc[:, cr] = jnp.dot(at[...], res[:, cr], preferred_element_type=F32)
     for x in range(n_mp):
         h = acc[pl.ds(pl.multiple_of((m ^ x) * kd, kd), kd), :]
         h_out[x][...] = h.astype(h_out[x].dtype)
 
 
-def gradients(at, half, d_blocks, bias, response, n_mp, n_item):
+def discrim_gradient(at, res, n_mp):
     k, rows = at.shape
-    kd, cols = d_blocks[0].shape
-    flops = 3 * 2 * rows * cols * k
+    cols = res.shape[1]
     shape = jax.ShapeDtypeStruct
     vmem = pl.BlockSpec(memory_space=pltpu.VMEM)
-    outs = [shape((k // 2, rows), F32), shape((k // 2, rows), BF)]
-    outs += [shape((kd, cols), BF if q else F32) for q in range(n_mp)]
-    return pl.pallas_call(
-        functools.partial(grad_kernel, n_mp, n_item),
-        out_shape=outs,
-        in_specs=[vmem] * (4 + n_mp),
-        out_specs=[vmem] * len(outs),
-        scratch_shapes=[
-            pltpu.VMEM((k, cols), BF),
-            pltpu.VMEM((ROW_TILE, cols), BF),
-            pltpu.VMEM((k, rows), F32),
-            pltpu.VMEM((k, cols), F32),
-        ],
-        compiler_params=pltpu.CompilerParams(vmem_limit_bytes=VMEM_BYTES),
+    return pl.pallas_call(
+        functools.partial(discrim_kernel, n_mp),
+        out_shape=[shape((k // n_mp, cols), BF if q else F32) for q in range(n_mp)],
+        in_specs=[vmem] * 2,
+        out_specs=[vmem] * n_mp,
+        scratch_shapes=[pltpu.VMEM((k, cols), F32)],
+        compiler_params=pltpu.CompilerParams(vmem_limit_bytes=SMALL_VMEM * 2),
         cost_estimate=pl.CostEstimate(
-            flops=flops, bytes_accessed=4 * rows * cols, transcendentals=rows * cols
+            flops=2 * rows * cols * k, bytes_accessed=2 * rows * cols, transcendentals=0
         ),
-        name="residual_gradients",
-    )(at, half, *d_blocks, bias, response)
+        name="discrim_gradient",
+    )(at, res)
 
 
 def pair_kernel(keep_ref, got_ref, *outs):
@@ -187,14 +219,28 @@
         out[...] = (keep_ref[rng, :] + got_ref[rng, :].astype(F32)).astype(out.dtype)
 
 
-def pair_sum(keep, got, chips):
-    shape = (keep.shape[0] // chips, keep.shape[1])
+def pair_sum(keep, got, kinds):
+    shape = (keep.shape[0] // len(kinds), keep.shape[1])
     return pl.pallas_call(
         pair_kernel,
-        out_shape=[jax.ShapeDtypeStruct(shape, BF if x else F32) for x in range(chips)],
+        out_shape=[jax.ShapeDtypeStruct(shape, kind) for kind in kinds],
         compiler_params=pltpu.CompilerParams(vmem_limit_bytes=SMALL_VMEM),
         name="core_pair_sum",
     )(keep, got)
+
+
+def add_kernel(x_ref, y_ref, out_ref):
+    out_ref[...] = (x_ref[...] + y_ref[...].astype(F32)).astype(BF)
+
+
+def add(x, y):
+    return pl.pallas_call(
+        add_kernel,
+        out_shape=jax.ShapeDtypeStruct(x.shape, BF),
+        compiler_params=pltpu.CompilerParams(vmem_limit_bytes=SMALL_VMEM),
+        cost_estimate=pl.CostEstimate(flops=4000000000, bytes_accessed=8 * x.size, transcendentals=0),
+        name="add_partial",
+    )(x, y)
 
 
 def adam_kernel(plan, *refs):
@@ -251,11 +297,20 @@
     theirs[0], difficulty = lax.optimization_barrier((theirs[0], difficulty))
     bias = (0.5 * difficulty).reshape(1, cols)
     at, half = place_ability(mine + theirs, n_item)
-    keep, give, *h = gradients(at, half, d_blocks, bias, response, n_mp, n_item)
-
+    res, keep, give = ability_gradient(half, d_blocks, bias, response, n_mp, n_item)
+    got = send_core(give)
+    h = list(discrim_gradient(at, res, n_mp))
+
+    via = [x for x in range(3, chips, 2)]
+    got, h[0] = lax.optimization_barrier((got, h[0]))
+    g = list(pair_sum(keep, got, [F32 if x == 0 or x ^ 1 in via else BF for x in range(chips)]))
+    for x in via:
+        g[x ^ 1] = add(g[x ^ 1], send_chip(g[x], 1))
+    if via:
+        last = max(via) ^ 1
+        g[1], g[last] = lax.optimization_barrier((g[1], g[last]))
     h_terms = [h[0]] + [send_mp(h[x], (x, x)) for x in range(1, n_mp)]
-    g = pair_sum(keep, send_core(give), chips)
-    g_terms = [g[0]] + [send_chip(g[x], x) for x in range(1, chips)]
+    g_terms = [g[0]] + [send_chip(g[x], x) for x in range(chips - 1, 0, -1) if x not in via]
     a_state = (a_t, ability_m.T, ability_v.T)
     d_state = (d_t, discrim_m.T, discrim_v.T)
     d_out = list(adam((h_terms, d_state, 0.5 * math.sqrt(1.0 / ckpts_total), 0.01)))

time: 50.3 us -> 49.1 us (0.976)
  starting transfers between devices: 20.6 us -> 18.4 us
  waiting for transfers between devices: 14.4 us -> 16.4 us
  local copies, waits for them, and re-layouts: 2.03 us -> 1.1 us
    ppermute x6, starting transfers between devices: 11.4 us -> 9.3 us  [send_chip(): return lax.ppermute(x, 'item', swap_item(n_item, 2 * mask))]
    ppermute x6, waiting for transfers between devices: 4.9 us -> 6.39 us  [send_mp(): return lax.ppermute(x, ('mp', 'item'), swap_mp(n_mp, n_item, *masks))]
    unnamed x20 -> x16, local copies, waits for them, and re-layouts: 2.03 us -> 1.1 us
    ppermute x6, waiting for transfers between devices: 8.16 us -> 8.73 us  [send_chip(): return lax.ppermute(x, 'item', swap_item(n_item, 2 * mask))]
    pallas_call x2 -> x5, Pallas kernels: 9.07 us -> 9.26 us  [the longest x1 6.67 us: ability_gradient(): pl.pallas_call(functools.partial(ability_kernel, n_mp, n_item), out_shape...]
  transfers between devices with their start and end apart: 17 -> 17, of which waited for: 8 -> 8; matrix products, arithmetic and copies ran while one was open for 0% -> 0% of each run, Pallas kernels for 4% -> 9%
where the time goes in v5:
time: 49.1 us; the launch traced here: 48.9 us
  starting transfers between devices  18.4 us (37%)
  waiting for transfers between devices  16.4 us (33%)
  Pallas kernels  12.2 us (25%)
  local copies, waits for them, and re-layouts  1.1 us (2%)
  between operations  0.8 us (2%)
    ppermute x6, starting transfers between devices, send_chip(): return lax.ppermute(x, 'item', swap_item(n_item, 2 * mask))  9.3 us
    ppermute x6, waiting for transfers between devices, send_chip(): return lax.ppermute(x, 'item', swap_item(n_item, 2 * mask))  8.73 us
    ppermute x6, starting transfers between devices, send_mp(): return lax.ppermute(x, ('mp', 'item'), swap_mp(n_mp, n_item, *masks))  8.52 us
    pallas_call x1, Pallas kernels, ability_gradient(): pl.pallas_call(functools.partial(ability_kernel, n_mp, n_item), out_shape...  6.67 us
    ppermute x6, waiting for transfers between devices, send_mp(): return lax.ppermute(x, ('mp', 'item'), swap_mp(n_mp, n_item, *masks))  6.39 us
    pallas_call x1, Pallas kernels, discrim_gradient(): pl.pallas_call(functools.partial(discrim_kernel, n_mp), out_shape=[shape(...  2.46 us
    pallas_call x2, Pallas kernels, adam(): pl.pallas_call(functools.partial(adam_kernel, plan), out_shape=outs, comp...  2.38 us
    ppermute x5, waiting for transfers between devices, send_core(): return lax.ppermute(x, 'item', swap_item(n_item, 1))  1.33 us
  transfers between devices with their start and end apart: 17, of which 8 were waited for; matrix products, arithmetic and copies ran while one was open for 0% of the time, Pallas kernels for 9%

profile of v5, /device:TPU:0, one launch (start us, length us, event | category | flops | bytes accessed | tf_op | source)
XLA Modules:
  0.0 48.9 jit_solution(152272297391933737)
XLA Ops:
  0.7 1.0 %copy-done.1 = f32[2048,64]{0,1:T(8,128)S(1)} copy-done((f32[2048,64]{0,1:T(8,128)S(1)}, f32[2048,64]{0,1:T(8,128)}, u32[]{:S(2)}) %copy-start.1) | copy-done | bytes 524312
  1.8 3.0 %collective-permute-start.1 = (bf16[64,2048]{1,0:T(8,128)(2,1)S(1)}, bf16[64,2048]{1,0:T(8,128)(2,1)S(1)}, u32[]{:S(2)}, u32[]{:S(2)}) collective-permute-start(bf16[64,2048]{1,0:T(8,128)(2,1)S(1)} %get-tuple-element.38.refs_1_), channel_id=1, source_target_pairs={{0,16},{1,9},{2,18},{3,11},{4,20},{5,13},{6,22},{7,15},{8,24},{9,1... | collective-permute-start | bytes 786440 | tf_op jit(solution)/shard_map/ppermute | solution.py:287
  4.9 1.5 %collective-permute-start.8 = (bf16[64,2048]{1,0:T(8,128)(2,1)S(1)}, bf16[64,2048]{1,0:T(8,128)(2,1)S(1)}, u32[]{:S(2)}, u32[]{:S(2)}) collective-permute-start(bf16[64,2048]{1,0:T(8,128)(2,1)S(1)} %get-tuple-element.38.refs_1_), channel_id=1, source_target_pairs={{0,8},{1,17},{2,10},{3,19},{4,12},{5,21},{6,14},{7,23},{8,0},{9,25... | collective-permute-start | bytes 786440 | tf_op jit(solution)/shard_map/ppermute | solution.py:287
  6.4 3.6 %collective-permute-start = (bf16[32,2048]{1,0:T(8,128)(2,1)S(1)}, bf16[32,2048]{1,0:T(8,128)(2,1)S(1)}, u32[]{:S(2)}, u32[]{:S(2)}) collective-permute-start(bf16[32,2048]{1,0:T(8,128)(2,1)S(1)} %get-tuple-element.37.refs_0_), channel_id=1, source_target_pairs={{0,6},{1,7},{2,4},{3,5},{4,2},{5,3},{6,0},{7,1},{8,14},{9,15},{10,... | collective-permute-start | bytes 393224 | tf_op jit(solution)/shard_map/ppermute | solution.py:281
  10.0 4.3 %collective-permute-done.refs_1_ = bf16[32,2048]{1,0:T(8,128)(2,1)S(1)} collective-permute-done((bf16[32,2048]{1,0:T(8,128)(2,1)S(1)}, bf16[32,2048]{1,0:T(8,128)(2,1)S(1)}, u32[]{:S(2)}, u32[]{:S(2)}) %collective-permute-start) | collective-permute-done | bytes 131104 | tf_op jit(solution)/shard_map/ppermute | solution.py:281
  14.3 1.1 %collective-permute-start.3 = (bf16[32,2048]{1,0:T(8,128)(2,1)S(1)}, bf16[32,2048]{1,0:T(8,128)(2,1)S(1)}, u32[]{:S(2)}, u32[]{:S(2)}) collective-permute-start(bf16[32,2048]{1,0:T(8,128)(2,1)S(1)} %collective-permute-done.refs_1_), channel_id=1, source_target_pairs={{0,2},{1,3},{2,0},{3,1},{4,6},{5,7},{6,4},{7,5},{8,10},{9,11},{10,... | collective-permute-start | bytes 393224 | tf_op jit(solution)/shard_map/ppermute | solution.py:281
  15.4 0.5 %collective-permute-start.9 = (bf16[64,2048]{1,0:T(8,128)(2,1)S(1)}, bf16[64,2048]{1,0:T(8,128)(2,1)S(1)}, u32[]{:S(2)}, u32[]{:S(2)}) collective-permute-start(bf16[64,2048]{1,0:T(8,128)(2,1)S(1)} %collective-permute-done.8.refs_2_), channel_id=1, source_target_pairs={{0,16},{1,9},{2,18},{3,11},{4,20},{5,13},{6,22},{7,15},{8,24},{9,1... | collective-permute-start | bytes 786440 | tf_op jit(solution)/shard_map/ppermute | solution.py:287
  16.0 0.8 %collective-permute-done.2.refs_2_ = bf16[32,2048]{1,0:T(8,128)(2,1)S(1)} collective-permute-done((bf16[32,2048]{1,0:T(8,128)(2,1)S(1)}, bf16[32,2048]{1,0:T(8,128)(2,1)S(1)}, u32[]{:S(2)}, u32[]{:S(2)}) %collective-permute-start.2) | collective-permute-done | bytes 131104 | tf_op jit(solution)/shard_map/ppermute | solution.py:281
  16.7 0.5 %collective-permute-start.5 = (bf16[32,2048]{1,0:T(8,128)(2,1)S(1)}, bf16[32,2048]{1,0:T(8,128)(2,1)S(1)}, u32[]{:S(2)}, u32[]{:S(2)}) collective-permute-start(bf16[32,2048]{1,0:T(8,128)(2,1)S(1)} %collective-permute-done.refs_1_), channel_id=1, source_target_pairs={{0,1},{1,0},{2,3},{3,2},{4,5},{5,4},{6,7},{7,6},{8,9},{9,8},{10,11... | collective-permute-start | bytes 393224 | tf_op jit(solution)/shard_map/ppermute | solution.py:284
  17.3 2.1 %collective-permute-done.3.refs_3_ = bf16[32,2048]{1,0:T(8,128)(2,1)S(1)} collective-permute-done((bf16[32,2048]{1,0:T(8,128)(2,1)S(1)}, bf16[32,2048]{1,0:T(8,128)(2,1)S(1)}, u32[]{:S(2)}, u32[]{:S(2)}) %collective-permute-start.3) | collective-permute-done | bytes 131104 | tf_op jit(solution)/shard_map/ppermute | solution.py:281
  19.4 1.3 %collective-permute-done.7.refs_7_ = bf16[32,2048]{1,0:T(8,128)(2,1)S(1)} collective-permute-done((bf16[32,2048]{1,0:T(8,128)(2,1)S(1)}, bf16[32,2048]{1,0:T(8,128)(2,1)S(1)}, u32[]{:S(2)}, u32[]{:S(2)}) %collective-permute-start.7) | collective-permute-done | bytes 131104 | tf_op jit(solution)/shard_map/ppermute | solution.py:284
  20.7 0.4 place_ability.1
  21.1 0.7 %collective-permute-done.9.refs_4_ = bf16[64,2048]{1,0:T(8,128)(2,1)S(1)} collective-permute-done((bf16[64,2048]{1,0:T(8,128)(2,1)S(1)}, bf16[64,2048]{1,0:T(8,128)(2,1)S(1)}, u32[]{:S(2)}, u32[]{:S(2)}) %collective-permute-start.9) | collective-permute-done | bytes 262176 | tf_op jit(solution)/shard_map/ppermute | solution.py:287
  21.8 6.7 %residual_ability_gradient.1 = (bf16[2048,2048]{1,0:T(8,128)(2,1)S(1)}, f32[128,2048]{1,0:T(8,128)S(1)}, bf16[128,2048]{1,0:T(8,128)(2,1)S(1)}) custom-call(bf16[2048,256]{1,0:T(8,128)(2,1)S(1)} %get-tuple-element.41.refs_0_, bf16[64,2048]{1,0:T(8,128)(2,1)S(1)} %get-tuple-element.38.refs_1_, bf16[64,2048]{1,0:T(8,128)(2,1)S(1)} %collective-permute-done.8.refs_2_, ...), custom_call_target="tpu_custom_call" | custom-call | flops 4294967296 | bytes 16777216 | tf_op jit(solution)/shard_map/residual_ability_gradient/pallas_call | solution.py:170
  28.6 2.5 %discrim_gradient.1 = (f32[64,2048]{1,0:T(8,128)S(1)}, bf16[64,2048]{1,0:T(8,128)(2,1)S(1)}, bf16[64,2048]{1,0:T(8,128)(2,1)S(1)}, bf16[64,2048]{1,0:T(8,128)(2,1)S(1)}) custom-call(bf16[256,2048]{1,0:T(8,128)(2,1)S(1)} %get-tuple-element.46.at, bf16[2048,2048]{1,0:T(8,128)(2,1)S(1)} %get-tuple-element.47.res), custom_call_target="tpu_custom_call" | custom-call | flops 2147483648 | bytes 8388608 | tf_op jit(solution)/shard_map/discrim_gradient/pallas_call | solution.py:201
  31.2 1.0 %collective-permute-start.14 = (bf16[32,2048]{1,0:T(8,128)(2,1)S(1)}, bf16[32,2048]{1,0:T(8,128)(2,1)S(1)}, u32[]{:S(2)}, u32[]{:S(2)}) collective-permute-start(bf16[32,2048]{1,0:T(8,128)(2,1)S(1)} %get-tuple-element.59), channel_id=1, source_target_pairs={{0,2},{1,3},{2,0},{3,1},{4,6},{5,7},{6,4},{7,5},{8,10},{9,11},{10,... | collective-permute-start | bytes 393224 | tf_op jit(solution)/shard_map/ppermute | solution.py:281
  32.2 0.5 %collective-permute-start.11 = (bf16[64,2048]{1,0:T(8,128)(2,1)S(1)}, bf16[64,2048]{1,0:T(8,128)(2,1)S(1)}, u32[]{:S(2)}, u32[]{:S(2)}) collective-permute-start(bf16[64,2048]{1,0:T(8,128)(2,1)S(1)} %get-tuple-element.52), channel_id=1, source_target_pairs={{0,8},{1,9},{2,10},{3,11},{4,12},{5,13},{6,14},{7,15},{8,0},{9,1},... | collective-permute-start | bytes 786440 | tf_op jit(solution)/shard_map/ppermute | solution.py:287
  33.0 2.7 %collective-permute-start.13 = (bf16[64,2048]{1,0:T(8,128)(2,1)S(1)}, bf16[64,2048]{1,0:T(8,128)(2,1)S(1)}, u32[]{:S(2)}, u32[]{:S(2)}) collective-permute-start(bf16[64,2048]{1,0:T(8,128)(2,1)S(1)} %get-tuple-element.54), channel_id=1, source_target_pairs={{0,24},{1,25},{2,26},{3,27},{4,28},{5,29},{6,30},{7,31},{8,16},{9,... | collective-permute-start | bytes 786440 | tf_op jit(solution)/shard_map/ppermute | solution.py:287
  35.7 1.5 %collective-permute-done.14.y_ref = bf16[32,2048]{1,0:T(8,128)(2,1)S(1)} collective-permute-done((bf16[32,2048]{1,0:T(8,128)(2,1)S(1)}, bf16[32,2048]{1,0:T(8,128)(2,1)S(1)}, u32[]{:S(2)}, u32[]{:S(2)}) %collective-permute-start.14) | collective-permute-done | bytes 131104 | tf_op jit(solution)/shard_map/ppermute | solution.py:281
  37.2 3.2 %collective-permute-start.15 = (bf16[32,2048]{1,0:T(8,128)(2,1)S(1)}, bf16[32,2048]{1,0:T(8,128)(2,1)S(1)}, u32[]{:S(2)}, u32[]{:S(2)}) collective-permute-start(bf16[32,2048]{1,0:T(8,128)(2,1)S(1)} %add_partial.1), channel_id=1, source_target_pairs={{0,4},{1,5},{2,6},{3,7},{4,0},{5,1},{6,2},{7,3},{8,12},{9,13},{10,... | collective-permute-start | bytes 393224 | tf_op jit(solution)/shard_map/ppermute | solution.py:281
  40.8 0.5 %collective-permute-done.11.refs_1_ = bf16[64,2048]{1,0:T(8,128)(2,1)S(1)} collective-permute-done((bf16[64,2048]{1,0:T(8,128)(2,1)S(1)}, bf16[64,2048]{1,0:T(8,128)(2,1)S(1)}, u32[]{:S(2)}, u32[]{:S(2)}) %collective-permute-start.11) | collective-permute-done | bytes 262176 | tf_op jit(solution)/shard_map/ppermute | solution.py:287
  41.3 5.2 %collective-permute-done.12.refs_2_ = bf16[64,2048]{1,0:T(8,128)(2,1)S(1)} collective-permute-done((bf16[64,2048]{1,0:T(8,128)(2,1)S(1)}, bf16[64,2048]{1,0:T(8,128)(2,1)S(1)}, u32[]{:S(2)}, u32[]{:S(2)}) %collective-permute-start.12) | collective-permute-done | bytes 262176 | tf_op jit(solution)/shard_map/ppermute | solution.py:287
  46.5 1.4 %adam.2 = (f32[64,2048]{1,0:T(8,128)}, f32[64,2048]{1,0:T(8,128)}, f32[64,2048]{1,0:T(8,128)}) custom-call(f32[64,2048]{1,0:T(8,128)S(1)} %get-tuple-element.51.refs_0_, bf16[64,2048]{1,0:T(8,128)(2,1)S(1)} %collective-permute-done.11.refs_1_, bf16[64,2048]{1,0:T(8,128)(2,1)S(1)} %collective-permute-done.12.refs_2_, ...), custom_call_target="tpu_custom_call" | custom-call | tf_op jit(solution)/shard_map/adam/pallas_call | solution.py:264
  47.9 1.0 %adam.3 = (f32[32,2048]{1,0:T(8,128)}, f32[32,2048]{1,0:T(8,128)}, f32[32,2048]{1,0:T(8,128)}) custom-call(f32[32,2048]{1,0:T(8,128)S(1)} %get-tuple-element.56.refs_0_, bf16[32,2048]{1,0:T(8,128)(2,1)S(1)} %collective-permute-done.15.refs_1_, bf16[32,2048]{1,0:T(8,128)(2,1)S(1)} %collective-permute-done.16.refs_2_, f32[32,2048]{1,0:T(8,128)S(1)} %bitcast.16, ...), custom_call_target="tpu_custom_call" | custom-call | tf_op jit(solution)/shard_map/adam/pallas_call | solution.py:264
  (36 shorter events, 1.1 us)
Async XLA Ops:
  0.6 1.1 %copy-start.2 = (f32[2048,32]{0,1:T(8,128)S(1)}, f32[2048,32]{0,1:T(8,128)}, u32[]{:S(2)}) copy-start(f32[2048,32]{0,1:T(8,128)} %param.10) | copy-start | bytes 786436
  0.7 18.7 %copy-start.7 = (f32[2048]{0:T(1024)S(1)}, f32[2048]{0:T(1024)}, u32[]{:S(2)}) copy-start(f32[2048]{0:T(1024)} %param.9) | copy-start | bytes 24580
  0.7 21.2 %copy-start = (s32[2048,2048]{1,0:T(8,128)S(1)}, s32[2048,2048]{1,0:T(8,128)}, u32[]{:S(2)}) copy-start(s32[2048,2048]{1,0:T(8,128)} %refs_6_.1) | copy-start | bytes 50331652
  1.8 12.5 %collective-permute-start.1 = (bf16[64,2048]{1,0:T(8,128)(2,1)S(1)}, bf16[64,2048]{1,0:T(8,128)(2,1)S(1)}, u32[]{:S(2)}, u32[]{:S(2)}) collective-permute-start(bf16[64,2048]{1,0:T(8,128)(2,1)S(1)} %get-tuple-element.38.refs_1_), channel_id=1, source_target_pairs={{0,16},{1,9},{2,18},{3,11},{4,20},{5,13},{6,22},{7,15},{8,24},{9,1... | collective-permute-start | bytes 786440 | tf_op jit(solution)/shard_map/ppermute | solution.py:287
  4.9 10.6 %collective-permute-start.8 = (bf16[64,2048]{1,0:T(8,128)(2,1)S(1)}, bf16[64,2048]{1,0:T(8,128)(2,1)S(1)}, u32[]{:S(2)}, u32[]{:S(2)}) collective-permute-start(bf16[64,2048]{1,0:T(8,128)(2,1)S(1)} %get-tuple-element.38.refs_1_), channel_id=1, source_target_pairs={{0,8},{1,17},{2,10},{3,19},{4,12},{5,21},{6,14},{7,23},{8,0},{9,25... | collective-permute-start | bytes 786440 | tf_op jit(solution)/shard_map/ppermute | solution.py:287
  6.4 8.0 %collective-permute-start = (bf16[32,2048]{1,0:T(8,128)(2,1)S(1)}, bf16[32,2048]{1,0:T(8,128)(2,1)S(1)}, u32[]{:S(2)}, u32[]{:S(2)}) collective-permute-start(bf16[32,2048]{1,0:T(8,128)(2,1)S(1)} %get-tuple-element.37.refs_0_), channel_id=1, source_target_pairs={{0,6},{1,7},{2,4},{3,5},{4,2},{5,3},{6,0},{7,1},{8,14},{9,15},{10,... | collective-permute-start | bytes 393224 | tf_op jit(solution)/shard_map/ppermute | solution.py:281
  10.0 6.0 %collective-permute-start.4 = (bf16[32,2048]{1,0:T(8,128)(2,1)S(1)}, bf16[32,2048]{1,0:T(8,128)(2,1)S(1)}, u32[]{:S(2)}, u32[]{:S(2)}) collective-permute-start(bf16[32,2048]{1,0:T(8,128)(2,1)S(1)} %get-tuple-element.37.refs_0_), channel_id=1, source_target_pairs={{0,1},{1,0},{2,3},{3,2},{4,5},{5,4},{6,7},{7,6},{8,9},{9,8},{10,11... | collective-permute-start | bytes 393224 | tf_op jit(solution)/shard_map/ppermute | solution.py:284
  10.0 6.8 %collective-permute-start.2 = (bf16[32,2048]{1,0:T(8,128)(2,1)S(1)}, bf16[32,2048]{1,0:T(8,128)(2,1)S(1)}, u32[]{:S(2)}, u32[]{:S(2)}) collective-permute-start(bf16[32,2048]{1,0:T(8,128)(2,1)S(1)} %get-tuple-element.37.refs_0_), channel_id=1, source_target_pairs={{0,2},{1,3},{2,0},{3,1},{4,6},{5,7},{6,4},{7,5},{8,10},{9,11},{10,... | collective-permute-start | bytes 393224 | tf_op jit(solution)/shard_map/ppermute | solution.py:281
  14.3 5.0 %collective-permute-start.3 = (bf16[32,2048]{1,0:T(8,128)(2,1)S(1)}, bf16[32,2048]{1,0:T(8,128)(2,1)S(1)}, u32[]{:S(2)}, u32[]{:S(2)}) collective-permute-start(bf16[32,2048]{1,0:T(8,128)(2,1)S(1)} %collective-permute-done.refs_1_), channel_id=1, source_target_pairs={{0,2},{1,3},{2,0},{3,1},{4,6},{5,7},{6,4},{7,5},{8,10},{9,11},{10,... | collective-permute-start | bytes 393224 | tf_op jit(solution)/shard_map/ppermute | solution.py:281
  15.4 6.4 %collective-permute-start.9 = (bf16[64,2048]{1,0:T(8,128)(2,1)S(1)}, bf16[64,2048]{1,0:T(8,128)(2,1)S(1)}, u32[]{:S(2)}, u32[]{:S(2)}) collective-permute-start(bf16[64,2048]{1,0:T(8,128)(2,1)S(1)} %collective-permute-done.8.refs_2_), channel_id=1, source_target_pairs={{0,16},{1,9},{2,18},{3,11},{4,20},{5,13},{6,22},{7,15},{8,24},{9,1... | collective-permute-start | bytes 786440 | tf_op jit(solution)/shard_map/ppermute | solution.py:287
  16.7 2.6 %collective-permute-start.6 = (bf16[32,2048]{1,0:T(8,128)(2,1)S(1)}, bf16[32,2048]{1,0:T(8,128)(2,1)S(1)}, u32[]{:S(2)}, u32[]{:S(2)}) collective-permute-start(bf16[32,2048]{1,0:T(8,128)(2,1)S(1)} %collective-permute-done.2.refs_2_), channel_id=1, source_target_pairs={{0,1},{1,0},{2,3},{3,2},{4,5},{5,4},{6,7},{7,6},{8,9},{9,8},{10,11... | collective-permute-start | bytes 393224 | tf_op jit(solution)/shard_map/ppermute | solution.py:284
  16.7 2.6 %collective-permute-start.5 = (bf16[32,2048]{1,0:T(8,128)(2,1)S(1)}, bf16[32,2048]{1,0:T(8,128)(2,1)S(1)}, u32[]{:S(2)}, u32[]{:S(2)}) collective-permute-start(bf16[32,2048]{1,0:T(8,128)(2,1)S(1)} %collective-permute-done.refs_1_), channel_id=1, source_target_pairs={{0,1},{1,0},{2,3},{3,2},{4,5},{5,4},{6,7},{7,6},{8,9},{9,8},{10,11... | collective-permute-start | bytes 393224 | tf_op jit(solution)/shard_map/ppermute | solution.py:284
  19.3 1.3 %collective-permute-start.7 = (bf16[32,2048]{1,0:T(8,128)(2,1)S(1)}, bf16[32,2048]{1,0:T(8,128)(2,1)S(1)}, u32[]{:S(2)}, u32[]{:S(2)}) collective-permute-start(bf16[32,2048]{1,0:T(8,128)(2,1)S(1)} %collective-permute-done.3.refs_3_), channel_id=1, source_target_pairs={{0,1},{1,0},{2,3},{3,2},{4,5},{5,4},{6,7},{7,6},{8,9},{9,8},{10,11... | collective-permute-start | bytes 393224 | tf_op jit(solution)/shard_map/ppermute | solution.py:284
  28.5 18.0 %copy-start.3 = (f32[2048,64]{0,1:T(8,128)S(1)}, f32[2048,64]{0,1:T(8,128)}, u32[]{:S(2)}) copy-start(f32[2048,64]{0,1:T(8,128)} %param.14) | copy-start | bytes 1572868
  28.5 18.0 %copy-start.4 = (f32[2048,64]{0,1:T(8,128)S(1)}, f32[2048,64]{0,1:T(8,128)}, u32[]{:S(2)}) copy-start(f32[2048,64]{0,1:T(8,128)} %param.15) | copy-start | bytes 1572868
  28.5 19.4 %copy-start.5 = (f32[2048,32]{0,1:T(8,128)S(1)}, f32[2048,32]{0,1:T(8,128)}, u32[]{:S(2)}) copy-start(f32[2048,32]{0,1:T(8,128)} %param.11) | copy-start | bytes 786436
  28.5 19.4 %copy-start.6 = (f32[2048,32]{0,1:T(8,128)S(1)}, f32[2048,32]{0,1:T(8,128)}, u32[]{:S(2)}) copy-start(f32[2048,32]{0,1:T(8,128)} %param.12) | copy-start | bytes 786436
  28.5 2.5 %collective-permute-start.10 = (bf16[128,2048]{1,0:T(8,128)(2,1)S(1)}, bf16[128,2048]{1,0:T(8,128)(2,1)S(1)}, u32[]{:S(2)}, u32[]{:S(2)}) collective-permute-start(bf16[128,2048]{1,0:T(8,128)(2,1)S(1)} %get-tuple-element.45), channel_id=1, source_target_pairs={{0,1},{1,0},{2,3},{3,2},{4,5},{5,4},{6,7},{7,6},{8,9},{9,8},{10,11... | collective-permute-start | bytes 1572872 | tf_op jit(solution)/shard_map/ppermute | solution.py:284
  31.2 6.0 %collective-permute-start.14 = (bf16[32,2048]{1,0:T(8,128)(2,1)S(1)}, bf16[32,2048]{1,0:T(8,128)(2,1)S(1)}, u32[]{:S(2)}, u32[]{:S(2)}) collective-permute-start(bf16[32,2048]{1,0:T(8,128)(2,1)S(1)} %get-tuple-element.59), channel_id=1, source_target_pairs={{0,2},{1,3},{2,0},{3,1},{4,6},{5,7},{6,4},{7,5},{8,10},{9,11},{10,... | collective-permute-start | bytes 393224 | tf_op jit(solution)/shard_map/ppermute | solution.py:281
  32.2 9.1 %collective-permute-start.11 = (bf16[64,2048]{1,0:T(8,128)(2,1)S(1)}, bf16[64,2048]{1,0:T(8,128)(2,1)S(1)}, u32[]{:S(2)}, u32[]{:S(2)}) collective-permute-start(bf16[64,2048]{1,0:T(8,128)(2,1)S(1)} %get-tuple-element.52), channel_id=1, source_target_pairs={{0,8},{1,9},{2,10},{3,11},{4,12},{5,13},{6,14},{7,15},{8,0},{9,1},... | collective-permute-start | bytes 786440 | tf_op jit(solution)/shard_map/ppermute | solution.py:287
  32.7 13.8 %collective-permute-start.12 = (bf16[64,2048]{1,0:T(8,128)(2,1)S(1)}, bf16[64,2048]{1,0:T(8,128)(2,1)S(1)}, u32[]{:S(2)}, u32[]{:S(2)}) collective-permute-start(bf16[64,2048]{1,0:T(8,128)(2,1)S(1)} %get-tuple-element.53), channel_id=1, source_target_pairs={{0,16},{1,17},{2,18},{3,19},{4,20},{5,21},{6,22},{7,23},{8,24},{9,... | collective-permute-start | bytes 786440 | tf_op jit(solution)/shard_map/ppermute | solution.py:287
  33.0 13.5 %collective-permute-start.13 = (bf16[64,2048]{1,0:T(8,128)(2,1)S(1)}, bf16[64,2048]{1,0:T(8,128)(2,1)S(1)}, u32[]{:S(2)}, u32[]{:S(2)}) collective-permute-start(bf16[64,2048]{1,0:T(8,128)(2,1)S(1)} %get-tuple-element.54), channel_id=1, source_target_pairs={{0,24},{1,25},{2,26},{3,27},{4,28},{5,29},{6,30},{7,31},{8,16},{9,... | collective-permute-start | bytes 786440 | tf_op jit(solution)/shard_map/ppermute | solution.py:287
  37.2 10.7 %collective-permute-start.15 = (bf16[32,2048]{1,0:T(8,128)(2,1)S(1)}, bf16[32,2048]{1,0:T(8,128)(2,1)S(1)}, u32[]{:S(2)}, u32[]{:S(2)}) collective-permute-start(bf16[32,2048]{1,0:T(8,128)(2,1)S(1)} %add_partial.1), channel_id=1, source_target_pairs={{0,4},{1,5},{2,6},{3,7},{4,0},{5,1},{6,2},{7,3},{8,12},{9,13},{10,... | collective-permute-start | bytes 393224 | tf_op jit(solution)/shard_map/ppermute | solution.py:281
  40.4 7.5 %collective-permute-start.16 = (bf16[32,2048]{1,0:T(8,128)(2,1)S(1)}, bf16[32,2048]{1,0:T(8,128)(2,1)S(1)}, u32[]{:S(2)}, u32[]{:S(2)}) collective-permute-start(bf16[32,2048]{1,0:T(8,128)(2,1)S(1)} %get-tuple-element.61), channel_id=1, source_target_pairs={{0,2},{1,3},{2,0},{3,1},{4,6},{5,7},{6,4},{7,5},{8,10},{9,11},{10,... | collective-permute-start | bytes 393224 | tf_op jit(solution)/shard_map/ppermute | solution.py:281
  (1 other events, 1.0 us)

commit v6 on v5

--- a/solution.py
+++ b/solution.py
@@ -142,7 +142,7 @@
         dt[pl.ds(off, kd), :] = d_in[q][...]
 
     def step(t, carry):
-        rng = pl.ds(pl.multiple_of(t * ROW_TILE, ROW_TILE), ROW_TILE)
+        rng = pl.ds(t * ROW_TILE, ROW_TILE)
         for c in range(0, cols, COL_TILE):
             cr = slice(c, c + COL_TILE)
             lg = jnp.dot(half[rng, :], dt[:, cr], preferred_element_type=F32) + bias_ref[:, cr]
@@ -154,7 +154,8 @@
         ).T
         return carry
 
-    lax.fori_loop(0, rows // ROW_TILE, step, 0)
+    for t in range(rows // ROW_TILE):
+        step(t, 0)
 
     for x in range(chips):
         dst = pl.ds(x * ka, ka)

time: 49.1 us -> 48.2 us (0.982)
  Pallas kernels: 12.2 us -> 11.3 us
    pallas_call x1, Pallas kernels: 6.67 us -> 5.78 us  [ability_gradient(): pl.pallas_call(functools.partial(ability_kernel, n_mp, n_item), out_shape...]
where the time goes in v6:
time: 48.2 us; the launch traced here: 48 us
  starting transfers between devices  18.4 us (38%)
  waiting for transfers between devices  16.4 us (34%)
  Pallas kernels  11.3 us (23%)
  local copies, waits for them, and re-layouts  1.1 us (2%)
  between operations  0.8 us (2%)
    ppermute x6, starting transfers between devices, send_chip(): return lax.ppermute(x, 'item', swap_item(n_item, 2 * mask))  9.29 us
    ppermute x6, waiting for transfers between devices, send_chip(): return lax.ppermute(x, 'item', swap_item(n_item, 2 * mask))  8.73 us
    ppermute x6, starting transfers between devices, send_mp(): return lax.ppermute(x, ('mp', 'item'), swap_mp(n_mp, n_item, *masks))  8.52 us
    ppermute x6, waiting for transfers between devices, send_mp(): return lax.ppermute(x, ('mp', 'item'), swap_mp(n_mp, n_item, *masks))  6.39 us
    pallas_call x1, Pallas kernels, ability_gradient(): pl.pallas_call(functools.partial(ability_kernel, n_mp, n_item), out_shape...  5.78 us
    pallas_call x1, Pallas kernels, discrim_gradient(): pl.pallas_call(functools.partial(discrim_kernel, n_mp), out_shape=[shape(...  2.47 us
    pallas_call x2, Pallas kernels, adam(): pl.pallas_call(functools.partial(adam_kernel, plan), out_shape=outs, comp...  2.38 us
    ppermute x5, waiting for transfers between devices, send_core(): return lax.ppermute(x, 'item', swap_item(n_item, 1))  1.33 us
  transfers between devices with their start and end apart: 17, of which 8 were waited for; matrix products, arithmetic and copies ran while one was open for 0% of the time, Pallas kernels for 9%

profile of v6, /device:TPU:0, one launch (start us, length us, event | category | flops | bytes accessed | tf_op | source)
XLA Modules:
  0.0 48.0 jit_solution(16463209073958412277)
XLA Ops:
  0.7 1.0 %copy-done.1 = f32[2048,64]{0,1:T(8,128)S(1)} copy-done((f32[2048,64]{0,1:T(8,128)S(1)}, f32[2048,64]{0,1:T(8,128)}, u32[]{:S(2)}) %copy-start.1) | copy-done | bytes 524312
  1.8 3.0 %collective-permute-start.1 = (bf16[64,2048]{1,0:T(8,128)(2,1)S(1)}, bf16[64,2048]{1,0:T(8,128)(2,1)S(1)}, u32[]{:S(2)}, u32[]{:S(2)}) collective-permute-start(bf16[64,2048]{1,0:T(8,128)(2,1)S(1)} %get-tuple-element.38.refs_1_), channel_id=1, source_target_pairs={{0,16},{1,9},{2,18},{3,11},{4,20},{5,13},{6,22},{7,15},{8,24},{9,1... | collective-permute-start | bytes 786440 | tf_op jit(solution)/shard_map/ppermute | solution.py:288
  4.9 1.5 %collective-permute-start.8 = (bf16[64,2048]{1,0:T(8,128)(2,1)S(1)}, bf16[64,2048]{1,0:T(8,128)(2,1)S(1)}, u32[]{:S(2)}, u32[]{:S(2)}) collective-permute-start(bf16[64,2048]{1,0:T(8,128)(2,1)S(1)} %get-tuple-element.38.refs_1_), channel_id=1, source_target_pairs={{0,8},{1,17},{2,10},{3,19},{4,12},{5,21},{6,14},{7,23},{8,0},{9,25... | collective-permute-start | bytes 786440 | tf_op jit(solution)/shard_map/ppermute | solution.py:288
  6.4 3.6 %collective-permute-start = (bf16[32,2048]{1,0:T(8,128)(2,1)S(1)}, bf16[32,2048]{1,0:T(8,128)(2,1)S(1)}, u32[]{:S(2)}, u32[]{:S(2)}) collective-permute-start(bf16[32,2048]{1,0:T(8,128)(2,1)S(1)} %get-tuple-element.37.refs_0_), channel_id=1, source_target_pairs={{0,6},{1,7},{2,4},{3,5},{4,2},{5,3},{6,0},{7,1},{8,14},{9,15},{10,... | collective-permute-start | bytes 393224 | tf_op jit(solution)/shard_map/ppermute | solution.py:282
  10.0 4.3 %collective-permute-done.refs_1_ = bf16[32,2048]{1,0:T(8,128)(2,1)S(1)} collective-permute-done((bf16[32,2048]{1,0:T(8,128)(2,1)S(1)}, bf16[32,2048]{1,0:T(8,128)(2,1)S(1)}, u32[]{:S(2)}, u32[]{:S(2)}) %collective-permute-start) | collective-permute-done | bytes 131104 | tf_op jit(solution)/shard_map/ppermute | solution.py:282
  14.3 1.1 %collective-permute-start.3 = (bf16[32,2048]{1,0:T(8,128)(2,1)S(1)}, bf16[32,2048]{1,0:T(8,128)(2,1)S(1)}, u32[]{:S(2)}, u32[]{:S(2)}) collective-permute-start(bf16[32,2048]{1,0:T(8,128)(2,1)S(1)} %collective-permute-done.refs_1_), channel_id=1, source_target_pairs={{0,2},{1,3},{2,0},{3,1},{4,6},{5,7},{6,4},{7,5},{8,10},{9,11},{10,... | collective-permute-start | bytes 393224 | tf_op jit(solution)/shard_map/ppermute | solution.py:282
  15.4 0.5 %collective-permute-start.9 = (bf16[64,2048]{1,0:T(8,128)(2,1)S(1)}, bf16[64,2048]{1,0:T(8,128)(2,1)S(1)}, u32[]{:S(2)}, u32[]{:S(2)}) collective-permute-start(bf16[64,2048]{1,0:T(8,128)(2,1)S(1)} %collective-permute-done.8.refs_2_), channel_id=1, source_target_pairs={{0,16},{1,9},{2,18},{3,11},{4,20},{5,13},{6,22},{7,15},{8,24},{9,1... | collective-permute-start | bytes 786440 | tf_op jit(solution)/shard_map/ppermute | solution.py:288
  16.0 0.8 %collective-permute-done.2.refs_2_ = bf16[32,2048]{1,0:T(8,128)(2,1)S(1)} collective-permute-done((bf16[32,2048]{1,0:T(8,128)(2,1)S(1)}, bf16[32,2048]{1,0:T(8,128)(2,1)S(1)}, u32[]{:S(2)}, u32[]{:S(2)}) %collective-permute-start.2) | collective-permute-done | bytes 131104 | tf_op jit(solution)/shard_map/ppermute | solution.py:282
  16.7 0.5 %collective-permute-start.5 = (bf16[32,2048]{1,0:T(8,128)(2,1)S(1)}, bf16[32,2048]{1,0:T(8,128)(2,1)S(1)}, u32[]{:S(2)}, u32[]{:S(2)}) collective-permute-start(bf16[32,2048]{1,0:T(8,128)(2,1)S(1)} %collective-permute-done.refs_1_), channel_id=1, source_target_pairs={{0,1},{1,0},{2,3},{3,2},{4,5},{5,4},{6,7},{7,6},{8,9},{9,8},{10,11... | collective-permute-start | bytes 393224 | tf_op jit(solution)/shard_map/ppermute | solution.py:285
  17.3 2.1 %collective-permute-done.3.refs_3_ = bf16[32,2048]{1,0:T(8,128)(2,1)S(1)} collective-permute-done((bf16[32,2048]{1,0:T(8,128)(2,1)S(1)}, bf16[32,2048]{1,0:T(8,128)(2,1)S(1)}, u32[]{:S(2)}, u32[]{:S(2)}) %collective-permute-start.3) | collective-permute-done | bytes 131104 | tf_op jit(solution)/shard_map/ppermute | solution.py:282
  19.4 1.3 %collective-permute-done.7.refs_7_ = bf16[32,2048]{1,0:T(8,128)(2,1)S(1)} collective-permute-done((bf16[32,2048]{1,0:T(8,128)(2,1)S(1)}, bf16[32,2048]{1,0:T(8,128)(2,1)S(1)}, u32[]{:S(2)}, u32[]{:S(2)}) %collective-permute-start.7) | collective-permute-done | bytes 131104 | tf_op jit(solution)/shard_map/ppermute | solution.py:285
  20.7 0.4 place_ability.1
  21.1 0.7 %collective-permute-done.9.refs_4_ = bf16[64,2048]{1,0:T(8,128)(2,1)S(1)} collective-permute-done((bf16[64,2048]{1,0:T(8,128)(2,1)S(1)}, bf16[64,2048]{1,0:T(8,128)(2,1)S(1)}, u32[]{:S(2)}, u32[]{:S(2)}) %collective-permute-start.9) | collective-permute-done | bytes 262176 | tf_op jit(solution)/shard_map/ppermute | solution.py:288
  21.8 5.8 %residual_ability_gradient.1 = (bf16[2048,2048]{1,0:T(8,128)(2,1)S(1)}, f32[128,2048]{1,0:T(8,128)S(1)}, bf16[128,2048]{1,0:T(8,128)(2,1)S(1)}) custom-call(bf16[2048,256]{1,0:T(8,128)(2,1)S(1)} %get-tuple-element.41.refs_0_, bf16[64,2048]{1,0:T(8,128)(2,1)S(1)} %get-tuple-element.38.refs_1_, bf16[64,2048]{1,0:T(8,128)(2,1)S(1)} %collective-permute-done.8.refs_2_, ...), custom_call_target="tpu_custom_call" | custom-call | flops 4294967296 | bytes 16777216 | tf_op jit(solution)/shard_map/residual_ability_gradient/pallas_call | solution.py:171
  27.7 2.5 %discrim_gradient.1 = (f32[64,2048]{1,0:T(8,128)S(1)}, bf16[64,2048]{1,0:T(8,128)(2,1)S(1)}, bf16[64,2048]{1,0:T(8,128)(2,1)S(1)}, bf16[64,2048]{1,0:T(8,128)(2,1)S(1)}) custom-call(bf16[256,2048]{1,0:T(8,128)(2,1)S(1)} %get-tuple-element.46.at, bf16[2048,2048]{1,0:T(8,128)(2,1)S(1)} %get-tuple-element.47.res), custom_call_target="tpu_custom_call" | custom-call | flops 2147483648 | bytes 8388608 | tf_op jit(solution)/shard_map/discrim_gradient/pallas_call | solution.py:202
  30.3 1.0 %collective-permute-start.14 = (bf16[32,2048]{1,0:T(8,128)(2,1)S(1)}, bf16[32,2048]{1,0:T(8,128)(2,1)S(1)}, u32[]{:S(2)}, u32[]{:S(2)}) collective-permute-start(bf16[32,2048]{1,0:T(8,128)(2,1)S(1)} %get-tuple-element.59), channel_id=1, source_target_pairs={{0,2},{1,3},{2,0},{3,1},{4,6},{5,7},{6,4},{7,5},{8,10},{9,11},{10,... | collective-permute-start | bytes 393224 | tf_op jit(solution)/shard_map/ppermute | solution.py:282
  31.3 0.5 %collective-permute-start.11 = (bf16[64,2048]{1,0:T(8,128)(2,1)S(1)}, bf16[64,2048]{1,0:T(8,128)(2,1)S(1)}, u32[]{:S(2)}, u32[]{:S(2)}) collective-permute-start(bf16[64,2048]{1,0:T(8,128)(2,1)S(1)} %get-tuple-element.52), channel_id=1, source_target_pairs={{0,8},{1,9},{2,10},{3,11},{4,12},{5,13},{6,14},{7,15},{8,0},{9,1},... | collective-permute-start | bytes 786440 | tf_op jit(solution)/shard_map/ppermute | solution.py:288
  32.1 2.7 %collective-permute-start.13 = (bf16[64,2048]{1,0:T(8,128)(2,1)S(1)}, bf16[64,2048]{1,0:T(8,128)(2,1)S(1)}, u32[]{:S(2)}, u32[]{:S(2)}) collective-permute-start(bf16[64,2048]{1,0:T(8,128)(2,1)S(1)} %get-tuple-element.54), channel_id=1, source_target_pairs={{0,24},{1,25},{2,26},{3,27},{4,28},{5,29},{6,30},{7,31},{8,16},{9,... | collective-permute-start | bytes 786440 | tf_op jit(solution)/shard_map/ppermute | solution.py:288
  34.8 1.5 %collective-permute-done.14.y_ref = bf16[32,2048]{1,0:T(8,128)(2,1)S(1)} collective-permute-done((bf16[32,2048]{1,0:T(8,128)(2,1)S(1)}, bf16[32,2048]{1,0:T(8,128)(2,1)S(1)}, u32[]{:S(2)}, u32[]{:S(2)}) %collective-permute-start.14) | collective-permute-done | bytes 131104 | tf_op jit(solution)/shard_map/ppermute | solution.py:282
  36.3 3.2 %collective-permute-start.15 = (bf16[32,2048]{1,0:T(8,128)(2,1)S(1)}, bf16[32,2048]{1,0:T(8,128)(2,1)S(1)}, u32[]{:S(2)}, u32[]{:S(2)}) collective-permute-start(bf16[32,2048]{1,0:T(8,128)(2,1)S(1)} %add_partial.1), channel_id=1, source_target_pairs={{0,4},{1,5},{2,6},{3,7},{4,0},{5,1},{6,2},{7,3},{8,12},{9,13},{10,... | collective-permute-start | bytes 393224 | tf_op jit(solution)/shard_map/ppermute | solution.py:282
  39.9 0.5 %collective-permute-done.11.refs_1_ = bf16[64,2048]{1,0:T(8,128)(2,1)S(1)} collective-permute-done((bf16[64,2048]{1,0:T(8,128)(2,1)S(1)}, bf16[64,2048]{1,0:T(8,128)(2,1)S(1)}, u32[]{:S(2)}, u32[]{:S(2)}) %collective-permute-start.11) | collective-permute-done | bytes 262176 | tf_op jit(solution)/shard_map/ppermute | solution.py:288
  40.4 5.1 %collective-permute-done.12.refs_2_ = bf16[64,2048]{1,0:T(8,128)(2,1)S(1)} collective-permute-done((bf16[64,2048]{1,0:T(8,128)(2,1)S(1)}, bf16[64,2048]{1,0:T(8,128)(2,1)S(1)}, u32[]{:S(2)}, u32[]{:S(2)}) %collective-permute-start.12) | collective-permute-done | bytes 262176 | tf_op jit(solution)/shard_map/ppermute | solution.py:288
  45.6 1.4 %adam.2 = (f32[64,2048]{1,0:T(8,128)}, f32[64,2048]{1,0:T(8,128)}, f32[64,2048]{1,0:T(8,128)}) custom-call(f32[64,2048]{1,0:T(8,128)S(1)} %get-tuple-element.51.refs_0_, bf16[64,2048]{1,0:T(8,128)(2,1)S(1)} %collective-permute-done.11.refs_1_, bf16[64,2048]{1,0:T(8,128)(2,1)S(1)} %collective-permute-done.12.refs_2_, ...), custom_call_target="tpu_custom_call" | custom-call | tf_op jit(solution)/shard_map/adam/pallas_call | solution.py:265
  47.0 1.0 %adam.3 = (f32[32,2048]{1,0:T(8,128)}, f32[32,2048]{1,0:T(8,128)}, f32[32,2048]{1,0:T(8,128)}) custom-call(f32[32,2048]{1,0:T(8,128)S(1)} %get-tuple-element.56.refs_0_, bf16[32,2048]{1,0:T(8,128)(2,1)S(1)} %collective-permute-done.15.refs_1_, bf16[32,2048]{1,0:T(8,128)(2,1)S(1)} %collective-permute-done.16.refs_2_, f32[32,2048]{1,0:T(8,128)S(1)} %bitcast.16, ...), custom_call_target="tpu_custom_call" | custom-call | tf_op jit(solution)/shard_map/adam/pallas_call | solution.py:265
  (36 shorter events, 1.1 us)
Async XLA Ops:
  0.6 1.1 %copy-start.2 = (f32[2048,32]{0,1:T(8,128)S(1)}, f32[2048,32]{0,1:T(8,128)}, u32[]{:S(2)}) copy-start(f32[2048,32]{0,1:T(8,128)} %param.10) | copy-start | bytes 786436
  0.7 18.7 %copy-start.7 = (f32[2048]{0:T(1024)S(1)}, f32[2048]{0:T(1024)}, u32[]{:S(2)}) copy-start(f32[2048]{0:T(1024)} %param.9) | copy-start | bytes 24580
  0.7 21.2 %copy-start = (s32[2048,2048]{1,0:T(8,128)S(1)}, s32[2048,2048]{1,0:T(8,128)}, u32[]{:S(2)}) copy-start(s32[2048,2048]{1,0:T(8,128)} %refs_6_.1) | copy-start | bytes 50331652
  1.8 12.5 %collective-permute-start.1 = (bf16[64,2048]{1,0:T(8,128)(2,1)S(1)}, bf16[64,2048]{1,0:T(8,128)(2,1)S(1)}, u32[]{:S(2)}, u32[]{:S(2)}) collective-permute-start(bf16[64,2048]{1,0:T(8,128)(2,1)S(1)} %get-tuple-element.38.refs_1_), channel_id=1, source_target_pairs={{0,16},{1,9},{2,18},{3,11},{4,20},{5,13},{6,22},{7,15},{8,24},{9,1... | collective-permute-start | bytes 786440 | tf_op jit(solution)/shard_map/ppermute | solution.py:288
  4.9 10.6 %collective-permute-start.8 = (bf16[64,2048]{1,0:T(8,128)(2,1)S(1)}, bf16[64,2048]{1,0:T(8,128)(2,1)S(1)}, u32[]{:S(2)}, u32[]{:S(2)}) collective-permute-start(bf16[64,2048]{1,0:T(8,128)(2,1)S(1)} %get-tuple-element.38.refs_1_), channel_id=1, source_target_pairs={{0,8},{1,17},{2,10},{3,19},{4,12},{5,21},{6,14},{7,23},{8,0},{9,25... | collective-permute-start | bytes 786440 | tf_op jit(solution)/shard_map/ppermute | solution.py:288
  6.4 8.0 %collective-permute-start = (bf16[32,2048]{1,0:T(8,128)(2,1)S(1)}, bf16[32,2048]{1,0:T(8,128)(2,1)S(1)}, u32[]{:S(2)}, u32[]{:S(2)}) collective-permute-start(bf16[32,2048]{1,0:T(8,128)(2,1)S(1)} %get-tuple-element.37.refs_0_), channel_id=1, source_target_pairs={{0,6},{1,7},{2,4},{3,5},{4,2},{5,3},{6,0},{7,1},{8,14},{9,15},{10,... | collective-permute-start | bytes 393224 | tf_op jit(solution)/shard_map/ppermute | solution.py:282
  10.0 6.0 %collective-permute-start.4 = (bf16[32,2048]{1,0:T(8,128)(2,1)S(1)}, bf16[32,2048]{1,0:T(8,128)(2,1)S(1)}, u32[]{:S(2)}, u32[]{:S(2)}) collective-permute-start(bf16[32,2048]{1,0:T(8,128)(2,1)S(1)} %get-tuple-element.37.refs_0_), channel_id=1, source_target_pairs={{0,1},{1,0},{2,3},{3,2},{4,5},{5,4},{6,7},{7,6},{8,9},{9,8},{10,11... | collective-permute-start | bytes 393224 | tf_op jit(solution)/shard_map/ppermute | solution.py:285
  10.0 6.8 %collective-permute-start.2 = (bf16[32,2048]{1,0:T(8,128)(2,1)S(1)}, bf16[32,2048]{1,0:T(8,128)(2,1)S(1)}, u32[]{:S(2)}, u32[]{:S(2)}) collective-permute-start(bf16[32,2048]{1,0:T(8,128)(2,1)S(1)} %get-tuple-element.37.refs_0_), channel_id=1, source_target_pairs={{0,2},{1,3},{2,0},{3,1},{4,6},{5,7},{6,4},{7,5},{8,10},{9,11},{10,... | collective-permute-start | bytes 393224 | tf_op jit(solution)/shard_map/ppermute | solution.py:282
  14.3 5.0 %collective-permute-start.3 = (bf16[32,2048]{1,0:T(8,128)(2,1)S(1)}, bf16[32,2048]{1,0:T(8,128)(2,1)S(1)}, u32[]{:S(2)}, u32[]{:S(2)}) collective-permute-start(bf16[32,2048]{1,0:T(8,128)(2,1)S(1)} %collective-permute-done.refs_1_), channel_id=1, source_target_pairs={{0,2},{1,3},{2,0},{3,1},{4,6},{5,7},{6,4},{7,5},{8,10},{9,11},{10,... | collective-permute-start | bytes 393224 | tf_op jit(solution)/shard_map/ppermute | solution.py:282
  15.4 6.4 %collective-permute-start.9 = (bf16[64,2048]{1,0:T(8,128)(2,1)S(1)}, bf16[64,2048]{1,0:T(8,128)(2,1)S(1)}, u32[]{:S(2)}, u32[]{:S(2)}) collective-permute-start(bf16[64,2048]{1,0:T(8,128)(2,1)S(1)} %collective-permute-done.8.refs_2_), channel_id=1, source_target_pairs={{0,16},{1,9},{2,18},{3,11},{4,20},{5,13},{6,22},{7,15},{8,24},{9,1... | collective-permute-start | bytes 786440 | tf_op jit(solution)/shard_map/ppermute | solution.py:288
  16.7 2.6 %collective-permute-start.6 = (bf16[32,2048]{1,0:T(8,128)(2,1)S(1)}, bf16[32,2048]{1,0:T(8,128)(2,1)S(1)}, u32[]{:S(2)}, u32[]{:S(2)}) collective-permute-start(bf16[32,2048]{1,0:T(8,128)(2,1)S(1)} %collective-permute-done.2.refs_2_), channel_id=1, source_target_pairs={{0,1},{1,0},{2,3},{3,2},{4,5},{5,4},{6,7},{7,6},{8,9},{9,8},{10,11... | collective-permute-start | bytes 393224 | tf_op jit(solution)/shard_map/ppermute | solution.py:285
  16.7 2.6 %collective-permute-start.5 = (bf16[32,2048]{1,0:T(8,128)(2,1)S(1)}, bf16[32,2048]{1,0:T(8,128)(2,1)S(1)}, u32[]{:S(2)}, u32[]{:S(2)}) collective-permute-start(bf16[32,2048]{1,0:T(8,128)(2,1)S(1)} %collective-permute-done.refs_1_), channel_id=1, source_target_pairs={{0,1},{1,0},{2,3},{3,2},{4,5},{5,4},{6,7},{7,6},{8,9},{9,8},{10,11... | collective-permute-start | bytes 393224 | tf_op jit(solution)/shard_map/ppermute | solution.py:285
  19.3 1.3 %collective-permute-start.7 = (bf16[32,2048]{1,0:T(8,128)(2,1)S(1)}, bf16[32,2048]{1,0:T(8,128)(2,1)S(1)}, u32[]{:S(2)}, u32[]{:S(2)}) collective-permute-start(bf16[32,2048]{1,0:T(8,128)(2,1)S(1)} %collective-permute-done.3.refs_3_), channel_id=1, source_target_pairs={{0,1},{1,0},{2,3},{3,2},{4,5},{5,4},{6,7},{7,6},{8,9},{9,8},{10,11... | collective-permute-start | bytes 393224 | tf_op jit(solution)/shard_map/ppermute | solution.py:285
  27.6 18.0 %copy-start.3 = (f32[2048,64]{0,1:T(8,128)S(1)}, f32[2048,64]{0,1:T(8,128)}, u32[]{:S(2)}) copy-start(f32[2048,64]{0,1:T(8,128)} %param.14) | copy-start | bytes 1572868
  27.6 18.0 %copy-start.4 = (f32[2048,64]{0,1:T(8,128)S(1)}, f32[2048,64]{0,1:T(8,128)}, u32[]{:S(2)}) copy-start(f32[2048,64]{0,1:T(8,128)} %param.15) | copy-start | bytes 1572868
  27.6 19.4 %copy-start.5 = (f32[2048,32]{0,1:T(8,128)S(1)}, f32[2048,32]{0,1:T(8,128)}, u32[]{:S(2)}) copy-start(f32[2048,32]{0,1:T(8,128)} %param.11) | copy-start | bytes 786436
  27.6 19.4 %copy-start.6 = (f32[2048,32]{0,1:T(8,128)S(1)}, f32[2048,32]{0,1:T(8,128)}, u32[]{:S(2)}) copy-start(f32[2048,32]{0,1:T(8,128)} %param.12) | copy-start | bytes 786436
  27.7 2.6 %collective-permute-start.10 = (bf16[128,2048]{1,0:T(8,128)(2,1)S(1)}, bf16[128,2048]{1,0:T(8,128)(2,1)S(1)}, u32[]{:S(2)}, u32[]{:S(2)}) collective-permute-start(bf16[128,2048]{1,0:T(8,128)(2,1)S(1)} %get-tuple-element.45), channel_id=1, source_target_pairs={{0,1},{1,0},{2,3},{3,2},{4,5},{5,4},{6,7},{7,6},{8,9},{9,8},{10,11... | collective-permute-start | bytes 1572872 | tf_op jit(solution)/shard_map/ppermute | solution.py:285
  30.3 6.0 %collective-permute-start.14 = (bf16[32,2048]{1,0:T(8,128)(2,1)S(1)}, bf16[32,2048]{1,0:T(8,128)(2,1)S(1)}, u32[]{:S(2)}, u32[]{:S(2)}) collective-permute-start(bf16[32,2048]{1,0:T(8,128)(2,1)S(1)} %get-tuple-element.59), channel_id=1, source_target_pairs={{0,2},{1,3},{2,0},{3,1},{4,6},{5,7},{6,4},{7,5},{8,10},{9,11},{10,... | collective-permute-start | bytes 393224 | tf_op jit(solution)/shard_map/ppermute | solution.py:282
  31.3 9.1 %collective-permute-start.11 = (bf16[64,2048]{1,0:T(8,128)(2,1)S(1)}, bf16[64,2048]{1,0:T(8,128)(2,1)S(1)}, u32[]{:S(2)}, u32[]{:S(2)}) collective-permute-start(bf16[64,2048]{1,0:T(8,128)(2,1)S(1)} %get-tuple-element.52), channel_id=1, source_target_pairs={{0,8},{1,9},{2,10},{3,11},{4,12},{5,13},{6,14},{7,15},{8,0},{9,1},... | collective-permute-start | bytes 786440 | tf_op jit(solution)/shard_map/ppermute | solution.py:288
  31.8 13.8 %collective-permute-start.12 = (bf16[64,2048]{1,0:T(8,128)(2,1)S(1)}, bf16[64,2048]{1,0:T(8,128)(2,1)S(1)}, u32[]{:S(2)}, u32[]{:S(2)}) collective-permute-start(bf16[64,2048]{1,0:T(8,128)(2,1)S(1)} %get-tuple-element.53), channel_id=1, source_target_pairs={{0,16},{1,17},{2,18},{3,19},{4,20},{5,21},{6,22},{7,23},{8,24},{9,... | collective-permute-start | bytes 786440 | tf_op jit(solution)/shard_map/ppermute | solution.py:288
  32.1 13.5 %collective-permute-start.13 = (bf16[64,2048]{1,0:T(8,128)(2,1)S(1)}, bf16[64,2048]{1,0:T(8,128)(2,1)S(1)}, u32[]{:S(2)}, u32[]{:S(2)}) collective-permute-start(bf16[64,2048]{1,0:T(8,128)(2,1)S(1)} %get-tuple-element.54), channel_id=1, source_target_pairs={{0,24},{1,25},{2,26},{3,27},{4,28},{5,29},{6,30},{7,31},{8,16},{9,... | collective-permute-start | bytes 786440 | tf_op jit(solution)/shard_map/ppermute | solution.py:288
  36.3 10.7 %collective-permute-start.15 = (bf16[32,2048]{1,0:T(8,128)(2,1)S(1)}, bf16[32,2048]{1,0:T(8,128)(2,1)S(1)}, u32[]{:S(2)}, u32[]{:S(2)}) collective-permute-start(bf16[32,2048]{1,0:T(8,128)(2,1)S(1)} %add_partial.1), channel_id=1, source_target_pairs={{0,4},{1,5},{2,6},{3,7},{4,0},{5,1},{6,2},{7,3},{8,12},{9,13},{10,... | collective-permute-start | bytes 393224 | tf_op jit(solution)/shard_map/ppermute | solution.py:282
  39.5 7.5 %collective-permute-start.16 = (bf16[32,2048]{1,0:T(8,128)(2,1)S(1)}, bf16[32,2048]{1,0:T(8,128)(2,1)S(1)}, u32[]{:S(2)}, u32[]{:S(2)}) collective-permute-start(bf16[32,2048]{1,0:T(8,128)(2,1)S(1)} %get-tuple-element.61), channel_id=1, source_target_pairs={{0,2},{1,3},{2,0},{3,1},{4,6},{5,7},{6,4},{7,5},{8,10},{9,11},{10,... | collective-permute-start | bytes 393224 | tf_op jit(solution)/shard_map/ppermute | solution.py:282
  (1 other events, 1.0 us)

commit v7 on v6

--- a/solution.py
+++ b/solution.py
@@ -18,7 +18,7 @@
 F32 = jnp.float32
 VMEM_BYTES = 26 * 2**20
 SMALL_VMEM = 8 * 2**20
-ROW_TILE = 1024
+ROW_TILE = 512
 COL_TILE = 512
 
 

time: 48.2 us -> 48.2 us (level)
  no operation moved by 1% of the time
where the time goes in v7:
time: 48.2 us; the launch traced here: 48 us
  starting transfers between devices  18.4 us (38%)
  waiting for transfers between devices  16.4 us (34%)
  Pallas kernels  11.3 us (23%)
  local copies, waits for them, and re-layouts  1.1 us (2%)
  between operations  0.8 us (2%)
    ppermute x6, starting transfers between devices, send_chip(): return lax.ppermute(x, 'item', swap_item(n_item, 2 * mask))  9.29 us
    ppermute x6, waiting for transfers between devices, send_chip(): return lax.ppermute(x, 'item', swap_item(n_item, 2 * mask))  8.72 us
    ppermute x6, starting transfers between devices, send_mp(): return lax.ppermute(x, ('mp', 'item'), swap_mp(n_mp, n_item, *masks))  8.52 us
    ppermute x6, waiting for transfers between devices, send_mp(): return lax.ppermute(x, ('mp', 'item'), swap_mp(n_mp, n_item, *masks))  6.4 us
    pallas_call x1, Pallas kernels, ability_gradient(): pl.pallas_call(functools.partial(ability_kernel, n_mp, n_item), out_shape...  5.77 us
    pallas_call x1, Pallas kernels, discrim_gradient(): pl.pallas_call(functools.partial(discrim_kernel, n_mp), out_shape=[shape(...  2.47 us
    pallas_call x2, Pallas kernels, adam(): pl.pallas_call(functools.partial(adam_kernel, plan), out_shape=outs, comp...  2.38 us
    ppermute x5, waiting for transfers between devices, send_core(): return lax.ppermute(x, 'item', swap_item(n_item, 1))  1.33 us
  transfers between devices with their start and end apart: 17, of which 8 were waited for; matrix products, arithmetic and copies ran while one was open for 0% of the time, Pallas kernels for 9%

profile of v7, /device:TPU:0, one launch (start us, length us, event | category | flops | bytes accessed | tf_op | source)
XLA Modules:
  0.0 48.0 jit_solution(1188471461879353452)
XLA Ops:
  0.7 1.0 %copy-done.1 = f32[2048,64]{0,1:T(8,128)S(1)} copy-done((f32[2048,64]{0,1:T(8,128)S(1)}, f32[2048,64]{0,1:T(8,128)}, u32[]{:S(2)}) %copy-start.1) | copy-done | bytes 524312
  1.8 3.0 %collective-permute-start.1 = (bf16[64,2048]{1,0:T(8,128)(2,1)S(1)}, bf16[64,2048]{1,0:T(8,128)(2,1)S(1)}, u32[]{:S(2)}, u32[]{:S(2)}) collective-permute-start(bf16[64,2048]{1,0:T(8,128)(2,1)S(1)} %get-tuple-element.38.refs_1_), channel_id=1, source_target_pairs={{0,16},{1,9},{2,18},{3,11},{4,20},{5,13},{6,22},{7,15},{8,24},{9,1... | collective-permute-start | bytes 786440 | tf_op jit(solution)/shard_map/ppermute | solution.py:288
  4.9 1.5 %collective-permute-start.8 = (bf16[64,2048]{1,0:T(8,128)(2,1)S(1)}, bf16[64,2048]{1,0:T(8,128)(2,1)S(1)}, u32[]{:S(2)}, u32[]{:S(2)}) collective-permute-start(bf16[64,2048]{1,0:T(8,128)(2,1)S(1)} %get-tuple-element.38.refs_1_), channel_id=1, source_target_pairs={{0,8},{1,17},{2,10},{3,19},{4,12},{5,21},{6,14},{7,23},{8,0},{9,25... | collective-permute-start | bytes 786440 | tf_op jit(solution)/shard_map/ppermute | solution.py:288
  6.4 3.6 %collective-permute-start = (bf16[32,2048]{1,0:T(8,128)(2,1)S(1)}, bf16[32,2048]{1,0:T(8,128)(2,1)S(1)}, u32[]{:S(2)}, u32[]{:S(2)}) collective-permute-start(bf16[32,2048]{1,0:T(8,128)(2,1)S(1)} %get-tuple-element.37.refs_0_), channel_id=1, source_target_pairs={{0,6},{1,7},{2,4},{3,5},{4,2},{5,3},{6,0},{7,1},{8,14},{9,15},{10,... | collective-permute-start | bytes 393224 | tf_op jit(solution)/shard_map/ppermute | solution.py:282
  10.0 4.3 %collective-permute-done.refs_1_ = bf16[32,2048]{1,0:T(8,128)(2,1)S(1)} collective-permute-done((bf16[32,2048]{1,0:T(8,128)(2,1)S(1)}, bf16[32,2048]{1,0:T(8,128)(2,1)S(1)}, u32[]{:S(2)}, u32[]{:S(2)}) %collective-permute-start) | collective-permute-done | bytes 131104 | tf_op jit(solution)/shard_map/ppermute | solution.py:282
  14.3 1.1 %collective-permute-start.3 = (bf16[32,2048]{1,0:T(8,128)(2,1)S(1)}, bf16[32,2048]{1,0:T(8,128)(2,1)S(1)}, u32[]{:S(2)}, u32[]{:S(2)}) collective-permute-start(bf16[32,2048]{1,0:T(8,128)(2,1)S(1)} %collective-permute-done.refs_1_), channel_id=1, source_target_pairs={{0,2},{1,3},{2,0},{3,1},{4,6},{5,7},{6,4},{7,5},{8,10},{9,11},{10,... | collective-permute-start | bytes 393224 | tf_op jit(solution)/shard_map/ppermute | solution.py:282
  15.4 0.5 %collective-permute-start.9 = (bf16[64,2048]{1,0:T(8,128)(2,1)S(1)}, bf16[64,2048]{1,0:T(8,128)(2,1)S(1)}, u32[]{:S(2)}, u32[]{:S(2)}) collective-permute-start(bf16[64,2048]{1,0:T(8,128)(2,1)S(1)} %collective-permute-done.8.refs_2_), channel_id=1, source_target_pairs={{0,16},{1,9},{2,18},{3,11},{4,20},{5,13},{6,22},{7,15},{8,24},{9,1... | collective-permute-start | bytes 786440 | tf_op jit(solution)/shard_map/ppermute | solution.py:288
  16.0 0.8 %collective-permute-done.2.refs_2_ = bf16[32,2048]{1,0:T(8,128)(2,1)S(1)} collective-permute-done((bf16[32,2048]{1,0:T(8,128)(2,1)S(1)}, bf16[32,2048]{1,0:T(8,128)(2,1)S(1)}, u32[]{:S(2)}, u32[]{:S(2)}) %collective-permute-start.2) | collective-permute-done | bytes 131104 | tf_op jit(solution)/shard_map/ppermute | solution.py:282
  16.7 0.5 %collective-permute-start.5 = (bf16[32,2048]{1,0:T(8,128)(2,1)S(1)}, bf16[32,2048]{1,0:T(8,128)(2,1)S(1)}, u32[]{:S(2)}, u32[]{:S(2)}) collective-permute-start(bf16[32,2048]{1,0:T(8,128)(2,1)S(1)} %collective-permute-done.refs_1_), channel_id=1, source_target_pairs={{0,1},{1,0},{2,3},{3,2},{4,5},{5,4},{6,7},{7,6},{8,9},{9,8},{10,11... | collective-permute-start | bytes 393224 | tf_op jit(solution)/shard_map/ppermute | solution.py:285
  17.3 2.1 %collective-permute-done.3.refs_3_ = bf16[32,2048]{1,0:T(8,128)(2,1)S(1)} collective-permute-done((bf16[32,2048]{1,0:T(8,128)(2,1)S(1)}, bf16[32,2048]{1,0:T(8,128)(2,1)S(1)}, u32[]{:S(2)}, u32[]{:S(2)}) %collective-permute-start.3) | collective-permute-done | bytes 131104 | tf_op jit(solution)/shard_map/ppermute | solution.py:282
  19.4 1.3 %collective-permute-done.7.refs_7_ = bf16[32,2048]{1,0:T(8,128)(2,1)S(1)} collective-permute-done((bf16[32,2048]{1,0:T(8,128)(2,1)S(1)}, bf16[32,2048]{1,0:T(8,128)(2,1)S(1)}, u32[]{:S(2)}, u32[]{:S(2)}) %collective-permute-start.7) | collective-permute-done | bytes 131104 | tf_op jit(solution)/shard_map/ppermute | solution.py:285
  20.7 0.4 place_ability.1
  21.1 0.7 %collective-permute-done.9.refs_4_ = bf16[64,2048]{1,0:T(8,128)(2,1)S(1)} collective-permute-done((bf16[64,2048]{1,0:T(8,128)(2,1)S(1)}, bf16[64,2048]{1,0:T(8,128)(2,1)S(1)}, u32[]{:S(2)}, u32[]{:S(2)}) %collective-permute-start.9) | collective-permute-done | bytes 262176 | tf_op jit(solution)/shard_map/ppermute | solution.py:288
  21.8 5.8 %residual_ability_gradient.1 = (bf16[2048,2048]{1,0:T(8,128)(2,1)S(1)}, f32[128,2048]{1,0:T(8,128)S(1)}, bf16[128,2048]{1,0:T(8,128)(2,1)S(1)}) custom-call(bf16[2048,256]{1,0:T(8,128)(2,1)S(1)} %get-tuple-element.41.refs_0_, bf16[64,2048]{1,0:T(8,128)(2,1)S(1)} %get-tuple-element.38.refs_1_, bf16[64,2048]{1,0:T(8,128)(2,1)S(1)} %collective-permute-done.8.refs_2_, ...), custom_call_target="tpu_custom_call" | custom-call | flops 4294967296 | bytes 16777216 | tf_op jit(solution)/shard_map/residual_ability_gradient/pallas_call | solution.py:171
  27.7 2.5 %discrim_gradient.1 = (f32[64,2048]{1,0:T(8,128)S(1)}, bf16[64,2048]{1,0:T(8,128)(2,1)S(1)}, bf16[64,2048]{1,0:T(8,128)(2,1)S(1)}, bf16[64,2048]{1,0:T(8,128)(2,1)S(1)}) custom-call(bf16[256,2048]{1,0:T(8,128)(2,1)S(1)} %get-tuple-element.46.at, bf16[2048,2048]{1,0:T(8,128)(2,1)S(1)} %get-tuple-element.47.res), custom_call_target="tpu_custom_call" | custom-call | flops 2147483648 | bytes 8388608 | tf_op jit(solution)/shard_map/discrim_gradient/pallas_call | solution.py:202
  30.3 1.0 %collective-permute-start.14 = (bf16[32,2048]{1,0:T(8,128)(2,1)S(1)}, bf16[32,2048]{1,0:T(8,128)(2,1)S(1)}, u32[]{:S(2)}, u32[]{:S(2)}) collective-permute-start(bf16[32,2048]{1,0:T(8,128)(2,1)S(1)} %get-tuple-element.59), channel_id=1, source_target_pairs={{0,2},{1,3},{2,0},{3,1},{4,6},{5,7},{6,4},{7,5},{8,10},{9,11},{10,... | collective-permute-start | bytes 393224 | tf_op jit(solution)/shard_map/ppermute | solution.py:282
  31.3 0.5 %collective-permute-start.11 = (bf16[64,2048]{1,0:T(8,128)(2,1)S(1)}, bf16[64,2048]{1,0:T(8,128)(2,1)S(1)}, u32[]{:S(2)}, u32[]{:S(2)}) collective-permute-start(bf16[64,2048]{1,0:T(8,128)(2,1)S(1)} %get-tuple-element.52), channel_id=1, source_target_pairs={{0,8},{1,9},{2,10},{3,11},{4,12},{5,13},{6,14},{7,15},{8,0},{9,1},... | collective-permute-start | bytes 786440 | tf_op jit(solution)/shard_map/ppermute | solution.py:288
  32.1 2.7 %collective-permute-start.13 = (bf16[64,2048]{1,0:T(8,128)(2,1)S(1)}, bf16[64,2048]{1,0:T(8,128)(2,1)S(1)}, u32[]{:S(2)}, u32[]{:S(2)}) collective-permute-start(bf16[64,2048]{1,0:T(8,128)(2,1)S(1)} %get-tuple-element.54), channel_id=1, source_target_pairs={{0,24},{1,25},{2,26},{3,27},{4,28},{5,29},{6,30},{7,31},{8,16},{9,... | collective-permute-start | bytes 786440 | tf_op jit(solution)/shard_map/ppermute | solution.py:288
  34.8 1.5 %collective-permute-done.14.y_ref = bf16[32,2048]{1,0:T(8,128)(2,1)S(1)} collective-permute-done((bf16[32,2048]{1,0:T(8,128)(2,1)S(1)}, bf16[32,2048]{1,0:T(8,128)(2,1)S(1)}, u32[]{:S(2)}, u32[]{:S(2)}) %collective-permute-start.14) | collective-permute-done | bytes 131104 | tf_op jit(solution)/shard_map/ppermute | solution.py:282
  36.3 3.2 %collective-permute-start.15 = (bf16[32,2048]{1,0:T(8,128)(2,1)S(1)}, bf16[32,2048]{1,0:T(8,128)(2,1)S(1)}, u32[]{:S(2)}, u32[]{:S(2)}) collective-permute-start(bf16[32,2048]{1,0:T(8,128)(2,1)S(1)} %add_partial.1), channel_id=1, source_target_pairs={{0,4},{1,5},{2,6},{3,7},{4,0},{5,1},{6,2},{7,3},{8,12},{9,13},{10,... | collective-permute-start | bytes 393224 | tf_op jit(solution)/shard_map/ppermute | solution.py:282
  39.9 0.5 %collective-permute-done.11.refs_1_ = bf16[64,2048]{1,0:T(8,128)(2,1)S(1)} collective-permute-done((bf16[64,2048]{1,0:T(8,128)(2,1)S(1)}, bf16[64,2048]{1,0:T(8,128)(2,1)S(1)}, u32[]{:S(2)}, u32[]{:S(2)}) %collective-permute-start.11) | collective-permute-done | bytes 262176 | tf_op jit(solution)/shard_map/ppermute | solution.py:288
  40.4 5.2 %collective-permute-done.12.refs_2_ = bf16[64,2048]{1,0:T(8,128)(2,1)S(1)} collective-permute-done((bf16[64,2048]{1,0:T(8,128)(2,1)S(1)}, bf16[64,2048]{1,0:T(8,128)(2,1)S(1)}, u32[]{:S(2)}, u32[]{:S(2)}) %collective-permute-start.12) | collective-permute-done | bytes 262176 | tf_op jit(solution)/shard_map/ppermute | solution.py:288
  45.6 1.4 %adam.2 = (f32[64,2048]{1,0:T(8,128)}, f32[64,2048]{1,0:T(8,128)}, f32[64,2048]{1,0:T(8,128)}) custom-call(f32[64,2048]{1,0:T(8,128)S(1)} %get-tuple-element.51.refs_0_, bf16[64,2048]{1,0:T(8,128)(2,1)S(1)} %collective-permute-done.11.refs_1_, bf16[64,2048]{1,0:T(8,128)(2,1)S(1)} %collective-permute-done.12.refs_2_, ...), custom_call_target="tpu_custom_call" | custom-call | tf_op jit(solution)/shard_map/adam/pallas_call | solution.py:265
  47.0 1.0 %adam.3 = (f32[32,2048]{1,0:T(8,128)}, f32[32,2048]{1,0:T(8,128)}, f32[32,2048]{1,0:T(8,128)}) custom-call(f32[32,2048]{1,0:T(8,128)S(1)} %get-tuple-element.56.refs_0_, bf16[32,2048]{1,0:T(8,128)(2,1)S(1)} %collective-permute-done.15.refs_1_, bf16[32,2048]{1,0:T(8,128)(2,1)S(1)} %collective-permute-done.16.refs_2_, f32[32,2048]{1,0:T(8,128)S(1)} %bitcast.16, ...), custom_call_target="tpu_custom_call" | custom-call | tf_op jit(solution)/shard_map/adam/pallas_call | solution.py:265
  (36 shorter events, 1.1 us)
Async XLA Ops:
  0.6 1.1 %copy-start.2 = (f32[2048,32]{0,1:T(8,128)S(1)}, f32[2048,32]{0,1:T(8,128)}, u32[]{:S(2)}) copy-start(f32[2048,32]{0,1:T(8,128)} %param.10) | copy-start | bytes 786436
  0.7 18.7 %copy-start.7 = (f32[2048]{0:T(1024)S(1)}, f32[2048]{0:T(1024)}, u32[]{:S(2)}) copy-start(f32[2048]{0:T(1024)} %param.9) | copy-start | bytes 24580
  0.7 21.2 %copy-start = (s32[2048,2048]{1,0:T(8,128)S(1)}, s32[2048,2048]{1,0:T(8,128)}, u32[]{:S(2)}) copy-start(s32[2048,2048]{1,0:T(8,128)} %refs_6_.1) | copy-start | bytes 50331652
  1.8 12.5 %collective-permute-start.1 = (bf16[64,2048]{1,0:T(8,128)(2,1)S(1)}, bf16[64,2048]{1,0:T(8,128)(2,1)S(1)}, u32[]{:S(2)}, u32[]{:S(2)}) collective-permute-start(bf16[64,2048]{1,0:T(8,128)(2,1)S(1)} %get-tuple-element.38.refs_1_), channel_id=1, source_target_pairs={{0,16},{1,9},{2,18},{3,11},{4,20},{5,13},{6,22},{7,15},{8,24},{9,1... | collective-permute-start | bytes 786440 | tf_op jit(solution)/shard_map/ppermute | solution.py:288
  4.9 10.6 %collective-permute-start.8 = (bf16[64,2048]{1,0:T(8,128)(2,1)S(1)}, bf16[64,2048]{1,0:T(8,128)(2,1)S(1)}, u32[]{:S(2)}, u32[]{:S(2)}) collective-permute-start(bf16[64,2048]{1,0:T(8,128)(2,1)S(1)} %get-tuple-element.38.refs_1_), channel_id=1, source_target_pairs={{0,8},{1,17},{2,10},{3,19},{4,12},{5,21},{6,14},{7,23},{8,0},{9,25... | collective-permute-start | bytes 786440 | tf_op jit(solution)/shard_map/ppermute | solution.py:288
  6.4 8.0 %collective-permute-start = (bf16[32,2048]{1,0:T(8,128)(2,1)S(1)}, bf16[32,2048]{1,0:T(8,128)(2,1)S(1)}, u32[]{:S(2)}, u32[]{:S(2)}) collective-permute-start(bf16[32,2048]{1,0:T(8,128)(2,1)S(1)} %get-tuple-element.37.refs_0_), channel_id=1, source_target_pairs={{0,6},{1,7},{2,4},{3,5},{4,2},{5,3},{6,0},{7,1},{8,14},{9,15},{10,... | collective-permute-start | bytes 393224 | tf_op jit(solution)/shard_map/ppermute | solution.py:282
  10.0 6.0 %collective-permute-start.4 = (bf16[32,2048]{1,0:T(8,128)(2,1)S(1)}, bf16[32,2048]{1,0:T(8,128)(2,1)S(1)}, u32[]{:S(2)}, u32[]{:S(2)}) collective-permute-start(bf16[32,2048]{1,0:T(8,128)(2,1)S(1)} %get-tuple-element.37.refs_0_), channel_id=1, source_target_pairs={{0,1},{1,0},{2,3},{3,2},{4,5},{5,4},{6,7},{7,6},{8,9},{9,8},{10,11... | collective-permute-start | bytes 393224 | tf_op jit(solution)/shard_map/ppermute | solution.py:285
  10.0 6.8 %collective-permute-start.2 = (bf16[32,2048]{1,0:T(8,128)(2,1)S(1)}, bf16[32,2048]{1,0:T(8,128)(2,1)S(1)}, u32[]{:S(2)}, u32[]{:S(2)}) collective-permute-start(bf16[32,2048]{1,0:T(8,128)(2,1)S(1)} %get-tuple-element.37.refs_0_), channel_id=1, source_target_pairs={{0,2},{1,3},{2,0},{3,1},{4,6},{5,7},{6,4},{7,5},{8,10},{9,11},{10,... | collective-permute-start | bytes 393224 | tf_op jit(solution)/shard_map/ppermute | solution.py:282
  14.3 5.0 %collective-permute-start.3 = (bf16[32,2048]{1,0:T(8,128)(2,1)S(1)}, bf16[32,2048]{1,0:T(8,128)(2,1)S(1)}, u32[]{:S(2)}, u32[]{:S(2)}) collective-permute-start(bf16[32,2048]{1,0:T(8,128)(2,1)S(1)} %collective-permute-done.refs_1_), channel_id=1, source_target_pairs={{0,2},{1,3},{2,0},{3,1},{4,6},{5,7},{6,4},{7,5},{8,10},{9,11},{10,... | collective-permute-start | bytes 393224 | tf_op jit(solution)/shard_map/ppermute | solution.py:282
  15.4 6.4 %collective-permute-start.9 = (bf16[64,2048]{1,0:T(8,128)(2,1)S(1)}, bf16[64,2048]{1,0:T(8,128)(2,1)S(1)}, u32[]{:S(2)}, u32[]{:S(2)}) collective-permute-start(bf16[64,2048]{1,0:T(8,128)(2,1)S(1)} %collective-permute-done.8.refs_2_), channel_id=1, source_target_pairs={{0,16},{1,9},{2,18},{3,11},{4,20},{5,13},{6,22},{7,15},{8,24},{9,1... | collective-permute-start | bytes 786440 | tf_op jit(solution)/shard_map/ppermute | solution.py:288
  16.7 2.6 %collective-permute-start.6 = (bf16[32,2048]{1,0:T(8,128)(2,1)S(1)}, bf16[32,2048]{1,0:T(8,128)(2,1)S(1)}, u32[]{:S(2)}, u32[]{:S(2)}) collective-permute-start(bf16[32,2048]{1,0:T(8,128)(2,1)S(1)} %collective-permute-done.2.refs_2_), channel_id=1, source_target_pairs={{0,1},{1,0},{2,3},{3,2},{4,5},{5,4},{6,7},{7,6},{8,9},{9,8},{10,11... | collective-permute-start | bytes 393224 | tf_op jit(solution)/shard_map/ppermute | solution.py:285
  16.7 2.6 %collective-permute-start.5 = (bf16[32,2048]{1,0:T(8,128)(2,1)S(1)}, bf16[32,2048]{1,0:T(8,128)(2,1)S(1)}, u32[]{:S(2)}, u32[]{:S(2)}) collective-permute-start(bf16[32,2048]{1,0:T(8,128)(2,1)S(1)} %collective-permute-done.refs_1_), channel_id=1, source_target_pairs={{0,1},{1,0},{2,3},{3,2},{4,5},{5,4},{6,7},{7,6},{8,9},{9,8},{10,11... | collective-permute-start | bytes 393224 | tf_op jit(solution)/shard_map/ppermute | solution.py:285
  19.3 1.3 %collective-permute-start.7 = (bf16[32,2048]{1,0:T(8,128)(2,1)S(1)}, bf16[32,2048]{1,0:T(8,128)(2,1)S(1)}, u32[]{:S(2)}, u32[]{:S(2)}) collective-permute-start(bf16[32,2048]{1,0:T(8,128)(2,1)S(1)} %collective-permute-done.3.refs_3_), channel_id=1, source_target_pairs={{0,1},{1,0},{2,3},{3,2},{4,5},{5,4},{6,7},{7,6},{8,9},{9,8},{10,11... | collective-permute-start | bytes 393224 | tf_op jit(solution)/shard_map/ppermute | solution.py:285
  27.6 18.0 %copy-start.3 = (f32[2048,64]{0,1:T(8,128)S(1)}, f32[2048,64]{0,1:T(8,128)}, u32[]{:S(2)}) copy-start(f32[2048,64]{0,1:T(8,128)} %param.14) | copy-start | bytes 1572868
  27.6 18.0 %copy-start.4 = (f32[2048,64]{0,1:T(8,128)S(1)}, f32[2048,64]{0,1:T(8,128)}, u32[]{:S(2)}) copy-start(f32[2048,64]{0,1:T(8,128)} %param.15) | copy-start | bytes 1572868
  27.6 19.4 %copy-start.5 = (f32[2048,32]{0,1:T(8,128)S(1)}, f32[2048,32]{0,1:T(8,128)}, u32[]{:S(2)}) copy-start(f32[2048,32]{0,1:T(8,128)} %param.11) | copy-start | bytes 786436
  27.6 19.4 %copy-start.6 = (f32[2048,32]{0,1:T(8,128)S(1)}, f32[2048,32]{0,1:T(8,128)}, u32[]{:S(2)}) copy-start(f32[2048,32]{0,1:T(8,128)} %param.12) | copy-start | bytes 786436
  27.6 2.6 %collective-permute-start.10 = (bf16[128,2048]{1,0:T(8,128)(2,1)S(1)}, bf16[128,2048]{1,0:T(8,128)(2,1)S(1)}, u32[]{:S(2)}, u32[]{:S(2)}) collective-permute-start(bf16[128,2048]{1,0:T(8,128)(2,1)S(1)} %get-tuple-element.45), channel_id=1, source_target_pairs={{0,1},{1,0},{2,3},{3,2},{4,5},{5,4},{6,7},{7,6},{8,9},{9,8},{10,11... | collective-permute-start | bytes 1572872 | tf_op jit(solution)/shard_map/ppermute | solution.py:285
  30.3 6.0 %collective-permute-start.14 = (bf16[32,2048]{1,0:T(8,128)(2,1)S(1)}, bf16[32,2048]{1,0:T(8,128)(2,1)S(1)}, u32[]{:S(2)}, u32[]{:S(2)}) collective-permute-start(bf16[32,2048]{1,0:T(8,128)(2,1)S(1)} %get-tuple-element.59), channel_id=1, source_target_pairs={{0,2},{1,3},{2,0},{3,1},{4,6},{5,7},{6,4},{7,5},{8,10},{9,11},{10,... | collective-permute-start | bytes 393224 | tf_op jit(solution)/shard_map/ppermute | solution.py:282
  31.3 9.1 %collective-permute-start.11 = (bf16[64,2048]{1,0:T(8,128)(2,1)S(1)}, bf16[64,2048]{1,0:T(8,128)(2,1)S(1)}, u32[]{:S(2)}, u32[]{:S(2)}) collective-permute-start(bf16[64,2048]{1,0:T(8,128)(2,1)S(1)} %get-tuple-element.52), channel_id=1, source_target_pairs={{0,8},{1,9},{2,10},{3,11},{4,12},{5,13},{6,14},{7,15},{8,0},{9,1},... | collective-permute-start | bytes 786440 | tf_op jit(solution)/shard_map/ppermute | solution.py:288
  31.8 13.8 %collective-permute-start.12 = (bf16[64,2048]{1,0:T(8,128)(2,1)S(1)}, bf16[64,2048]{1,0:T(8,128)(2,1)S(1)}, u32[]{:S(2)}, u32[]{:S(2)}) collective-permute-start(bf16[64,2048]{1,0:T(8,128)(2,1)S(1)} %get-tuple-element.53), channel_id=1, source_target_pairs={{0,16},{1,17},{2,18},{3,19},{4,20},{5,21},{6,22},{7,23},{8,24},{9,... | collective-permute-start | bytes 786440 | tf_op jit(solution)/shard_map/ppermute | solution.py:288
  32.1 13.5 %collective-permute-start.13 = (bf16[64,2048]{1,0:T(8,128)(2,1)S(1)}, bf16[64,2048]{1,0:T(8,128)(2,1)S(1)}, u32[]{:S(2)}, u32[]{:S(2)}) collective-permute-start(bf16[64,2048]{1,0:T(8,128)(2,1)S(1)} %get-tuple-element.54), channel_id=1, source_target_pairs={{0,24},{1,25},{2,26},{3,27},{4,28},{5,29},{6,30},{7,31},{8,16},{9,... | collective-permute-start | bytes 786440 | tf_op jit(solution)/shard_map/ppermute | solution.py:288
  36.3 10.7 %collective-permute-start.15 = (bf16[32,2048]{1,0:T(8,128)(2,1)S(1)}, bf16[32,2048]{1,0:T(8,128)(2,1)S(1)}, u32[]{:S(2)}, u32[]{:S(2)}) collective-permute-start(bf16[32,2048]{1,0:T(8,128)(2,1)S(1)} %add_partial.1), channel_id=1, source_target_pairs={{0,4},{1,5},{2,6},{3,7},{4,0},{5,1},{6,2},{7,3},{8,12},{9,13},{10,... | collective-permute-start | bytes 393224 | tf_op jit(solution)/shard_map/ppermute | solution.py:282
  39.5 7.5 %collective-permute-start.16 = (bf16[32,2048]{1,0:T(8,128)(2,1)S(1)}, bf16[32,2048]{1,0:T(8,128)(2,1)S(1)}, u32[]{:S(2)}, u32[]{:S(2)}) collective-permute-start(bf16[32,2048]{1,0:T(8,128)(2,1)S(1)} %get-tuple-element.61), channel_id=1, source_target_pairs={{0,2},{1,3},{2,0},{3,1},{4,6},{5,7},{6,4},{7,5},{8,10},{9,11},{10,... | collective-permute-start | bytes 393224 | tf_op jit(solution)/shard_map/ppermute | solution.py:282
  (1 other events, 1.0 us)
